TPU v7x, 32 devices: a whole 2x2x4 slice. The times are simulated.
32 devices in a mesh: shot: 2 (over y), gy: 4 (over z), freq: 2 (over x), fld: 2 (over core).
Axes of the slice: x: 2, y: 2, z: 4, core: 2. Of those that a mesh axis runs over, the one named last changes fastest.
Arguments:
- wavefields: float32 [2, 2, 8, 1024, 1024], P('fld', None, ('shot', 'freq'), 'gy'), parts along dimension 2, may hold values from -6 to 6
- slowness: float32 [2, 1024, 1024], P(None, 'gy'), may hold values from 0.7 to 1.3
- freq_index: int32 [4], P('freq'), may hold values from 15 to 27
Outputs:
- image: float32 [4, 1024, 1024], P('shot', 'gy', ('freq', 'fld')), parts along dimension 0
There are 2 independent parts, one for each index of `shot`. A program takes and returns all parts, laid end to end along the dimension named above; an argument that names none is the same for every part. Nothing has to cross between parts.
Inputs may be any that keep to these rules, and one draw needn't show every extreme that they name: `freq_index`: frequency index k stands for the angular frequency 0.1 k.
All inputs are finite; a program needn't handle non-finite values.
Results may differ from a plain program's by a relative error of at most 0.0003.
Values sent between devices are 32-bit elements; how exact they have to be, the bound alone decides.
No kernel may reach another device: no remote copies, remote signals or barrier semaphores. Data moves between devices by JAX's collectives and lax.ppermute only.
A program may use at most 64 MiB of HBM per device.

v0:
```python
import math

import jax
import jax.numpy as jnp
from jax import lax
from jax.sharding import PartitionSpec as P

DEPTH = 2


omega_unit = 0.1
reference_slowness = 1.0
depth_interval = 1.0
inner_length = 128


def contract(pattern, values, matrix):
    return jnp.einsum(
        pattern, values, matrix, precision=lax.Precision.HIGHEST, preferred_element_type=jnp.float32
    )


def complex_table(length, polarity):
    indices = jnp.arange(length, dtype=jnp.int32)
    angles = (
        2.0 * math.pi / length * (indices[:, None] * indices[None, :] % length).astype(jnp.float32)
    )
    cosine = jnp.cos(angles)
    sine_part = polarity * jnp.sin(angles)
    upper = jnp.stack([cosine, sine_part], axis=1)
    lower = jnp.stack([-sine_part, cosine], axis=1)
    return jnp.stack([upper, lower], axis=0)


def twiddle(outer_size, inner_size, length, polarity):
    outer_index = jnp.arange(outer_size, dtype=jnp.int32)[:, None]
    inner_index = jnp.arange(inner_size, dtype=jnp.int32)[None, :]
    angles = 2.0 * math.pi / length * (outer_index * inner_index % length).astype(jnp.float32)
    return (jnp.cos(angles), polarity * jnp.sin(angles))


def rotate(values, cosine, sine_part):
    real_part = values[0]
    imag_part = values[1]
    return jnp.stack(
        [real_part * cosine - imag_part * sine_part, real_part * sine_part + imag_part * cosine]
    )


def wave_number(indices, length):
    signed = jnp.where(indices < length // 2, indices, indices - length)
    return 2.0 * math.pi / length * signed.astype(jnp.float32)


def forward_rows(wave_field):
    batches, x_rows, y_cols = wave_field.shape[1:]
    outer_size = y_cols // inner_length
    blocks = wave_field.reshape(2, batches, x_rows, outer_size, inner_length)
    blocks = contract("cbxan,cadk->dbxkn", blocks, complex_table(outer_size, -1.0))
    cosine, sine_part = twiddle(outer_size, inner_length, y_cols, -1.0)
    blocks = rotate(blocks, cosine, sine_part)
    blocks = contract("cbxkn,cndm->dbxkm", blocks, complex_table(inner_length, -1.0))
    return blocks.reshape(2, batches, x_rows, y_cols)


def inverse_rows(wave_field):
    batches, x_rows, y_cols = wave_field.shape[1:]
    outer_size = y_cols // inner_length
    blocks = wave_field.reshape(2, batches, x_rows, outer_size, inner_length)
    blocks = contract("cbxkm,cmdn->dbxkn", blocks, complex_table(inner_length, 1.0))
    cosine, sine_part = twiddle(outer_size, inner_length, y_cols, 1.0)
    blocks = rotate(blocks, cosine, sine_part)
    blocks = contract("cbxkn,ckda->dbxan", blocks, complex_table(outer_size, 1.0))
    return blocks.reshape(2, batches, x_rows, y_cols) / y_cols


def forward_columns(blocks):
    inner_size = blocks.shape[2]
    pencils = blocks.shape[3]
    blocks = contract("cbnsy,csdk->dbnky", blocks, complex_table(pencils, -1.0))
    cosine, sine_part = twiddle(pencils, inner_size, inner_size * pencils, -1.0)
    blocks = rotate(blocks, cosine.T[:, :, None], sine_part.T[:, :, None])
    return contract("cbnky,cndm->dbmky", blocks, complex_table(inner_size, -1.0))


def inverse_columns(blocks):
    inner_size = blocks.shape[2]
    pencils = blocks.shape[3]
    blocks = contract("cbmky,cmdn->dbnky", blocks, complex_table(inner_size, 1.0))
    cosine, sine_part = twiddle(pencils, inner_size, inner_size * pencils, 1.0)
    blocks = rotate(blocks, cosine.T[:, :, None], sine_part.T[:, :, None])
    blocks = contract("cbnky,ckds->dbnsy", blocks, complex_table(pencils, 1.0))
    return blocks / (inner_size * pencils)


def propagate(blocks, omegas, polarities, y_total):
    inner_size, pencils, y_local = blocks.shape[2:]
    x_index = (
        jnp.arange(pencils, dtype=jnp.int32)[None, :]
        + pencils * jnp.arange(inner_size, dtype=jnp.int32)[:, None]
    )
    stored = lax.axis_index("gy") * y_local + jnp.arange(y_local, dtype=jnp.int32)
    y_index = stored // inner_length + y_total // inner_length * (stored % inner_length)
    x_waves = wave_number(x_index, inner_size * pencils)
    y_waves = wave_number(y_index, y_total)
    lateral = x_waves[:, :, None] ** 2 + y_waves[None, None, :] ** 2
    kz_square = ((omegas * reference_slowness) ** 2)[:, None, None, None] - lateral[None]
    kz_root = jnp.sqrt(jnp.abs(kz_square))
    travels = kz_square >= 0.0
    amplitude = jnp.where(travels, 1.0, jnp.exp(-kz_root * depth_interval))
    angles = jnp.where(travels, polarities[:, None, None, None] * kz_root * depth_interval, 0.0)
    return rotate(blocks, amplitude * jnp.cos(angles), amplitude * jnp.sin(angles))


def apply_screen(wave_field, slowness_now, omegas, polarities):
    phases = (polarities * omegas)[:, None, None] * (
        (slowness_now - reference_slowness) * depth_interval
    )[None]
    return rotate(wave_field, jnp.cos(phases), jnp.sin(phases))


def per_device(wavefields, slowness, freq_index):
    x_rows = wavefields.shape[3]
    y_cols = wavefields.shape[4]
    pencils = lax.axis_size("gy")
    freq_devs = lax.axis_size("freq")
    fld_devs = lax.axis_size("fld")
    column_width = y_cols // (freq_devs * fld_devs)
    omegas = omega_unit * freq_index.astype(jnp.float32)
    per_side = wavefields.shape[2] // fld_devs
    regrouped = wavefields.reshape(2, 1, fld_devs, per_side, x_rows, y_cols)
    paired = lax.all_to_all(regrouped, "fld", split_axis=2, concat_axis=1, tiled=True)
    wave_field = paired.reshape(2, fld_devs * per_side, x_rows, y_cols)
    local_omegas = lax.dynamic_slice_in_dim(omegas, lax.axis_index("fld") * per_side, per_side)
    omegas = jnp.tile(local_omegas, fld_devs)
    polarities = jnp.repeat(jnp.array([-1.0, 1.0], jnp.float32), per_side)
    batches = wave_field.shape[1]
    images = []
    for depth_step in range(DEPTH):
        wave_field = forward_rows(wave_field)
        blocks = wave_field.reshape(2, batches, x_rows, pencils, y_cols // pencils)
        blocks = lax.all_to_all(blocks, "gy", split_axis=3, concat_axis=3, tiled=True)
        blocks = forward_columns(blocks)
        blocks = propagate(blocks, omegas, polarities, y_cols)
        blocks = inverse_columns(blocks)
        blocks = lax.all_to_all(blocks, "gy", split_axis=3, concat_axis=3, tiled=True)
        wave_field = inverse_rows(blocks.reshape(2, batches, x_rows, y_cols))
        wave_field = apply_screen(wave_field, slowness[depth_step], omegas, polarities)
        source = wave_field[:, :per_side]
        receiver = wave_field[:, per_side:]
        summed = jnp.sum(source[0] * receiver[0] + source[1] * receiver[1], axis=0)
        partial_image = summed.reshape(x_rows, freq_devs * fld_devs, column_width)[None]
        images.append(
            lax.psum_scatter(partial_image, ("freq", "fld"), scatter_dimension=2, tiled=True)
        )
    combined = jnp.concatenate(images, axis=0)
    return combined.reshape(DEPTH, x_rows, column_width)


def solution(mesh):
    placed = (P("fld", None, ("shot", "freq"), "gy", None), P(None, "gy", None), P("freq"))
    return jax.shard_map(
        per_device,
        mesh=mesh,
        in_specs=placed,
        out_specs=P("shot", "gy", ("freq", "fld")),
        check_vma=False,
    )
```

profile of v0, /device:TPU:0, one launch (start us, length us, event | category | flops | bytes accessed | tf_op | source)
XLA Modules:
  0.0 677.4 jit_solution(15536558963621516833)
XLA Ops:
  6.5 4.8 copy.383
  11.3 5.6 all-to-all-start
  18.7 2.7 all-to-all-done
  21.4 3.2 copy.295
  24.6 3.7 fusion.54
  29.8 5.3 fusion.29
  35.1 7.3 %copy.203 = f32[2,2,256,4,256]{4,0,2,1,3:T(2,128)} copy(f32[2,2,256,4,256]{2,4,3,1,0:T(8,128)} %bitcast.290) | data formatting | bytes 8388608 | tf_op jit(solution)/shard_map/reshape;reshape | solution.py:141
  42.3 6.6 all-to-all-start.1
  60.9 81.8 %all-to-all-done.1 = f32[2,2,256,4,256]{4,0,2,1,3:T(2,128)} async-done(((f32[2,2,256,4,256]{4,0,2,1,3:T(2,128)}), f32[2,2,256,4,256]{4,0,2,1,3:T(2,128)}, u32[]{:S(2)}, u32[]{:S(2)}) %all-to-all-start.1) | async-done | bytes 4194336 | tf_op jit(solution)/shard_map/all_to_all | solution.py:142
  142.7 14.5 %fusion.57 = f32[2,2,256,4,256]{4,3,2,1,0:T(4,128)S(1)} fusion(f32[2,2,256,4,256]{4,0,2,1,3:T(2,128)} %all-to-all-done.1, f32[1,4,2,4]{1,3,0,2:T(4,128)} %copy.196, f32[1,4,2,4]{1,3,0,2:T(4,128)} %copy.195), kind=kOutput, calls=%fused_computation.79 | convolution fusion | flops 100663360 | bytes 8388864 | tf_op jit(solution)/shard_map/cbnsy,csdk->dbnky/dot_general | solution.py:18
  160.0 7.3 %fusion.72 = f32[2,2,256,4,256]{4,2,3,1,0:T(8,128)S(1)} fusion(f32[2,2,256,4,256]{4,3,2,1,0:T(4,128)S(1)} %pad_maximum_fusion.1, f32[1,256,2,256]{1,3,0,2:T(8,128)S(1)} %copy-done.6, f32[1,256,2,256]{1,3,0,2:T(8,128)S(1)} %copy-done.8), kind=kOutput, calls=%fused_computation.84 | convolution fusion | flops 6442713088 | bytes 9437184 | tf_op jit(solution)/shard_map/cbnky,cndm->dbmky/dot_general | solution.py:18
  167.3 8.5 %multiply_subtract_fusion.7 = (f32[1,2,256,4,256]{4,2,3,1,0:T(8,128)S(1)}, f32[1,2,256,4,256]{4,2,3,1,0:T(8,128)S(1)}) fusion(f32[2,2,256,4,256]{4,2,3,1,0:T(8,128)S(1)} %fusion.72, f32[256,4,256]{2,0,1:T(8,128)S(1)} %get-tuple-element.44, f32[2]{0:T(128)S(1)} %copy-done.37, f32[256,4,256]{2,0,1:T(8,128)S(1)} %get-tuple-element.43, ...), kind=kLoop, calls=%fused_computation.107 | loop fusion | flops 5767168 | bytes 10747912 | tf_op jit(solution)/shard_map/sub | solution.py:46
  175.8 7.2 %fusion.75 = f32[2,256,2,4,256]{4,1,3,2,0:T(8,128)S(1)} fusion(f32[1,2,256,4,256]{4,2,3,1,0:T(8,128)S(1)} %get-tuple-element.8, f32[1,2,256,4,256]{4,2,3,1,0:T(8,128)S(1)} %get-tuple-element.7, f32[1,256,2,256]{1,3,2,0:T(8,128)S(1)} %get-tuple-element.38, f32[1,256,2,256]{1,3,2,0:T(8,128)S(1)} %get-tuple-element.35), kind=kOutput, calls=%fused_computation.85 | convolution fusion | flops 6443761664 | bytes 9437184 | tf_op jit(solution)/shard_map/cbmky,cmdn->dbnky/dot_general | solution.py:18
  183.0 2.7 copy.382
  186.9 9.5 %fusion.20 = f32[2,2,256,4,256]{4,3,2,1,0:T(4,128)S(1)} fusion(f32[1,4,2,4]{1,3,0,2:T(4,128)S(1)} %copy-done.35, f32[1,4,2,4]{1,3,0,2:T(4,128)S(1)} %copy-done.33, f32[1,2,256,4,256]{4,3,2,1,0:T(4,128)S(1)} %get-tuple-element.18, f32[1,2,256,4,256]{4,3,2,1,0:T(4,128)S(1)} %get-tuple-element.17), kind=kOutput, calls=%fused_computation.35 | convolution fusion | flops 102760512 | bytes 8388864 | tf_op jit(solution)/shard_map/cbnky,ckds->dbnsy/dot_general | solution.py:18
  196.4 2.8 copy.213
  199.2 5.4 all-to-all-start.2
  204.8 2.8 add_bitcast_fusion
  210.2 87.3 %all-to-all-done.2 = f32[2,2,256,4,256]{4,2,1,0,3:T(8,128)} async-done(((f32[2,2,256,4,256]{4,2,1,0,3:T(8,128)}), f32[2,2,256,4,256]{4,2,1,0,3:T(8,128)}, u32[]{:S(2)}, u32[]{:S(2)}) %all-to-all-start.2) | async-done | bytes 4194336 | tf_op jit(solution)/shard_map/all_to_all | solution.py:146
  297.5 5.3 copy.214
  302.8 5.6 copy.259
  308.4 5.3 convolution_bitcast_fusion.1
  314.2 3.7 fusion.17
  319.5 2.9 copy.291
  324.2 10.6 %fusion.86 = (f32[1,2,256,1024]{2,3,1,0:T(8,128)S(1)}, f32[1,2,256,1024]{2,3,1,0:T(8,128)}) fusion(f32[1,2,256,8,128]{2,4,3,1,0:T(8,128)} %copy.292, f32[1,2,256,8,128]{2,4,3,1,0:T(8,128)} %copy.291, f32[256,1024]{0,1:T(8,128)} %copy.219, f32[2]{0:T(128)} %broadcast_multiply_fusion.6), kind=kLoop, calls=%fused_computation.90 | loop fusion | flops 3670016 | bytes 9437192 | tf_op jit(solution)/shard_map/sub | solution.py:46
  336.7 2.9 copy.287
  339.6 5.5 fusion.71
  346.5 5.2 fusion.15
  351.7 7.3 %copy.227 = f32[2,2,256,4,256]{4,0,2,1,3:T(2,128)} copy(f32[2,2,256,4,256]{2,4,3,1,0:T(8,128)} %bitcast.288) | data formatting | bytes 8388608 | tf_op jit(solution)/shard_map/reshape;reshape | solution.py:141
  359.0 96.6 %all_to_all.29 = f32[2,2,256,4,256]{4,0,2,1,3:T(2,128)S(1)} all-to-all(f32[2,2,256,4,256]{4,0,2,1,3:T(2,128)} %copy.227), channel_id=1, replica_groups=mesh['shot'=2,'gy'=4,'freq'=2,'fld'=2] {'gy'}, dimensions={3} | all-to-all | bytes 8388608 | tf_op jit(solution)/shard_map/all_to_all | solution.py:142
  455.5 10.3 %fusion.64 = f32[2,2,256,4,256]{4,3,2,1,0:T(4,128)S(1)} fusion(f32[2,2,256,4,256]{4,0,2,1,3:T(2,128)S(1)} %all_to_all.29, f32[1,4,2,4]{1,3,0,2:T(4,128)S(1)} %copy-done.28, f32[1,4,2,4]{1,3,0,2:T(4,128)S(1)} %copy-done.27), kind=kOutput, calls=%fused_computation.80 | convolution fusion | flops 100663360 | bytes 8388864 | tf_op jit(solution)/shard_map/cbnsy,csdk->dbnky/dot_general | solution.py:18
  468.4 7.3 %fusion.78 = f32[2,2,256,4,256]{4,2,3,1,0:T(8,128)S(1)} fusion(f32[2,2,256,4,256]{4,3,2,1,0:T(4,128)S(1)} %pad_maximum_fusion.6, f32[1,256,2,256]{1,3,0,2:T(8,128)S(1)} %copy-done.7, f32[1,256,2,256]{1,3,0,2:T(8,128)S(1)} %copy-done.9), kind=kOutput, calls=%fused_computation.86 | convolution fusion | flops 6442713088 | bytes 9437184 | tf_op jit(solution)/shard_map/cbnky,cndm->dbmky/dot_general | solution.py:18
  475.8 8.7 %multiply_subtract_fusion.2 = (f32[1,2,256,4,256]{4,2,3,1,0:T(8,128)S(1)}, f32[1,2,256,4,256]{4,2,3,1,0:T(8,128)S(1)}) fusion(f32[2,2,256,4,256]{4,2,3,1,0:T(8,128)S(1)} %fusion.78, f32[256,4,256]{2,0,1:T(8,128)S(1)} %copy-done.1, f32[2]{0:T(128)S(1)} %copy-done.39, f32[256,4,256]{2,0,1:T(8,128)S(1)} %get-tuple-element.43, pred[256,4,256]{2,0,1:T(8,128)(4,1)S(1)} %fusion.90), kind=kLoop, calls=%fused_computation.97 | loop fusion | flops 5767168 | bytes 10747912 | tf_op jit(solution)/shard_map/sub | solution.py:46
  484.5 7.2 %fusion.81 = f32[2,256,2,4,256]{4,1,3,2,0:T(8,128)S(1)} fusion(f32[1,2,256,4,256]{4,2,3,1,0:T(8,128)S(1)} %get-tuple-element.6, f32[1,2,256,4,256]{4,2,3,1,0:T(8,128)S(1)} %get-tuple-element.5, f32[1,256,2,256]{1,3,2,0:T(8,128)S(1)} %copy-done.5, f32[1,256,2,256]{1,3,2,0:T(8,128)S(1)} %copy-done.3), kind=kOutput, calls=%fused_computation.87 | convolution fusion | flops 6443761664 | bytes 9437184 | tf_op jit(solution)/shard_map/cbmky,cmdn->dbnky/dot_general | solution.py:18
  491.7 2.7 copy.381
  495.6 9.7 %fusion.6 = f32[2,2,256,4,256]{4,3,2,1,0:T(4,128)S(1)} fusion(f32[1,4,2,4]{1,3,0,2:T(4,128)S(1)} %copy-done.36, f32[1,4,2,4]{1,3,0,2:T(4,128)S(1)} %copy-done.34, f32[1,2,256,4,256]{4,3,2,1,0:T(4,128)S(1)} %get-tuple-element.14, f32[1,2,256,4,256]{4,3,2,1,0:T(4,128)S(1)} %get-tuple-element.13), kind=kOutput, calls=%fused_computation.19 | convolution fusion | flops 102760512 | bytes 8388864 | tf_op jit(solution)/shard_map/cbnky,ckds->dbnsy/dot_general | solution.py:18
  505.3 2.8 copy.234
  508.1 4.9 all-to-all-start.4
  514.5 2.8 fusion.89
  517.4 87.8 %all-to-all-done.4 = f32[2,2,256,4,256]{4,2,1,0,3:T(8,128)} async-done(((f32[2,2,256,4,256]{4,2,1,0,3:T(8,128)}), f32[2,2,256,4,256]{4,2,1,0,3:T(8,128)}, u32[]{:S(2)}, u32[]{:S(2)}) %all-to-all-start.4) | async-done | bytes 4194336 | tf_op jit(solution)/shard_map/all_to_all | solution.py:146
  605.2 5.5 copy.235
  610.7 5.6 copy.271
  616.3 5.3 convolution_bitcast_fusion
  622.3 3.7 fusion.3
  626.0 2.3 fusion.181
  630.3 2.9 copy.294
  633.2 9.5 %fusion.84 = (f32[1,2,256,1024]{2,3,1,0:T(8,128)S(1)}, f32[1,2,256,1024]{2,3,1,0:T(8,128)S(1)}) fusion(f32[1,2,256,8,128]{2,4,3,1,0:T(8,128)} %copy.294, f32[1,2,256,8,128]{2,4,3,1,0:T(8,128)S(1)} %copy.293, f32[256,1024]{0,1:T(8,128)S(1)} %copy.240, f32[2]{0:T(128)S(1)} %copy-done.40), kind=kLoop, calls=%fused_computation.88 | loop fusion | flops 3670016 | bytes 9437192 | tf_op jit(solution)/shard_map/sub | solution.py:46
  644.0 24.2 %reduce-scatter.5.cloned.1.call-done = f32[1,256,1,256]{1,3,2,0:T(8,128)} async-done(((f32[1,256,4,256]{1,3,2,0:T(8,128)}), f32[1,256,1,256]{1,3,2,0:T(8,128)}) %reduce-scatter.5.cloned.1.call-update) | async-done | bytes 262160 | tf_op jit(solution)/shard_map/reduce_scatter | solution.py:154
  (150 shorter events, 38.8 us)
Async XLA Ops:
  11.3 10.1 %all-to-all-start = ((f32[2,1,2,1,256,1024]{5,4,0,3,1,2:T(8,128)}), f32[2,1,2,1,256,1024]{5,4,0,3,1,2:T(8,128)}, u32[]{:S(2)}, u32[]{:S(2)}) async-start(f32[2,1,2,1,256,1024]{5,4,0,3,1,2:T(8,128)} %bitcast.285), calls=%async_computation | async-start | bytes 8388608 | tf_op jit(solution)/shard_map/all_to_all | solution.py:132
  18.7 5.9 copy-start.22
  29.8 5.3 copy-start.18
  29.8 5.3 copy-start.20
  42.3 9.3 %copy-start.41 = (s32[2]{0:T(128)S(1)}, s32[2]{0:T(128)}, u32[]{:S(2)}) copy-start(s32[2]{0:T(128)} %param.6) | copy-start | bytes 28
  42.3 100.4 %all-to-all-start.1 = ((f32[2,2,256,4,256]{4,0,2,1,3:T(2,128)}), f32[2,2,256,4,256]{4,0,2,1,3:T(2,128)}, u32[]{:S(2)}, u32[]{:S(2)}) async-start(f32[2,2,256,4,256]{4,0,2,1,3:T(2,128)} %copy.203), calls=%async_computation.1 | async-start | bytes 8388608 | tf_op jit(solution)/shard_map/all_to_all | solution.py:142
  60.1 115.7 %copy-start.2 = (f32[1,256,2,256]{1,3,2,0:T(8,128)}, f32[1,256,2,256]{1,3,2,0:T(8,128)S(1)}, u32[]{:S(2)}) copy-start(f32[1,256,2,256]{1,3,2,0:T(8,128)S(1)} %get-tuple-element.35) | copy-start | bytes 1572868
  60.1 115.7 %copy-start.4 = (f32[1,256,2,256]{1,3,2,0:T(8,128)}, f32[1,256,2,256]{1,3,2,0:T(8,128)S(1)}, u32[]{:S(2)}) copy-start(f32[1,256,2,256]{1,3,2,0:T(8,128)S(1)} %get-tuple-element.38) | copy-start | bytes 1572868
  60.9 106.4 %copy-start = (f32[256,4,256]{2,0,1:T(8,128)}, f32[256,4,256]{2,0,1:T(8,128)S(1)}, u32[]{:S(2)}) copy-start(f32[256,4,256]{2,0,1:T(8,128)S(1)} %get-tuple-element.44) | copy-start | bytes 3145732
  142.7 14.5 %copy-start.12 = (f32[256,4]{1,0:T(8,128)S(1)}, f32[256,4]{1,0:T(8,128)}, u32[]{:S(2)}) copy-start(f32[256,4]{1,0:T(8,128)} %copy.206) | copy-start | bytes 12292
  158.8 1.0 copy-start.6
  158.8 1.2 copy-start.8
  160.0 7.3 %copy-start.37 = (f32[2]{0:T(128)S(1)}, f32[2]{0:T(128)}, u32[]{:S(2)}) copy-start(f32[2]{0:T(128)} %constant.219.clone) | copy-start | bytes 28
  183.0 2.7 copy-start.10
  185.7 1.2 copy-start.33
  185.7 1.2 copy-start.35
  199.2 5.4 copy-start.32
  199.2 5.5 copy-start.31
  199.2 98.3 %all-to-all-start.2 = ((f32[2,2,256,4,256]{4,2,1,0,3:T(8,128)}), f32[2,2,256,4,256]{4,2,1,0,3:T(8,128)}, u32[]{:S(2)}, u32[]{:S(2)}) async-start(f32[2,2,256,4,256]{4,2,1,0,3:T(8,128)} %copy.213), calls=%async_computation.2 | async-start | bytes 8388608 | tf_op jit(solution)/shard_map/all_to_all | solution.py:146
  204.7 109.5 %copy-start.23 = (f32[1,8,2,8]{1,3,0,2:T(8,128)}, f32[1,8,2,8]{1,3,0,2:T(8,128)S(1)}, u32[]{:S(2)}) copy-start(f32[1,8,2,8]{1,3,0,2:T(8,128)S(1)} %copy.190) | copy-start | bytes 1540
  204.8 109.4 %copy-start.25 = (f32[1,8,2,8]{1,3,0,2:T(8,128)}, f32[1,8,2,8]{1,3,0,2:T(8,128)S(1)}, u32[]{:S(2)}) copy-start(f32[1,8,2,8]{1,3,0,2:T(8,128)S(1)} %copy.191) | copy-start | bytes 1540
  207.6 1.4 copy-start.38
  209.0 104.7 %copy-start.29 = (f32[8,128]{1,0:T(8,128)}, f32[8,128]{1,0:T(8,128)S(1)}, u32[]{:S(2)}) copy-start(f32[8,128]{1,0:T(8,128)S(1)} %fusion.154) | copy-start | bytes 12292
  302.8 5.6 copy-start.14
  302.8 5.6 copy-start.16
  345.5 0.9 copy-start.19
  345.5 1.0 copy-start.21
  359.0 96.6 %copy-start.27 = (f32[1,4,2,4]{1,3,0,2:T(4,128)S(1)}, f32[1,4,2,4]{1,3,0,2:T(4,128)}, u32[]{:S(2)}) copy-start(f32[1,4,2,4]{1,3,0,2:T(4,128)} %copy.195) | copy-start | bytes 388
  359.0 96.6 %copy-start.28 = (f32[1,4,2,4]{1,3,0,2:T(4,128)S(1)}, f32[1,4,2,4]{1,3,0,2:T(4,128)}, u32[]{:S(2)}) copy-start(f32[1,4,2,4]{1,3,0,2:T(4,128)} %copy.196) | copy-start | bytes 388
  455.5 10.3 %copy-start.13 = (f32[256,4]{1,0:T(8,128)S(1)}, f32[256,4]{1,0:T(8,128)}, u32[]{:S(2)}) copy-start(f32[256,4]{1,0:T(8,128)} %copy.206) | copy-start | bytes 12292
  467.2 1.0 copy-start.7
  467.2 1.2 copy-start.9
  468.4 7.3 %copy-start.1 = (f32[256,4,256]{2,0,1:T(8,128)S(1)}, f32[256,4,256]{2,0,1:T(8,128)}, u32[]{:S(2)}) copy-start(f32[256,4,256]{2,0,1:T(8,128)} %copy-done) | copy-start | bytes 3145732
  468.4 7.3 %copy-start.39 = (f32[2]{0:T(128)S(1)}, f32[2]{0:T(128)}, u32[]{:S(2)}) copy-start(f32[2]{0:T(128)} %constant.219.clone) | copy-start | bytes 28
  475.8 8.7 %copy-start.3 = (f32[1,256,2,256]{1,3,2,0:T(8,128)S(1)}, f32[1,256,2,256]{1,3,2,0:T(8,128)}, u32[]{:S(2)}) copy-start(f32[1,256,2,256]{1,3,2,0:T(8,128)} %copy-done.2) | copy-start | bytes 1572868
  475.8 8.7 %copy-start.5 = (f32[1,256,2,256]{1,3,2,0:T(8,128)S(1)}, f32[1,256,2,256]{1,3,2,0:T(8,128)}, u32[]{:S(2)}) copy-start(f32[1,256,2,256]{1,3,2,0:T(8,128)} %copy-done.4) | copy-start | bytes 1572868
  491.7 2.7 copy-start.11
  494.4 1.2 copy-start.34
  494.4 1.2 copy-start.36
  508.1 97.1 %all-to-all-start.4 = ((f32[2,2,256,4,256]{4,2,1,0,3:T(8,128)}), f32[2,2,256,4,256]{4,2,1,0,3:T(8,128)}, u32[]{:S(2)}, u32[]{:S(2)}) async-start(f32[2,2,256,4,256]{4,2,1,0,3:T(8,128)} %copy.234), calls=%async_computation.5 | async-start | bytes 8388608 | tf_op jit(solution)/shard_map/all_to_all | solution.py:146
  512.9 131.1 %reduce-scatter.3.cloned.1.call-start = ((), (), s32[]{:S(2)}) async-start(), calls=%async_computation.7 | async-start | bytes 1310720 | tf_op jit(solution)/shard_map/reduce_scatter | solution.py:154
  517.4 150.9 %reduce-scatter.5.cloned.1.call-start = ((), (), s32[]{:S(2)}) async-start(), calls=%async_computation.8 | async-start | bytes 1310720 | tf_op jit(solution)/shard_map/reduce_scatter | solution.py:154
  610.7 5.6 copy-start.15
  610.7 5.6 copy-start.17
  616.3 5.3 copy-start.30
  621.6 0.7 copy-start.24
  621.6 0.7 copy-start.26
  630.3 2.9 copy-start.40
Sparse Core Ops, SparseCore 0:
  517.5 26.3 reduce-scatter.2
  644.1 24.0 reduce-scatter.4
where the time goes:
time: 686 us; the launch traced here: 677 us
  waiting for transfers between devices  284 us (41%)
  matrix products  111 us (16%)
  blocking collectives  96.6 us (14%)
  local copies, waits for them, and re-layouts  84.5 us (12%)
  other arithmetic  63.5 us (9%)
  starting transfers between devices  22.5 us (3%)
  between operations  15.8 us (2%)
    all_to_all x3, waiting for transfers between devices, per_device(): lax.all_to_all(blocks, 'gy', split_axis=3, concat_axis=3, tiled=True)  257 us
    dot_general x16, matrix products, contract(): jnp.einsum(pattern, values, matrix, precision=lax.Precision.HIGHEST, pref...  111 us
    all_to_all x1, blocking collectives, per_device(): lax.all_to_all(blocks, 'gy', split_axis=3, concat_axis=3, tiled=True)  96.6 us
    sub x12, other arithmetic, rotate(): real_part * cosine - imag_part * sine_part  44 us
    reduce_scatter x2, waiting for transfers between devices, per_device(): lax.psum_scatter(partial_image, ('freq', 'fld'), scatter_dimension=2, til...  24.2 us
    all_to_all x3, starting transfers between devices, per_device(): lax.all_to_all(blocks, 'gy', split_axis=3, concat_axis=3, tiled=True)  16.9 us
    another operation x2, local copies, waits for them, and re-layouts, per_device(): blocks = wave_field.reshape(2, batches, x_rows, pencils, y_cols // pencils)  14.5 us
  transfers between devices with their start and end apart: 6, of which 5 were waited for; matrix products, arithmetic and copies ran while one was open for 9% of the time, Pallas kernels for 0%

commit v1 on v0

--- a/solution.py
+++ b/solution.py
@@ -1,8 +1,12 @@
+import functools
 import math
 
 import jax
 import jax.numpy as jnp
+import numpy as np
 from jax import lax
+from jax.experimental import pallas as pl
+from jax.experimental.pallas import tpu as pltpu
 from jax.sharding import PartitionSpec as P
 
 DEPTH = 2
@@ -119,7 +123,7 @@
     return rotate(wave_field, jnp.cos(phases), jnp.sin(phases))
 
 
-def per_device(wavefields, slowness, freq_index):
+def per_device_pencils(wavefields, slowness, freq_index):
     x_rows = wavefields.shape[3]
     y_cols = wavefields.shape[4]
     pencils = lax.axis_size("gy")
@@ -157,7 +161,557 @@
     return combined.reshape(DEPTH, x_rows, column_width)
 
 
+axes = ("shot", "gy", "freq", "fld")
+lanes = 128
+y_radix = 8
+x_radix = 4
+row_block = 64
+strip = 16
+
+
+def fits_one_field_per_chip(sizes, shape):
+    return (
+        sizes["gy"] == 4
+        and sizes["freq"] == 2
+        and sizes["fld"] == 2
+        and shape[2] == 2
+        and shape[4] == y_radix * lanes
+        and shape[3] % row_block == 0
+        and shape[3] * 4 == shape[4]
+    )
+
+
+def route(sizes, target):
+    pairs = []
+    for place in np.ndindex(*(sizes[axis] for axis in axes)):
+        goal = target(*place)
+        if goal is not None:
+            dims = tuple(sizes[axis] for axis in axes)
+            pairs.append(
+                (int(np.ravel_multi_index(place, dims)), int(np.ravel_multi_index(goal, dims)))
+            )
+    return pairs
+
+
+def split_constant(matrix):
+    upper = matrix.astype(jnp.bfloat16)
+    lower = (matrix - upper.astype(np.float64)).astype(jnp.bfloat16)
+    return upper, lower
+
+
+def dft_parts(length, polarity):
+    indices = np.arange(length)
+    angles = 2.0 * np.pi / length * (indices[:, None] * indices[None, :] % length)
+    return np.cos(angles), polarity * np.sin(angles)
+
+
+def row_matrix(length, polarity):
+    cosine, sine = dft_parts(length, polarity)
+    return split_constant(np.block([[cosine, sine], [-sine, cosine]]))
+
+
+def column_matrix(length, polarity):
+    cosine, sine = dft_parts(length, polarity)
+    return split_constant(np.block([[cosine, -sine], [sine, cosine]]))
+
+
+def add(one, two):
+    return one[0] + two[0], one[1] + two[1]
+
+
+def subtract(one, two):
+    return one[0] - two[0], one[1] - two[1]
+
+
+def multiply(one, two):
+    return one[0] * two[0] - one[1] * two[1], one[0] * two[1] + one[1] * two[0]
+
+
+def conjugate(one):
+    return one[0], -one[1]
+
+
+def quarter_turn(one, polarity):
+    if polarity > 0:
+        return -one[1], one[0]
+    return one[1], -one[0]
+
+
+def dft4(terms, polarity):
+    even = add(terms[0], terms[2])
+    odd = subtract(terms[0], terms[2])
+    even_other = add(terms[1], terms[3])
+    odd_other = quarter_turn(subtract(terms[1], terms[3]), polarity)
+    return [
+        add(even, even_other),
+        add(odd, odd_other),
+        subtract(even, even_other),
+        subtract(odd, odd_other),
+    ]
+
+
+def eighth_turn(one, polarity):
+    half = math.sqrt(0.5)
+    if polarity > 0:
+        return (one[0] - one[1]) * half, (one[0] + one[1]) * half
+    return (one[0] + one[1]) * half, (one[1] - one[0]) * half
+
+
+def dft8(terms, polarity):
+    sums = [add(terms[a], terms[a + 4]) for a in range(4)]
+    differences = [subtract(terms[a], terms[a + 4]) for a in range(4)]
+    turned = [
+        differences[0],
+        eighth_turn(differences[1], polarity),
+        quarter_turn(differences[2], polarity),
+        quarter_turn(eighth_turn(differences[3], polarity), polarity),
+    ]
+    even = dft4(sums, polarity)
+    odd = dft4(turned, polarity)
+    return [even[k // 2] if k % 2 == 0 else odd[k // 2] for k in range(8)]
+
+
+def two_parts(values):
+    upper = values.astype(jnp.bfloat16)
+    lower = (values - upper.astype(jnp.float32)).astype(jnp.bfloat16)
+    return upper, lower
+
+
+def dot(left, right):
+    return jnp.dot(left, right, preferred_element_type=jnp.float32)
+
+
+def rows_product(values, upper_ref, lower_ref):
+    upper, lower = two_parts(values)
+    return dot(upper, upper_ref[...]) + dot(lower, upper_ref[...]) + dot(upper, lower_ref[...])
+
+
+def columns_product(upper_ref, lower_ref, upper, lower):
+    return dot(upper_ref[...], upper) + dot(upper_ref[...], lower) + dot(lower_ref[...], upper)
+
+
+def stack_blocks(terms):
+    return jnp.concatenate([jnp.concatenate(term, axis=1) for term in terms], axis=0)
+
+
+def unstack_blocks(values, rows):
+    blocks = [values[k * rows : (k + 1) * rows] for k in range(y_radix)]
+    return [(block[:, :lanes], block[:, lanes:]) for block in blocks]
+
+
+def y_twiddle(table_ref, k):
+    return table_ref[k, 0:1, :], table_ref[k, 1:2, :]
+
+
+def forward_y(terms, table_ref, upper_ref, lower_ref):
+    rows = terms[0][0].shape[0]
+    turned = dft8(terms, -1.0)
+    turned = [multiply(turned[k], y_twiddle(table_ref, k)) for k in range(y_radix)]
+    return unstack_blocks(rows_product(stack_blocks(turned), upper_ref, lower_ref), rows)
+
+
+def inverse_y(terms, table_ref, upper_ref, lower_ref):
+    rows = terms[0][0].shape[0]
+    inner = unstack_blocks(rows_product(stack_blocks(terms), upper_ref, lower_ref), rows)
+    inner = [multiply(inner[k], conjugate(y_twiddle(table_ref, k))) for k in range(y_radix)]
+    return dft8(inner, 1.0)
+
+
+def lane_block(index):
+    return slice(index * lanes, (index + 1) * lanes)
+
+
+def origin_kernel(place_ref, field_ref, table_ref, upper_ref, lower_ref, *outs):
+    sign = (1 - 2 * place_ref[3]).astype(jnp.float32)
+    terms = []
+    for a in range(y_radix):
+        term = (field_ref[0, 0, :, lane_block(a)], field_ref[1, 0, :, lane_block(a)])
+        terms.append((term[0] * sign, term[1] * sign) if a % 2 else term)
+    spectrum = forward_y(terms, table_ref, upper_ref, lower_ref)
+    for k in range(y_radix):
+        for part in range(2):
+            outs[k // 2][0, part, :, lane_block(k % 2)] = spectrum[k][part]
+
+
+def read_y_blocks(blocks):
+    return [
+        tuple(blocks[k // 2][part, :, lane_block(k % 2)] for part in range(2))
+        for k in range(y_radix)
+    ]
+
+
+def read_screen(screen_ref, a):
+    return screen_ref[0, 0, :, lane_block(a)], screen_ref[0, 1, :, lane_block(a)]
+
+
+def turn_kernel(keeps_field, *refs):
+    blocks, rest = refs[:4], refs[4:]
+    screen_ref, table_ref, inv_upper, inv_lower, upper_ref, lower_ref = rest[:6]
+    outs = rest[6:]
+    terms = inverse_y(read_y_blocks(blocks), table_ref, inv_upper, inv_lower)
+    terms = [multiply(terms[a], read_screen(screen_ref, a)) for a in range(y_radix)]
+    if keeps_field:
+        for a in range(y_radix):
+            for part in range(2):
+                outs[4][part, :, lane_block(a)] = terms[a][part]
+    spectrum = forward_y(terms, table_ref, upper_ref, lower_ref)
+    for k in range(y_radix):
+        for part in range(2):
+            outs[k // 2][part, :, lane_block(k % 2)] = spectrum[k][part]
+
+
+def image_kernel(own_ready, place_ref, *refs):
+    own_count = 1 if own_ready else 4
+    own, refs = refs[:own_count], refs[own_count:]
+    blocks, refs = refs[:4], refs[4:]
+    screen_ref, table_ref, inv_upper, inv_lower = refs[:4]
+    outs, quarters = refs[4:8], refs[8]
+    other = inverse_y(read_y_blocks(blocks), table_ref, inv_upper, inv_lower)
+    if not own_ready:
+        mine = inverse_y(read_y_blocks(own), table_ref, inv_upper, inv_lower)
+    for a in range(y_radix):
+        screen = read_screen(screen_ref, a)
+        if own_ready:
+            near = (own[0][0, :, lane_block(a)], own[0][1, :, lane_block(a)])
+        else:
+            near = multiply(mine[a], screen)
+        far = multiply(other[a], conjugate(screen))
+        quarters[a // 2, :, lane_block(a % 2)] = near[0] * far[0] + near[1] * far[1]
+    for r in range(4):
+        outs[r][...] = quarters[lax.bitwise_xor(place_ref[1], r)]
+
+
+def x_kernel(
+    swap_ref, b0, b1, b2, b3, table_in, table_out, move_ref,
+    upper_ref, lower_ref, inv_upper, inv_lower, o0, o1, o2, o3, high, low, held,
+):
+    blocks, outs = (b0, b1, b2, b3), (o0, o1, o2, o3)
+    rows = b0.shape[1]
+
+    def wide(table, k, part, span):
+        values = table[k, part, span, :]
+        return jnp.concatenate([values] * (b0.shape[2] // lanes), axis=1)
+
+    def actual(k, swaps):
+        return k if k % 2 == 0 else lax.bitwise_xor(k, 2 * swaps)
+
+    def gather_rows(step, carry):
+        span = pl.ds(pl.multiple_of(step * strip, strip), strip)
+        lower_span = pl.ds(pl.multiple_of(step * strip + rows, strip), strip)
+        terms = dft4([(block[0, span, :], block[1, span, :]) for block in blocks], -1.0)
+        for k in range(x_radix):
+            factor = (wide(table_in, k, 0, span), wide(table_in, k, 1, span))
+            real, imag = multiply(terms[k], factor)
+            goal = actual(k, swap_ref[0])
+            high[goal, span, :], low[goal, span, :] = two_parts(real)
+            high[goal, lower_span, :], low[goal, lower_span, :] = two_parts(imag)
+        return carry
+
+    lax.fori_loop(0, rows // strip, gather_rows, 0)
+
+    def one_block(k, carry):
+        values = columns_product(upper_ref, lower_ref, high[k], low[k])
+        moved = multiply((values[:rows], values[rows:]), (move_ref[k, 0], move_ref[k, 1]))
+        upper, lower = two_parts(jnp.concatenate(moved, axis=0))
+        held[k] = columns_product(inv_upper, inv_lower, upper, lower)
+        return carry
+
+    lax.fori_loop(0, x_radix, one_block, 0)
+
+    def scatter_rows(step, carry):
+        span = pl.ds(pl.multiple_of(step * strip, strip), strip)
+        lower_span = pl.ds(pl.multiple_of(step * strip + rows, strip), strip)
+        terms = []
+        for k in range(x_radix):
+            source = actual(k, swap_ref[1])
+            factor = (wide(table_out, k, 0, span), -wide(table_out, k, 1, span))
+            terms.append(multiply((held[source, span, :], held[source, lower_span, :]), factor))
+        terms = dft4(terms, 1.0)
+        for q in range(x_radix):
+            for part in range(2):
+                outs[q][part, span, :] = terms[q][part]
+        return carry
+
+    lax.fori_loop(0, rows // strip, scatter_rows, 0)
+
+
+def whole(array):
+    return pl.BlockSpec(array.shape, lambda *step: (0,) * array.ndim)
+
+
+smem = pl.BlockSpec(memory_space=pltpu.SMEM)
+vmem = pl.BlockSpec(memory_space=pltpu.VMEM)
+vmem_limit = 40 * 1024 * 1024
+
+
+def parameters(steps):
+    return pltpu.CompilerParams(
+        vmem_limit_bytes=vmem_limit, dimension_semantics=("arbitrary",) * steps
+    )
+
+
+def estimate(microseconds):
+    return pl.CostEstimate(
+        flops=int(microseconds * 1e9), bytes_accessed=int(microseconds * 3e6), transcendentals=0
+    )
+
+
+def origin_rows(field, place, table, matrices):
+    parts, freqs, rows, y_cols = field.shape
+    width = y_cols // 4
+    out = jax.ShapeDtypeStruct((freqs, parts, rows, width), jnp.float32)
+    return pl.pallas_call(
+        origin_kernel,
+        grid=(freqs, rows // row_block),
+        in_specs=[
+            smem,
+            pl.BlockSpec((parts, 1, row_block, y_cols), lambda j, i: (0, j, i, 0)),
+            whole(table),
+            whole(matrices[0]),
+            whole(matrices[1]),
+        ],
+        out_specs=[pl.BlockSpec((1, parts, row_block, width), lambda j, i: (j, 0, i, 0))] * 4,
+        out_shape=[out] * 4,
+        compiler_params=parameters(2),
+        cost_estimate=estimate(6),
+        name="origin_rows",
+    )(place, field, table, *matrices)
+
+
+def turn_rows(keeps_field, slot, blocks, screen, table, inverse, forward):
+    parts, rows, width = blocks[0].shape
+    y_cols = screen.shape[-1]
+    block = pl.BlockSpec((parts, row_block, width), lambda i: (0, i, 0))
+    full = pl.BlockSpec((parts, row_block, y_cols), lambda i: (0, i, 0))
+    out = [jax.ShapeDtypeStruct((parts, rows, width), jnp.float32)] * 4
+    out_specs = [block] * 4
+    if keeps_field:
+        out = out + [jax.ShapeDtypeStruct((parts, rows, y_cols), jnp.float32)]
+        out_specs = out_specs + [full]
+    return pl.pallas_call(
+        functools.partial(turn_kernel, keeps_field),
+        grid=(rows // row_block,),
+        in_specs=[block] * 4
+        + [pl.BlockSpec((1, 2, row_block, y_cols), lambda i: (slot, 0, i, 0))]
+        + [whole(array) for array in (table, *inverse, *forward)],
+        out_specs=out_specs,
+        out_shape=out,
+        compiler_params=parameters(1),
+        cost_estimate=estimate(5),
+        name="turn_rows",
+    )(*blocks, screen, table, *inverse, *forward)
+
+
+def image_rows(place, own, blocks, screen, table, inverse):
+    parts, rows, width = blocks[0].shape
+    y_cols = screen.shape[-1]
+    own_ready = len(own) == 1
+    block = pl.BlockSpec((parts, row_block, width), lambda i: (0, i, 0))
+    full = pl.BlockSpec((parts, row_block, y_cols), lambda i: (0, i, 0))
+    return pl.pallas_call(
+        functools.partial(image_kernel, own_ready),
+        grid=(rows // row_block,),
+        in_specs=[smem]
+        + ([full] if own_ready else [block] * 4)
+        + [block] * 4
+        + [pl.BlockSpec((1, 2, row_block, y_cols), lambda i: (0, 0, i, 0))]
+        + [whole(array) for array in (table, *inverse)],
+        out_specs=[pl.BlockSpec((row_block, width), lambda i: (i, 0))] * 4,
+        out_shape=[jax.ShapeDtypeStruct((rows, width), jnp.float32)] * 4,
+        scratch_shapes=[pltpu.VMEM((4, row_block, width), jnp.float32)],
+        compiler_params=parameters(1),
+        cost_estimate=estimate(4),
+        name="image_rows",
+    )(place, *own, *blocks, screen, table, *inverse)
+
+
+def move_columns(chunk, swaps, blocks, table_in, table_out, move, forward, inverse):
+    parts, rows, width = blocks[0].shape
+    move_block = pl.BlockSpec(
+        (x_radix, parts, rows, width), lambda i: (0, 0, 0, chunk)
+    )
+    block = whole(blocks[0])
+    return pl.pallas_call(
+        x_kernel,
+        grid=(1,),
+        in_specs=[smem] + [block] * 4 + [whole(table_in), whole(table_out), move_block]
+        + [whole(array) for array in (*forward, *inverse)],
+        out_specs=[block] * 4,
+        out_shape=[jax.ShapeDtypeStruct((parts, rows, width), jnp.float32)] * 4,
+        scratch_shapes=[
+            pltpu.VMEM((x_radix, parts * rows, width), jnp.bfloat16),
+            pltpu.VMEM((x_radix, parts * rows, width), jnp.bfloat16),
+            pltpu.VMEM((x_radix, parts * rows, width), jnp.float32),
+        ],
+        compiler_params=parameters(1),
+        cost_estimate=estimate(8),
+        name="move_columns",
+    )(swaps, *blocks, table_in, table_out, move, *forward, *inverse)
+
+
+def y_table(core, y_cols):
+    k = (jnp.arange(y_radix, dtype=jnp.int32) ^ (4 * core))[:, None]
+    r = jnp.arange(lanes, dtype=jnp.int32)[None, :]
+    angles = 2.0 * math.pi / y_cols * (k * r % y_cols).astype(jnp.float32)
+    return jnp.stack([jnp.cos(angles), -jnp.sin(angles)], axis=1)
+
+
+def x_table(order, x_total):
+    rows = x_total // x_radix
+    low_bit, high_bit = order & 1, order >> 1
+    slot = jnp.arange(x_radix, dtype=jnp.int32)
+    k = jnp.where(slot % 2 == 1, slot ^ (2 * low_bit), slot)
+    eighths = jnp.where(k % 2 == 1, 4 * high_bit, 0)
+    turns = jnp.array([0, 6, 4, 2], jnp.int32)
+    eighths = eighths + low_bit * turns[k]
+    row = jnp.arange(rows, dtype=jnp.int32)[None, :]
+    steps = (x_total // 8 * eighths[:, None] - k[:, None] * row) % x_total
+    angles = 2.0 * math.pi / x_total * steps.astype(jnp.float32)
+    table = jnp.stack([jnp.cos(angles), jnp.sin(angles)], axis=1)
+    return jnp.broadcast_to(table[..., None], table.shape + (lanes,))
+
+
+def move_table(omega, polarity, core, x_total, y_total):
+    k = jnp.arange(x_radix, dtype=jnp.int32)[:, None]
+    inner = jnp.arange(x_total // x_radix, dtype=jnp.int32)[None, :]
+    x_waves = wave_number(k + x_radix * inner, x_total)
+    ky = jnp.arange(y_radix // 2, dtype=jnp.int32)[:, None] + y_radix // 2 * core
+    inner = jnp.arange(lanes, dtype=jnp.int32)[None, :]
+    y_waves = wave_number((ky + y_radix * inner).reshape(-1), y_total)
+    lateral = x_waves[:, :, None] ** 2 + y_waves[None, None, :] ** 2
+    kz_square = (omega * reference_slowness) ** 2 - lateral
+    kz_root = jnp.sqrt(jnp.abs(kz_square))
+    travels = kz_square >= 0.0
+    amplitude = jnp.where(travels, 1.0, jnp.exp(-kz_root * depth_interval))
+    amplitude = amplitude / (x_total * y_total)
+    angles = jnp.where(travels, polarity * kz_root * depth_interval, 0.0)
+    return jnp.stack([amplitude * jnp.cos(angles), amplitude * jnp.sin(angles)], axis=1)
+
+
+def per_device_fields(sizes, wavefields, slowness, freq_index):
+    s, z, x, c = (lax.axis_index(axis) for axis in axes)
+    rows, y_cols = wavefields.shape[3:]
+    x_total = rows * sizes["gy"]
+    place = jnp.stack([s, z, x, c]).astype(jnp.int32)
+
+    def send(array, target):
+        return lax.ppermute(array, axes, route(sizes, target))
+
+    def to_core(array):
+        return send(array, lambda s, z, x, c: (s, z, x, 1 - c))
+
+    def to_partner(array):
+        return send(array, lambda s, z, x, c: (s, z, 1 - x, c))
+
+    def to_partner_core(array):
+        return send(array, lambda s, z, x, c: (s, z, 1 - x, 1 - c))
+
+    def to_shot(array):
+        return send(array, lambda s, z, x, c: (1 - s, z, x, c))
+
+    def along_z(array, r):
+        return send(array, lambda s, z, x, c: (s, z ^ r, x, c))
+
+    row_forward = row_matrix(lanes, -1.0)
+    row_inverse = row_matrix(lanes, 1.0)
+    column_forward = column_matrix(rows, -1.0)
+    column_inverse = column_matrix(rows, 1.0)
+
+    y_steps = y_table(c, y_cols)
+    spectra = origin_rows(wavefields[0], place, y_steps, row_forward)
+    own_field = c == x
+    arrived = []
+    for chunk in range(2):
+        kept, crossed = spectra[chunk], to_core(spectra[2 + chunk])
+        stays = jnp.where(own_field, kept, crossed)
+        moved = to_partner(jnp.where(own_field, crossed, kept))
+        blocks = []
+        for r in range(4):
+            goal = z ^ r
+            choice = jnp.where(goal % 2 == x, stays, moved)
+            block = lax.dynamic_index_in_dim(choice, goal // 2, 0, keepdims=False)
+            blocks.append(block if r == 0 else along_z(block, r))
+        arrived.append(blocks)
+
+    other_index = to_partner(freq_index)
+    indices = jnp.where(z % 2 == x, freq_index, other_index)
+    omega = omega_unit * lax.dynamic_index_in_dim(indices, z // 2, 0, keepdims=False).astype(jnp.float32)
+    polarity = (2 * x - 1).astype(jnp.float32)
+    order = 2 * c + x
+    move = move_table(omega, polarity, c, x_total, y_cols)
+    table_z = x_table(z, x_total)
+    table_order = x_table(order, x_total)
+
+    width = y_cols // 4
+
+    def screens_of(layer):
+        piece = lax.dynamic_slice_in_dim(layer, (2 * s + c) * width, width, 1)
+        pieces = jnp.stack([piece] + [along_z(piece, r) for r in range(1, 4)])
+        mine = lax.dynamic_slice_in_dim(pieces, 2 * ((z // 2) ^ c), 2, 0)
+        theirs = to_core(lax.dynamic_slice_in_dim(pieces, 2 * ((z // 2) ^ (1 - c)), 2, 0))
+        half = jnp.where(
+            c == 0, jnp.concatenate([mine, theirs], 2), jnp.concatenate([theirs, mine], 2)
+        )
+        far = to_shot(half)
+        both = jnp.where(s == 0, jnp.concatenate([half, far], 2), jnp.concatenate([far, half], 2))
+        both = jnp.where((z % 2) == x, both, both[::-1])
+        phases = (polarity * omega) * ((both - reference_slowness) * depth_interval)
+        return jnp.stack([jnp.cos(phases), jnp.sin(phases)], axis=1)
+
+    images = []
+    blocks_in, order_in, table_in = arrived, z, table_z
+    for depth_step in range(DEPTH):
+        last = depth_step == DEPTH - 1
+        swaps = jnp.stack([order_in & 1, order & 1]).astype(jnp.int32)
+        screen = screens_of(slowness[depth_step])
+        near, partner = [], []
+        for chunk in range(2):
+            out = move_columns(
+                chunk, swaps, blocks_in[chunk], table_in, table_order, move,
+                column_forward, column_inverse,
+            )
+            crossed = [to_core(out[2]), None if last else to_core(out[3])]
+            near.append([[out[0], crossed[0]], [out[1], crossed[1]]])
+            partner.append([to_partner(out[1]), to_partner_core(out[3])])
+
+        def y_blocks(pairs):
+            return [pairs[0][0], pairs[1][0], pairs[0][1], pairs[1][1]]
+
+        own = y_blocks([near[0][0], near[1][0]])
+        if not last:
+            turned = [None, None]
+            for slot in (1, 0):
+                blocks = y_blocks([near[0][slot], near[1][slot]])
+                turned[slot] = turn_rows(
+                    slot == 0, slot, blocks, screen, y_steps, row_inverse, row_forward
+                )
+            blocks_in = [
+                [turned[0][k], turned[1][k], to_core(turned[0][2 + k]), to_core(turned[1][2 + k])]
+                for k in range(2)
+            ]
+            order_in, table_in = order, table_order
+            own = [turned[0][4]]
+        terms = image_rows(place, own, y_blocks(partner), screen, y_steps, row_inverse)
+
+        def gather(r):
+            def target(s, z, x, c):
+                quarter = z ^ r
+                return s, 2 * c + x, quarter // 2, quarter % 2
+
+            return send(terms[r], target)
+
+        images.append(sum(gather(r) for r in range(4)))
+    return jnp.stack(images)
+
+
 def solution(mesh):
+    sizes = dict(mesh.shape)
+
+    def per_device(wavefields, slowness, freq_index):
+        if fits_one_field_per_chip(sizes, wavefields.shape):
+            return per_device_fields(sizes, wavefields, slowness, freq_index)
+        return per_device_pencils(wavefields, slowness, freq_index)
+
     placed = (P("fld", None, ("shot", "freq"), "gy", None), P(None, "gy", None), P("freq"))
     return jax.shard_map(
         per_device,

time: 686 us -> 369 us (0.54); the launches traced: 677 us -> 368 us
  waiting for transfers between devices: 284 us -> 160 us
  matrix products: 111 us -> 0 us
  blocking collectives: 96.6 us -> 0 us
  local copies, waits for them, and re-layouts: 84.5 us -> 19 us
  Pallas kernels: 0 us -> 62.2 us
  starting transfers between devices: 22.5 us -> 75.7 us
  between operations: 15.8 us -> 1.4 us
  other arithmetic: 63.5 us -> 49.4 us
    all_to_all x4 -> x0, waiting for transfers between devices: 260 us -> none  [the longest x3 257 us: per_device(): lax.all_to_all(blocks, 'gy', split_axis=3, concat_axis=3, tiled=True)]
    ppermute x0 -> x47, waiting for transfers between devices: none -> 160 us  [send(): return lax.ppermute(array, axes, route(sizes, target))]
    dot_general x16 -> x0, matrix products: 111 us -> none  [contract(): jnp.einsum(pattern, values, matrix, precision=lax.Precision.HIGHEST, pref...]
    all_to_all x1 -> x0, blocking collectives: 96.6 us -> none  [per_device(): lax.all_to_all(blocks, 'gy', split_axis=3, concat_axis=3, tiled=True)]
    ppermute x0 -> x47, starting transfers between devices: none -> 75.7 us  [send(): return lax.ppermute(array, axes, route(sizes, target))]
    pallas_call x0 -> x9, Pallas kernels: none -> 62.2 us  [the longest x4 38 us: move_columns(): pl.pallas_call(x_kernel, grid=(1,), in_specs=[smem] + [block] * 4 + [whol...]
    sub x12 -> x0, other arithmetic: 44 us -> none  [rotate(): real_part * cosine - imag_part * sine_part]
    another operation x14 -> x3, local copies, waits for them, and re-layouts: 33.4 us -> 0.33 us  [the longest x1 0.32 us: screens_of(): return jnp.stack([jnp.cos(phases), jnp.sin(phases)], axis=1)]
  transfers between devices with their start and end apart: 6 -> 47, of which waited for: 5 -> 16; matrix products, arithmetic and copies ran while one was open for 9% -> 16% of each run, Pallas kernels for 0% -> 17%
where the time goes in v1:
time: 369 us; the launch traced here: 368 us
  waiting for transfers between devices  160 us (43%)
  starting transfers between devices  75.7 us (21%)
  Pallas kernels  62.2 us (17%)
  other arithmetic  49.4 us (13%)
  local copies, waits for them, and re-layouts  19 us (5%)
    ppermute x47, waiting for transfers between devices, send(): return lax.ppermute(array, axes, route(sizes, target))  160 us
    ppermute x47, starting transfers between devices, send(): return lax.ppermute(array, axes, route(sizes, target))  75.7 us
    pallas_call x4, Pallas kernels, move_columns(): pl.pallas_call(x_kernel, grid=(1,), in_specs=[smem] + [block] * 4 + [whol...  38 us
    another operation x4, other arithmetic, screens_of(): return jnp.stack([jnp.cos(phases), jnp.sin(phases)], axis=1)  18.6 us
    pallas_call x2, Pallas kernels, turn_rows(): pl.pallas_call(functools.partial(turn_kernel, keeps_field), grid=(rows //...  11 us
    mul x1, other arithmetic, move_table(): amplitude * jnp.cos(angles)  8.59 us
    pallas_call x2, Pallas kernels, image_rows(): pl.pallas_call(functools.partial(image_kernel, own_ready), grid=(rows //...  7.66 us
  transfers between devices with their start and end apart: 47, of which 16 were waited for; matrix products, arithmetic and copies ran while one was open for 16% of the time, Pallas kernels for 17%

profile of v1, /device:TPU:0, one launch (start us, length us, event | category | flops | bytes accessed | tf_op | source)
XLA Modules:
  0.0 368.3 jit_solution(9377779715370398917)
XLA Ops:
  0.0 2.8 fusion.42
  3.6 5.0 %collective-permute-start.15 = (f32[256,256]{1,0:T(8,128)}, f32[256,256]{1,0:T(8,128)}, u32[]{:S(2)}, u32[]{:S(2)}) collective-permute-start(f32[256,256]{1,0:T(8,128)} %fusion.44), channel_id=1, source_target_pairs={{0,12},{1,13},{2,14},{3,15},{4,8},{5,9},{6,10},{7,11},{8,4},{9,5},... | collective-permute-start | bytes 786440 | tf_op jit(solution)/shard_map/ppermute | solution.py:598
  9.5 2.2 copy-done.1
  11.7 5.6 %origin_rows.1 = (f32[2,2,256,256]{3,2,1,0:T(8,128)S(1)}, f32[2,2,256,256]{3,2,1,0:T(8,128)S(1)}, f32[2,2,256,256]{3,2,1,0:T(8,128)}, f32[2,2,256,256]{3,2,1,0:T(8,128)S(1)}) custom-call(s32[4]{0:T(128)S(1)} %pad_add_fusion.place_ref, f32[2,2,256,1024]{3,2,1,0:T(8,128)S(1)} %bitcast.56, f32[8,2,128]{2,1,0:T(2,128)S(1)} %pad_maximum_fusion.6.table_ref.refs_5_.refs_6_.refs_9_, ...), custom_call_target="tpu_custom_call" | custom-call | flops 6000000000 | bytes 18000000 | tf_op jit(solution)/shard_map/origin_rows/pallas_call | solution.py:463
  20.9 1.7 fusion.43
  22.9 1.7 constant_dynamic-slice_fusion.2
  24.8 3.9 %collective-permute-start.40 = (f32[256,256]{1,0:T(8,128)}, f32[256,256]{1,0:T(8,128)S(1)}, u32[]{:S(2)}, u32[]{:S(2)}) collective-permute-start(f32[256,256]{1,0:T(8,128)} %fusion.43), channel_id=1, source_target_pairs={{0,12},{1,13},{2,14},{3,15},{4,8},{5,9},{6,10},{7,11},{8,4},{9,5},... | collective-permute-start | bytes 786440 | tf_op jit(solution)/shard_map/ppermute | solution.py:598
  28.7 11.9 %collective-permute-done.14 = f32[256,256]{1,0:T(8,128)} collective-permute-done((f32[256,256]{1,0:T(8,128)}, f32[256,256]{1,0:T(8,128)}, u32[]{:S(2)}, u32[]{:S(2)}) %collective-permute-start.14) | collective-permute-done | bytes 262176 | tf_op jit(solution)/shard_map/ppermute | solution.py:598
  44.0 9.6 %collective-permute-done.39 = f32[256,256]{1,0:T(8,128)S(1)} collective-permute-done((f32[256,256]{1,0:T(8,128)}, f32[256,256]{1,0:T(8,128)S(1)}, u32[]{:S(2)}, u32[]{:S(2)}) %collective-permute-start.39) | collective-permute-done | bytes 262176 | tf_op jit(solution)/shard_map/ppermute | solution.py:598
  60.4 2.3 broadcast_select_fusion.1
  64.5 8.6 %cosine_multiply_fusion = (f32[4,1,256,512]{3,2,1,0:T(8,128)S(1)}, f32[4,1,256,512]{3,2,1,0:T(8,128)S(1)}) fusion(f32[]{:T(128)S(6)} %convert_element_type.69, f32[512]{0:T(512)S(1)} %fusion.29, f32[4,256]{1,0:T(4,128)S(1)} %fusion.23, f32[]{:T(128)} %bitcast.14), kind=kLoop, calls=%fused_computation.18 | loop fusion | flops 5767168 | bytes 4200456 | tf_op jit(solution)/shard_map/mul | solution.py:588
  73.1 8.0 %collective-permute-done.1 = f32[2,2,256,256]{3,2,1,0:T(8,128)S(1)} collective-permute-done((f32[2,2,256,256]{3,2,1,0:T(8,128)S(1)}, f32[2,2,256,256]{3,2,1,0:T(8,128)S(1)}, u32[]{:S(2)}, u32[]{:S(2)}) %collective-permute-start.1) | collective-permute-done | bytes 1048608 | tf_op jit(solution)/shard_map/ppermute | solution.py:598
  82.4 3.0 collective-permute-start.3
  87.6 2.9 pad_maximum_fusion.move_ref
  90.5 2.7 maximum_select_fusion.3
  94.7 2.8 maximum_select_fusion
  97.5 5.8 %collective-permute-done.7 = f32[2,2,256,256]{3,2,1,0:T(8,128)} collective-permute-done((f32[2,2,256,256]{3,2,1,0:T(8,128)}, f32[2,2,256,256]{3,2,1,0:T(8,128)}, u32[]{:S(2)}, u32[]{:S(2)}) %collective-permute-start.7) | collective-permute-done | bytes 1048608 | tf_op jit(solution)/shard_map/ppermute | solution.py:598
  103.3 1.9 fusion.5
  106.2 2.2 collective-permute-start.9
  108.4 12.6 %collective-permute-done.3.b2 = f32[2,256,256]{2,1,0:T(8,128)S(1)} collective-permute-done((f32[2,256,256]{2,1,0:T(8,128)}, f32[2,256,256]{2,1,0:T(8,128)S(1)}, u32[]{:S(2)}, u32[]{:S(2)}) %collective-permute-start.3) | collective-permute-done | bytes 524320 | tf_op jit(solution)/shard_map/ppermute | solution.py:598
  121.0 2.4 collective-permute-start.10
  124.1 9.4 %move_columns.4 = (f32[2,256,256]{2,1,0:T(8,128)S(1)}, f32[2,256,256]{2,1,0:T(8,128)S(1)}, f32[2,256,256]{2,1,0:T(8,128)S(1)}, f32[2,256,256]{2,1,0:T(8,128)S(1)}) custom-call(s32[2]{0:T(128)S(1)} %pad_add_fusion.1.swap_ref, f32[2,256,256]{2,1,0:T(8,128)S(1)} %get-tuple-element.94.b0, f32[2,256,256]{2,1,0:T(8,128)S(1)} %collective-permute-done.2.b1, ...), custom_call_target="tpu_custom_call" | custom-call | flops 8000000000 | bytes 24000000 | tf_op jit(solution)/shard_map/move_columns/pallas_call | solution.py:534
  133.6 32.3 %collective-permute-done.9.b2 = f32[2,256,256]{2,1,0:T(8,128)S(1)} collective-permute-done((f32[2,256,256]{2,1,0:T(8,128)S(1)}, f32[2,256,256]{2,1,0:T(8,128)S(1)}, u32[]{:S(2)}, u32[]{:S(2)}) %collective-permute-start.9) | collective-permute-done | bytes 524320 | tf_op jit(solution)/shard_map/ppermute | solution.py:598
  165.9 9.4 %move_columns.5 = (f32[2,256,256]{2,1,0:T(8,128)S(1)}, f32[2,256,256]{2,1,0:T(8,128)S(1)}, f32[2,256,256]{2,1,0:T(8,128)S(1)}, f32[2,256,256]{2,1,0:T(8,128)S(1)}) custom-call(s32[2]{0:T(128)S(1)} %pad_add_fusion.1.swap_ref, f32[2,256,256]{2,1,0:T(8,128)S(1)} %get-tuple-element.88.b0, f32[2,256,256]{2,1,0:T(8,128)S(1)} %collective-permute-done.8.b1, ...), custom_call_target="tpu_custom_call" | custom-call | flops 8000000000 | bytes 24000000 | tf_op jit(solution)/shard_map/move_columns/pallas_call | solution.py:534
  175.4 7.5 %cosine_bitcast_fusion.1 = (f32[2,1,256,1024]{3,2,0,1:T(8,128)S(1)}, f32[2,1,256,1024]{3,2,0,1:T(8,128)S(1)}) fusion(f32[2,256,1024]{2,1,0:T(8,128)S(1)} %maximum_select_fusion, f32[]{:T(128)S(6)} %mul.318, pred[]{:T(512)S(6)} %eq.99), kind=kLoop, calls=%fused_computation.16 | loop fusion | flops 1572864 | bytes 6291461 | tf_op jit(solution)/shard_map/stack | solution.py:659
  184.9 5.6 %turn_rows.2 = (f32[2,256,256]{2,1,0:T(8,128)S(1)}, f32[2,256,256]{2,1,0:T(8,128)S(1)}, f32[2,256,256]{2,1,0:T(8,128)S(1)}, f32[2,256,256]{2,1,0:T(8,128)S(1)}, f32[2,256,1024]{2,1,0:T(8,128)S(1)}) custom-call(f32[2,256,256]{2,1,0:T(8,128)S(1)} %get-tuple-element.44.refs_0_, f32[2,256,256]{2,1,0:T(8,128)S(1)} %get-tuple-element.47.refs_1_, ...), custom_call_target="tpu_custom_call" | custom-call | flops 5000000000 | bytes 15000000 | tf_op jit(solution)/shard_map/turn_rows/pallas_call | solution.py:491
  192.3 5.4 %turn_rows.3 = (f32[2,256,256]{2,1,0:T(8,128)S(1)}, f32[2,256,256]{2,1,0:T(8,128)S(1)}, f32[2,256,256]{2,1,0:T(8,128)S(1)}, f32[2,256,256]{2,1,0:T(8,128)S(1)}) custom-call(f32[2,256,256]{2,1,0:T(8,128)S(1)} %get-tuple-element.51.refs_0_, f32[2,256,256]{2,1,0:T(8,128)S(1)} %get-tuple-element.52.refs_1_, f32[2,256,256]{2,1,0:T(8,128)S(1)} %collective-permute-done.26.refs_2_, ...), custom_call_target="tpu_custom_call" | custom-call | flops 5000000000 | bytes 15000000 | tf_op jit(solution)/shard_map/turn_rows/pallas_call | solution.py:491
  197.8 2.6 maximum_select_fusion.1
  200.5 8.5 %cosine_bitcast_fusion = (f32[2,1,256,1024]{3,2,1,0:T(8,128)}, f32[2,1,256,1024]{3,2,1,0:T(8,128)}) fusion(f32[2,256,1024]{2,1,0:T(8,128)S(1)} %maximum_select_fusion.1, f32[]{:T(128)S(6)} %mul.318, pred[]{:T(512)S(6)} %eq.99), kind=kLoop, calls=%fused_computation.14 | loop fusion | flops 1572864 | bytes 6291461 | tf_op jit(solution)/shard_map/stack | solution.py:659
  212.7 9.7 %move_columns.6 = (f32[2,256,256]{2,1,0:T(8,128)S(1)}, f32[2,256,256]{2,1,0:T(8,128)S(1)}, f32[2,256,256]{2,1,0:T(8,128)S(1)}, f32[2,256,256]{2,1,0:T(8,128)S(1)}) custom-call(s32[2]{0:T(128)S(1)} %pad_add_fusion.2.swap_ref, f32[2,256,256]{2,1,0:T(8,128)S(1)} %get-tuple-element.59.b0, f32[2,256,256]{2,1,0:T(8,128)S(1)} %get-tuple-element.60.b1, ...), custom_call_target="tpu_custom_call" | custom-call | flops 8000000000 | bytes 24000000 | tf_op jit(solution)/shard_map/move_columns/pallas_call | solution.py:534
  223.8 9.4 %move_columns.7 = (f32[2,256,256]{2,1,0:T(8,128)S(1)}, f32[2,256,256]{2,1,0:T(8,128)S(1)}, f32[2,256,256]{2,1,0:T(8,128)S(1)}, f32[2,256,256]{2,1,0:T(8,128)S(1)}) custom-call(s32[2]{0:T(128)S(1)} %pad_add_fusion.2.swap_ref, f32[2,256,256]{2,1,0:T(8,128)S(1)} %get-tuple-element.64.b0, f32[2,256,256]{2,1,0:T(8,128)S(1)} %copy-done.20, ...), custom_call_target="tpu_custom_call" | custom-call | flops 8000000000 | bytes 24000000 | tf_op jit(solution)/shard_map/move_columns/pallas_call | solution.py:534
  236.5 8.8 %collective-permute-done.20.refs_3_ = f32[2,256,256]{2,1,0:T(8,128)S(1)} collective-permute-done((f32[2,256,256]{2,1,0:T(8,128)S(1)}, f32[2,256,256]{2,1,0:T(8,128)S(1)}, u32[]{:S(2)}, u32[]{:S(2)}) %collective-permute-start.20) | collective-permute-done | bytes 524320 | tf_op jit(solution)/shard_map/ppermute | solution.py:598
  246.7 9.7 %collective-permute-done.21.refs_4_ = f32[2,256,256]{2,1,0:T(8,128)S(1)} collective-permute-done((f32[2,256,256]{2,1,0:T(8,128)S(1)}, f32[2,256,256]{2,1,0:T(8,128)S(1)}, u32[]{:S(2)}, u32[]{:S(2)}) %collective-permute-start.21) | collective-permute-done | bytes 524320 | tf_op jit(solution)/shard_map/ppermute | solution.py:598
  256.5 1.9 collective-permute-start.36
  258.4 2.3 pad_maximum_fusion.2.refs_8_
  260.7 3.1 image_rows.2
  263.9 3.6 collective-permute-start.25
  268.7 9.1 %collective-permute-start.24 = (f32[256,256]{1,0:T(8,128)S(1)}, f32[256,256]{1,0:T(8,128)S(1)}, u32[]{:S(2)}, u32[]{:S(2)}) collective-permute-start(f32[256,256]{1,0:T(8,128)S(1)} %get-tuple-element.57), channel_id=1, source_target_pairs={{0,2},{1,10},{2,6},{3,14},{4,3},{5,11},{6,7},{7,15},{8,0},{9,8},{1... | collective-permute-start | bytes 786440 | tf_op jit(solution)/shard_map/ppermute | solution.py:598
  277.8 2.1 collective-permute-done.35.refs_5_
  280.6 18.0 %collective-permute-done.36.refs_6_ = f32[2,256,256]{2,1,0:T(8,128)S(1)} collective-permute-done((f32[2,256,256]{2,1,0:T(8,128)S(1)}, f32[2,256,256]{2,1,0:T(8,128)S(1)}, u32[]{:S(2)}, u32[]{:S(2)}) %collective-permute-start.36) | collective-permute-done | bytes 524320 | tf_op jit(solution)/shard_map/ppermute | solution.py:598
  298.6 4.8 %collective-permute-start.23 = (f32[256,256]{1,0:T(8,128)S(1)}, f32[256,256]{1,0:T(8,128)S(1)}, u32[]{:S(2)}, u32[]{:S(2)}) collective-permute-start(f32[256,256]{1,0:T(8,128)S(1)} %get-tuple-element.56), channel_id=1, source_target_pairs={{0,1},{1,9},{2,5},{3,13},{4,0},{5,8},{6,4},{7,12},{8,3},{9,11},{10... | collective-permute-start | bytes 786440 | tf_op jit(solution)/shard_map/ppermute | solution.py:598
  303.4 11.6 %collective-permute-done.37.refs_7_ = f32[2,256,256]{2,1,0:T(8,128)S(1)} collective-permute-done((f32[2,256,256]{2,1,0:T(8,128)S(1)}, f32[2,256,256]{2,1,0:T(8,128)S(1)}, u32[]{:S(2)}, u32[]{:S(2)}) %collective-permute-start.37) | collective-permute-done | bytes 524320 | tf_op jit(solution)/shard_map/ppermute | solution.py:598
  315.0 4.5 %image_rows.3 = (f32[256,256]{1,0:T(8,128)S(1)}, f32[256,256]{1,0:T(8,128)S(1)}, f32[256,256]{1,0:T(8,128)S(1)}, f32[256,256]{1,0:T(8,128)S(1)}) custom-call(s32[4]{0:T(128)S(1)} %pad_add_fusion.place_ref, f32[2,256,256]{2,1,0:T(8,128)S(1)} %copy-done.16, f32[2,256,256]{2,1,0:T(8,128)S(1)} %copy-done.18, f32[2,256,256]{2,1,0:T(8,128)S(1)} %collective-permute-done.32.refs_2_, ...), custom_call_target="tpu_custom_call" | custom-call | flops 4000000000 | bytes 12000000 | tf_op jit(solution)/shard_map/image_rows/pallas_call | solution.py:511
  319.5 3.8 %collective-permute-start.46 = (f32[256,256]{1,0:T(8,128)S(1)}, f32[256,256]{1,0:T(8,128)S(1)}, u32[]{:S(2)}, u32[]{:S(2)}) collective-permute-start(f32[256,256]{1,0:T(8,128)S(1)} %get-tuple-element.78), channel_id=1, source_target_pairs={{0,3},{1,11},{2,7},{3,15},{4,2},{5,10},{6,6},{7,14},{8,1},{9,9},{1... | collective-permute-start | bytes 786440 | tf_op jit(solution)/shard_map/ppermute | solution.py:598
  323.4 11.0 %collective-permute-start.45 = (f32[256,256]{1,0:T(8,128)S(1)}, f32[256,256]{1,0:T(8,128)S(1)}, u32[]{:S(2)}, u32[]{:S(2)}) collective-permute-start(f32[256,256]{1,0:T(8,128)S(1)} %get-tuple-element.77), channel_id=1, source_target_pairs={{0,2},{1,10},{2,6},{3,14},{4,3},{5,11},{6,7},{7,15},{8,0},{9,8},{1... | collective-permute-start | bytes 786440 | tf_op jit(solution)/shard_map/ppermute | solution.py:598
  335.0 4.7 %collective-permute-start.44 = (f32[256,256]{1,0:T(8,128)S(1)}, f32[256,256]{1,0:T(8,128)S(1)}, u32[]{:S(2)}, u32[]{:S(2)}) collective-permute-start(f32[256,256]{1,0:T(8,128)S(1)} %get-tuple-element.76), channel_id=1, source_target_pairs={{0,1},{1,9},{2,5},{3,13},{4,0},{5,8},{6,4},{7,12},{8,3},{9,11},{10... | collective-permute-start | bytes 786440 | tf_op jit(solution)/shard_map/ppermute | solution.py:598
  339.8 3.6 collective-permute-done.45
  343.4 24.0 %collective-permute-done.44 = f32[256,256]{1,0:T(8,128)S(1)} collective-permute-done((f32[256,256]{1,0:T(8,128)S(1)}, f32[256,256]{1,0:T(8,128)S(1)}, u32[]{:S(2)}, u32[]{:S(2)}) %collective-permute-start.44) | collective-permute-done | bytes 262176 | tf_op jit(solution)/shard_map/ppermute | solution.py:598
  (167 shorter events, 40.7 us)
Async XLA Ops:
  3.6 21.3 %collective-permute-start.15 = (f32[256,256]{1,0:T(8,128)}, f32[256,256]{1,0:T(8,128)}, u32[]{:S(2)}, u32[]{:S(2)}) collective-permute-start(f32[256,256]{1,0:T(8,128)} %fusion.44), channel_id=1, source_target_pairs={{0,12},{1,13},{2,14},{3,15},{4,8},{5,9},{6,10},{7,11},{8,4},{9,5},... | collective-permute-start | bytes 786440 | tf_op jit(solution)/shard_map/ppermute | solution.py:598
  8.6 32.0 %collective-permute-start.14 = (f32[256,256]{1,0:T(8,128)}, f32[256,256]{1,0:T(8,128)}, u32[]{:S(2)}, u32[]{:S(2)}) collective-permute-start(f32[256,256]{1,0:T(8,128)} %fusion.44), channel_id=1, source_target_pairs={{0,8},{1,9},{2,10},{3,11},{4,12},{5,13},{6,14},{7,15},{8,0},{9,1},... | collective-permute-start | bytes 786440 | tf_op jit(solution)/shard_map/ppermute | solution.py:598
  8.6 32.0 %collective-permute-start.13 = (f32[256,256]{1,0:T(8,128)}, f32[256,256]{1,0:T(8,128)}, u32[]{:S(2)}, u32[]{:S(2)}) collective-permute-start(f32[256,256]{1,0:T(8,128)} %fusion.44), channel_id=1, source_target_pairs={{0,4},{1,5},{2,6},{3,7},{4,0},{5,1},{6,2},{7,3},{8,12},{9,13},{10,... | collective-permute-start | bytes 786440 | tf_op jit(solution)/shard_map/ppermute | solution.py:598
  17.3 36.4 %collective-permute-start = (f32[2,2,256,256]{3,2,1,0:T(8,128)}, f32[2,2,256,256]{3,2,1,0:T(8,128)}, u32[]{:S(2)}, u32[]{:S(2)}) collective-permute-start(f32[2,2,256,256]{3,2,1,0:T(8,128)} %get-tuple-element.43), channel_id=1, source_target_pairs={{0,1},{1,0},{2,3},{3,2},{4,5},{5,4},{6,7},{7,6},{8,9},{9,8},{10,11... | collective-permute-start | bytes 3145736 | tf_op jit(solution)/shard_map/ppermute | solution.py:598
  17.3 43.1 %collective-permute-start.6 = (f32[2,2,256,256]{3,2,1,0:T(8,128)S(1)}, f32[2,2,256,256]{3,2,1,0:T(8,128)}, u32[]{:S(2)}, u32[]{:S(2)}) collective-permute-start(f32[2,2,256,256]{3,2,1,0:T(8,128)S(1)} %get-tuple-element.46), channel_id=1, source_target_pairs={{0,1},{1,0},{2,3},{3,2},{4,5},{5,4},{6,7},{7,6},{8,9},{9,8},{10,11... | collective-permute-start | bytes 3145736 | tf_op jit(solution)/shard_map/ppermute | solution.py:598
  24.8 17.6 %collective-permute-start.40 = (f32[256,256]{1,0:T(8,128)}, f32[256,256]{1,0:T(8,128)S(1)}, u32[]{:S(2)}, u32[]{:S(2)}) collective-permute-start(f32[256,256]{1,0:T(8,128)} %fusion.43), channel_id=1, source_target_pairs={{0,12},{1,13},{2,14},{3,15},{4,8},{5,9},{6,10},{7,11},{8,4},{9,5},... | collective-permute-start | bytes 786440 | tf_op jit(solution)/shard_map/ppermute | solution.py:598
  40.6 13.0 %collective-permute-start.39 = (f32[256,256]{1,0:T(8,128)}, f32[256,256]{1,0:T(8,128)S(1)}, u32[]{:S(2)}, u32[]{:S(2)}) collective-permute-start(f32[256,256]{1,0:T(8,128)} %fusion.43), channel_id=1, source_target_pairs={{0,8},{1,9},{2,10},{3,11},{4,12},{5,13},{6,14},{7,15},{8,0},{9,1},... | collective-permute-start | bytes 786440 | tf_op jit(solution)/shard_map/ppermute | solution.py:598
  40.6 13.0 %collective-permute-start.38 = (f32[256,256]{1,0:T(8,128)}, f32[256,256]{1,0:T(8,128)S(1)}, u32[]{:S(2)}, u32[]{:S(2)}) collective-permute-start(f32[256,256]{1,0:T(8,128)} %fusion.43), channel_id=1, source_target_pairs={{0,4},{1,5},{2,6},{3,7},{4,0},{5,1},{6,2},{7,3},{8,12},{9,13},{10,... | collective-permute-start | bytes 786440 | tf_op jit(solution)/shard_map/ppermute | solution.py:598
  42.5 20.8 %collective-permute-start.5 = (s32[2]{0:T(128)S(1)}, s32[2]{0:T(128)S(1)}, u32[]{:S(2)}, u32[]{:S(2)}) collective-permute-start(s32[2]{0:T(128)S(1)} %copy-done.26), channel_id=1, source_target_pairs={{0,2},{1,3},{2,0},{3,1},{4,6},{5,7},{6,4},{7,5},{8,10},{9,11},{10,... | collective-permute-start | bytes 32 | tf_op jit(solution)/shard_map/ppermute | solution.py:598
  53.6 4.2 %collective-permute-start.16 = (f32[2,256,256]{2,1,0:T(8,128)S(1)}, f32[2,256,256]{2,1,0:T(8,128)S(1)}, u32[]{:S(2)}, u32[]{:S(2)}) collective-permute-start(f32[2,256,256]{2,1,0:T(8,128)S(1)} %get-tuple-element.100), channel_id=1, source_target_pairs={{0,1},{1,0},{2,3},{3,2},{4,5},{5,4},{6,7},{7,6},{8,9},{9,8},{10,11... | collective-permute-start | bytes 1572872 | tf_op jit(solution)/shard_map/ppermute | solution.py:598
  55.1 26.0 %collective-permute-start.1 = (f32[2,2,256,256]{3,2,1,0:T(8,128)S(1)}, f32[2,2,256,256]{3,2,1,0:T(8,128)S(1)}, u32[]{:S(2)}, u32[]{:S(2)}) collective-permute-start(f32[2,2,256,256]{3,2,1,0:T(8,128)S(1)} %get-tuple-element.96), channel_id=1, source_target_pairs={{0,2},{1,3},{2,0},{3,1},{4,6},{5,7},{6,4},{7,5},{8,10},{9,11},{10,... | collective-permute-start | bytes 3145736 | tf_op jit(solution)/shard_map/ppermute | solution.py:598
  57.5 27.9 %collective-permute-start.41 = (f32[2,256,256]{2,1,0:T(8,128)S(1)}, f32[2,256,256]{2,1,0:T(8,128)S(1)}, u32[]{:S(2)}, u32[]{:S(2)}) collective-permute-start(f32[2,256,256]{2,1,0:T(8,128)S(1)} %get-tuple-element.98), channel_id=1, source_target_pairs={{0,1},{1,0},{2,3},{3,2},{4,5},{5,4},{6,7},{7,6},{8,9},{9,8},{10,11... | collective-permute-start | bytes 1572872 | tf_op jit(solution)/shard_map/ppermute | solution.py:598
  58.9 34.3 %collective-permute-start.17 = (f32[2,256,512]{2,1,0:T(8,128)}, f32[2,256,512]{2,1,0:T(8,128)}, u32[]{:S(2)}, u32[]{:S(2)}) collective-permute-start(f32[2,256,512]{2,1,0:T(8,128)} %maximum_select_fusion.2), channel_id=1, source_target_pairs={{0,16},{1,17},{2,18},{3,19},{4,20},{5,21},{6,22},{7,23},{8,24},{9,... | collective-permute-start | bytes 3145736 | tf_op jit(solution)/shard_map/ppermute | solution.py:598
  62.8 40.5 %collective-permute-start.7 = (f32[2,2,256,256]{3,2,1,0:T(8,128)}, f32[2,2,256,256]{3,2,1,0:T(8,128)}, u32[]{:S(2)}, u32[]{:S(2)}) collective-permute-start(f32[2,2,256,256]{3,2,1,0:T(8,128)} %get-tuple-element.90), channel_id=1, source_target_pairs={{0,2},{1,3},{2,0},{3,1},{4,6},{5,7},{6,4},{7,5},{8,10},{9,11},{10,... | collective-permute-start | bytes 3145736 | tf_op jit(solution)/shard_map/ppermute | solution.py:598
  82.4 23.8 %collective-permute-start.2 = (f32[2,256,256]{2,1,0:T(8,128)}, f32[2,256,256]{2,1,0:T(8,128)S(1)}, u32[]{:S(2)}, u32[]{:S(2)}) collective-permute-start(f32[2,256,256]{2,1,0:T(8,128)} %get-tuple-element.93), channel_id=1, source_target_pairs={{0,4},{1,5},{2,6},{3,7},{4,0},{5,1},{6,2},{7,3},{8,12},{9,13},{10,... | collective-permute-start | bytes 1572872 | tf_op jit(solution)/shard_map/ppermute | solution.py:598
  82.4 38.6 %collective-permute-start.3 = (f32[2,256,256]{2,1,0:T(8,128)}, f32[2,256,256]{2,1,0:T(8,128)S(1)}, u32[]{:S(2)}, u32[]{:S(2)}) collective-permute-start(f32[2,256,256]{2,1,0:T(8,128)} %get-tuple-element.92), channel_id=1, source_target_pairs={{0,8},{1,9},{2,10},{3,11},{4,12},{5,13},{6,14},{7,15},{8,0},{9,1},... | collective-permute-start | bytes 1572872 | tf_op jit(solution)/shard_map/ppermute | solution.py:598
  86.2 37.1 %collective-permute-start.4 = (f32[2,256,256]{2,1,0:T(8,128)}, f32[2,256,256]{2,1,0:T(8,128)S(1)}, u32[]{:S(2)}, u32[]{:S(2)}) collective-permute-start(f32[2,256,256]{2,1,0:T(8,128)} %get-tuple-element.91), channel_id=1, source_target_pairs={{0,12},{1,13},{2,14},{3,15},{4,8},{5,9},{6,10},{7,11},{8,4},{9,5},... | collective-permute-start | bytes 1572872 | tf_op jit(solution)/shard_map/ppermute | solution.py:598
  93.2 104.6 %collective-permute-start.42 = (f32[2,256,512]{2,1,0:T(8,128)}, f32[2,256,512]{2,1,0:T(8,128)}, u32[]{:S(2)}, u32[]{:S(2)}) collective-permute-start(f32[2,256,512]{2,1,0:T(8,128)} %maximum_select_fusion.3), channel_id=1, source_target_pairs={{0,16},{1,17},{2,18},{3,19},{4,20},{5,21},{6,22},{7,23},{8,24},{9,... | collective-permute-start | bytes 3145736 | tf_op jit(solution)/shard_map/ppermute | solution.py:598
  105.3 28.3 %collective-permute-start.8 = (f32[2,256,256]{2,1,0:T(8,128)S(1)}, f32[2,256,256]{2,1,0:T(8,128)S(1)}, u32[]{:S(2)}, u32[]{:S(2)}) collective-permute-start(f32[2,256,256]{2,1,0:T(8,128)S(1)} %get-tuple-element.87), channel_id=1, source_target_pairs={{0,4},{1,5},{2,6},{3,7},{4,0},{5,1},{6,2},{7,3},{8,12},{9,13},{10,... | collective-permute-start | bytes 1572872 | tf_op jit(solution)/shard_map/ppermute | solution.py:598
  106.2 59.7 %collective-permute-start.9 = (f32[2,256,256]{2,1,0:T(8,128)S(1)}, f32[2,256,256]{2,1,0:T(8,128)S(1)}, u32[]{:S(2)}, u32[]{:S(2)}) collective-permute-start(f32[2,256,256]{2,1,0:T(8,128)S(1)} %get-tuple-element.86), channel_id=1, source_target_pairs={{0,8},{1,9},{2,10},{3,11},{4,12},{5,13},{6,14},{7,15},{8,0},{9,1},... | collective-permute-start | bytes 1572872 | tf_op jit(solution)/shard_map/ppermute | solution.py:598
  121.0 44.9 %collective-permute-start.10 = (f32[2,256,256]{2,1,0:T(8,128)S(1)}, f32[2,256,256]{2,1,0:T(8,128)S(1)}, u32[]{:S(2)}, u32[]{:S(2)}) collective-permute-start(f32[2,256,256]{2,1,0:T(8,128)S(1)} %get-tuple-element.85), channel_id=1, source_target_pairs={{0,12},{1,13},{2,14},{3,15},{4,8},{5,9},{6,10},{7,11},{8,4},{9,5},... | collective-permute-start | bytes 1572872 | tf_op jit(solution)/shard_map/ppermute | solution.py:598
  133.5 50.7 %collective-permute-start.11 = (f32[2,256,256]{2,1,0:T(8,128)S(1)}, f32[2,256,256]{2,1,0:T(8,128)S(1)}, u32[]{:S(2)}, u32[]{:S(2)}) collective-permute-start(f32[2,256,256]{2,1,0:T(8,128)S(1)} %get-tuple-element.48), channel_id=1, source_target_pairs={{0,1},{1,0},{2,3},{3,2},{4,5},{5,4},{6,7},{7,6},{8,9},{9,8},{10,11... | collective-permute-start | bytes 1572872 | tf_op jit(solution)/shard_map/ppermute | solution.py:598
  175.4 8.9 %collective-permute-start.12 = (f32[2,256,256]{2,1,0:T(8,128)S(1)}, f32[2,256,256]{2,1,0:T(8,128)S(1)}, u32[]{:S(2)}, u32[]{:S(2)}) collective-permute-start(f32[2,256,256]{2,1,0:T(8,128)S(1)} %get-tuple-element.49), channel_id=1, source_target_pairs={{0,1},{1,0},{2,3},{3,2},{4,5},{5,4},{6,7},{7,6},{8,9},{9,8},{10,11... | collective-permute-start | bytes 1572872 | tf_op jit(solution)/shard_map/ppermute | solution.py:598
  182.9 9.3 %collective-permute-start.26 = (f32[2,256,256]{2,1,0:T(8,128)S(1)}, f32[2,256,256]{2,1,0:T(8,128)S(1)}, u32[]{:S(2)}, u32[]{:S(2)}) collective-permute-start(f32[2,256,256]{2,1,0:T(8,128)S(1)} %get-tuple-element.53), channel_id=1, source_target_pairs={{0,1},{1,0},{2,3},{3,2},{4,5},{5,4},{6,7},{7,6},{8,9},{9,8},{10,11... | collective-permute-start | bytes 1572872 | tf_op jit(solution)/shard_map/ppermute | solution.py:598
  183.5 8.8 %collective-permute-start.27 = (f32[2,256,256]{2,1,0:T(8,128)S(1)}, f32[2,256,256]{2,1,0:T(8,128)S(1)}, u32[]{:S(2)}, u32[]{:S(2)}) collective-permute-start(f32[2,256,256]{2,1,0:T(8,128)S(1)} %get-tuple-element.54), channel_id=1, source_target_pairs={{0,1},{1,0},{2,3},{3,2},{4,5},{5,4},{6,7},{7,6},{8,9},{9,8},{10,11... | collective-permute-start | bytes 1572872 | tf_op jit(solution)/shard_map/ppermute | solution.py:598
  191.8 20.2 %collective-permute-start.28 = (f32[2,256,256]{2,1,0:T(8,128)S(1)}, f32[2,256,256]{2,1,0:T(8,128)S(1)}, u32[]{:S(2)}, u32[]{:S(2)}) collective-permute-start(f32[2,256,256]{2,1,0:T(8,128)S(1)} %get-tuple-element.61), channel_id=1, source_target_pairs={{0,1},{1,0},{2,3},{3,2},{4,5},{5,4},{6,7},{7,6},{8,9},{9,8},{10,11... | collective-permute-start | bytes 1572872 | tf_op jit(solution)/shard_map/ppermute | solution.py:598
  197.7 14.9 %collective-permute-start.29 = (f32[2,256,256]{2,1,0:T(8,128)S(1)}, f32[2,256,256]{2,1,0:T(8,128)S(1)}, u32[]{:S(2)}, u32[]{:S(2)}) collective-permute-start(f32[2,256,256]{2,1,0:T(8,128)S(1)} %get-tuple-element.62), channel_id=1, source_target_pairs={{0,1},{1,0},{2,3},{3,2},{4,5},{5,4},{6,7},{7,6},{8,9},{9,8},{10,11... | collective-permute-start | bytes 1572872 | tf_op jit(solution)/shard_map/ppermute | solution.py:598
  209.0 25.1 %collective-permute-start.18 = (f32[2,256,256]{2,1,0:T(8,128)S(1)}, f32[2,256,256]{2,1,0:T(8,128)S(1)}, u32[]{:S(2)}, u32[]{:S(2)}) collective-permute-start(f32[2,256,256]{2,1,0:T(8,128)S(1)} %get-tuple-element.51.refs_0_), channel_id=1, source_target_pairs={{0,2},{1,3},{2,0},{3,1},{4,6},{5,7},{6,4},{7,5},{8,10},{9,11},{10,... | collective-permute-start | bytes 1572872 | tf_op jit(solution)/shard_map/ppermute | solution.py:598
  210.5 24.5 %collective-permute-start.19 = (f32[2,256,256]{2,1,0:T(8,128)S(1)}, f32[2,256,256]{2,1,0:T(8,128)S(1)}, u32[]{:S(2)}, u32[]{:S(2)}) collective-permute-start(f32[2,256,256]{2,1,0:T(8,128)S(1)} %get-tuple-element.52.refs_1_), channel_id=1, source_target_pairs={{0,2},{1,3},{2,0},{3,1},{4,6},{5,7},{6,4},{7,5},{8,10},{9,11},{10,... | collective-permute-start | bytes 1572872 | tf_op jit(solution)/shard_map/ppermute | solution.py:598
  211.0 34.2 %collective-permute-start.20 = (f32[2,256,256]{2,1,0:T(8,128)S(1)}, f32[2,256,256]{2,1,0:T(8,128)S(1)}, u32[]{:S(2)}, u32[]{:S(2)}) collective-permute-start(f32[2,256,256]{2,1,0:T(8,128)S(1)} %get-tuple-element.53), channel_id=1, source_target_pairs={{0,3},{1,2},{2,1},{3,0},{4,7},{5,6},{6,5},{7,4},{8,11},{9,10},{10,... | collective-permute-start | bytes 1572872 | tf_op jit(solution)/shard_map/ppermute | solution.py:598
  212.0 11.2 %collective-permute-start.30 = (f32[2,256,256]{2,1,0:T(8,128)S(1)}, f32[2,256,256]{2,1,0:T(8,128)S(1)}, u32[]{:S(2)}, u32[]{:S(2)}) collective-permute-start(f32[2,256,256]{2,1,0:T(8,128)S(1)} %get-tuple-element.66), channel_id=1, source_target_pairs={{0,1},{1,0},{2,3},{3,2},{4,5},{5,4},{6,7},{7,6},{8,9},{9,8},{10,11... | collective-permute-start | bytes 1572872 | tf_op jit(solution)/shard_map/ppermute | solution.py:598
  212.6 11.1 %collective-permute-start.31 = (f32[2,256,256]{2,1,0:T(8,128)S(1)}, f32[2,256,256]{2,1,0:T(8,128)S(1)}, u32[]{:S(2)}, u32[]{:S(2)}) collective-permute-start(f32[2,256,256]{2,1,0:T(8,128)S(1)} %get-tuple-element.67), channel_id=1, source_target_pairs={{0,1},{1,0},{2,3},{3,2},{4,5},{5,4},{6,7},{7,6},{8,9},{9,8},{10,11... | collective-permute-start | bytes 1572872 | tf_op jit(solution)/shard_map/ppermute | solution.py:598
  223.2 33.3 %collective-permute-start.21 = (f32[2,256,256]{2,1,0:T(8,128)S(1)}, f32[2,256,256]{2,1,0:T(8,128)S(1)}, u32[]{:S(2)}, u32[]{:S(2)}) collective-permute-start(f32[2,256,256]{2,1,0:T(8,128)S(1)} %get-tuple-element.54), channel_id=1, source_target_pairs={{0,3},{1,2},{2,1},{3,0},{4,7},{5,6},{6,5},{7,4},{8,11},{9,10},{10,... | collective-permute-start | bytes 1572872 | tf_op jit(solution)/shard_map/ppermute | solution.py:598
  223.8 34.6 %collective-permute-start.32 = (f32[2,256,256]{2,1,0:T(8,128)S(1)}, f32[2,256,256]{2,1,0:T(8,128)S(1)}, u32[]{:S(2)}, u32[]{:S(2)}) collective-permute-start(f32[2,256,256]{2,1,0:T(8,128)S(1)} %get-tuple-element.69), channel_id=1, source_target_pairs={{0,1},{1,0},{2,3},{3,2},{4,5},{5,4},{6,7},{7,6},{8,9},{9,8},{10,11... | collective-permute-start | bytes 1572872 | tf_op jit(solution)/shard_map/ppermute | solution.py:598
  234.1 29.8 %collective-permute-start.33 = (f32[2,256,256]{2,1,0:T(8,128)S(1)}, f32[2,256,256]{2,1,0:T(8,128)S(1)}, u32[]{:S(2)}, u32[]{:S(2)}) collective-permute-start(f32[2,256,256]{2,1,0:T(8,128)S(1)} %get-tuple-element.70), channel_id=1, source_target_pairs={{0,1},{1,0},{2,3},{3,2},{4,5},{5,4},{6,7},{7,6},{8,9},{9,8},{10,11... | collective-permute-start | bytes 1572872 | tf_op jit(solution)/shard_map/ppermute | solution.py:598
  235.0 33.7 %collective-permute-start.34 = (f32[2,256,256]{2,1,0:T(8,128)S(1)}, f32[2,256,256]{2,1,0:T(8,128)S(1)}, u32[]{:S(2)}, u32[]{:S(2)}) collective-permute-start(f32[2,256,256]{2,1,0:T(8,128)S(1)} %get-tuple-element.71), channel_id=1, source_target_pairs={{0,2},{1,3},{2,0},{3,1},{4,6},{5,7},{6,4},{7,5},{8,10},{9,11},{10,... | collective-permute-start | bytes 1572872 | tf_op jit(solution)/shard_map/ppermute | solution.py:598
  245.3 34.6 %collective-permute-start.35 = (f32[2,256,256]{2,1,0:T(8,128)S(1)}, f32[2,256,256]{2,1,0:T(8,128)S(1)}, u32[]{:S(2)}, u32[]{:S(2)}) collective-permute-start(f32[2,256,256]{2,1,0:T(8,128)S(1)} %get-tuple-element.72), channel_id=1, source_target_pairs={{0,2},{1,3},{2,0},{3,1},{4,6},{5,7},{6,4},{7,5},{8,10},{9,11},{10,... | collective-permute-start | bytes 1572872 | tf_op jit(solution)/shard_map/ppermute | solution.py:598
  256.5 42.1 %collective-permute-start.36 = (f32[2,256,256]{2,1,0:T(8,128)S(1)}, f32[2,256,256]{2,1,0:T(8,128)S(1)}, u32[]{:S(2)}, u32[]{:S(2)}) collective-permute-start(f32[2,256,256]{2,1,0:T(8,128)S(1)} %get-tuple-element.73), channel_id=1, source_target_pairs={{0,3},{1,2},{2,1},{3,0},{4,7},{5,6},{6,5},{7,4},{8,11},{9,10},{10,... | collective-permute-start | bytes 1572872 | tf_op jit(solution)/shard_map/ppermute | solution.py:598
  258.4 56.6 %collective-permute-start.37 = (f32[2,256,256]{2,1,0:T(8,128)S(1)}, f32[2,256,256]{2,1,0:T(8,128)S(1)}, u32[]{:S(2)}, u32[]{:S(2)}) collective-permute-start(f32[2,256,256]{2,1,0:T(8,128)S(1)} %get-tuple-element.74), channel_id=1, source_target_pairs={{0,3},{1,2},{2,1},{3,0},{4,7},{5,6},{6,5},{7,4},{8,11},{9,10},{10,... | collective-permute-start | bytes 1572872 | tf_op jit(solution)/shard_map/ppermute | solution.py:598
  260.7 54.2 %copy-start.16 = (f32[2,256,256]{2,1,0:T(8,128)S(1)}, f32[2,256,256]{2,1,0:T(8,128)}, u32[]{:S(2)}) copy-start(f32[2,256,256]{2,1,0:T(8,128)} %copy-done.15) | copy-start | bytes 1572868
  263.9 59.5 %collective-permute-start.25 = (f32[256,256]{1,0:T(8,128)S(1)}, f32[256,256]{1,0:T(8,128)S(1)}, u32[]{:S(2)}, u32[]{:S(2)}) collective-permute-start(f32[256,256]{1,0:T(8,128)S(1)} %get-tuple-element.58), channel_id=1, source_target_pairs={{0,3},{1,11},{2,7},{3,15},{4,2},{5,10},{6,6},{7,14},{8,1},{9,9},{1... | collective-permute-start | bytes 786440 | tf_op jit(solution)/shard_map/ppermute | solution.py:598
  268.7 65.7 %collective-permute-start.24 = (f32[256,256]{1,0:T(8,128)S(1)}, f32[256,256]{1,0:T(8,128)S(1)}, u32[]{:S(2)}, u32[]{:S(2)}) collective-permute-start(f32[256,256]{1,0:T(8,128)S(1)} %get-tuple-element.57), channel_id=1, source_target_pairs={{0,2},{1,10},{2,6},{3,14},{4,3},{5,11},{6,7},{7,15},{8,0},{9,8},{1... | collective-permute-start | bytes 786440 | tf_op jit(solution)/shard_map/ppermute | solution.py:598
  279.9 55.1 %collective-permute-start.22 = (f32[256,256]{1,0:T(8,128)S(1)}, f32[256,256]{1,0:T(8,128)S(1)}, u32[]{:S(2)}, u32[]{:S(2)}) collective-permute-start(f32[256,256]{1,0:T(8,128)S(1)} %get-tuple-element.55), channel_id=1, source_target_pairs={{0,0},{1,8},{2,4},{3,12},{4,1},{5,9},{6,5},{7,13},{8,2},{9,10},{10... | collective-permute-start | bytes 786440 | tf_op jit(solution)/shard_map/ppermute | solution.py:598
  298.6 41.1 %collective-permute-start.23 = (f32[256,256]{1,0:T(8,128)S(1)}, f32[256,256]{1,0:T(8,128)S(1)}, u32[]{:S(2)}, u32[]{:S(2)}) collective-permute-start(f32[256,256]{1,0:T(8,128)S(1)} %get-tuple-element.56), channel_id=1, source_target_pairs={{0,1},{1,9},{2,5},{3,13},{4,0},{5,8},{6,4},{7,12},{8,3},{9,11},{10... | collective-permute-start | bytes 786440 | tf_op jit(solution)/shard_map/ppermute | solution.py:598
  319.5 20.2 %collective-permute-start.46 = (f32[256,256]{1,0:T(8,128)S(1)}, f32[256,256]{1,0:T(8,128)S(1)}, u32[]{:S(2)}, u32[]{:S(2)}) collective-permute-start(f32[256,256]{1,0:T(8,128)S(1)} %get-tuple-element.78), channel_id=1, source_target_pairs={{0,3},{1,11},{2,7},{3,15},{4,2},{5,10},{6,6},{7,14},{8,1},{9,9},{1... | collective-permute-start | bytes 786440 | tf_op jit(solution)/shard_map/ppermute | solution.py:598
  323.4 20.1 %collective-permute-start.45 = (f32[256,256]{1,0:T(8,128)S(1)}, f32[256,256]{1,0:T(8,128)S(1)}, u32[]{:S(2)}, u32[]{:S(2)}) collective-permute-start(f32[256,256]{1,0:T(8,128)S(1)} %get-tuple-element.77), channel_id=1, source_target_pairs={{0,2},{1,10},{2,6},{3,14},{4,3},{5,11},{6,7},{7,15},{8,0},{9,8},{1... | collective-permute-start | bytes 786440 | tf_op jit(solution)/shard_map/ppermute | solution.py:598
  334.3 9.1 %collective-permute-start.43 = (f32[256,256]{1,0:T(8,128)S(1)}, f32[256,256]{1,0:T(8,128)S(1)}, u32[]{:S(2)}, u32[]{:S(2)}) collective-permute-start(f32[256,256]{1,0:T(8,128)S(1)} %get-tuple-element.75), channel_id=1, source_target_pairs={{0,0},{1,8},{2,4},{3,12},{4,1},{5,9},{6,5},{7,13},{8,2},{9,10},{10... | collective-permute-start | bytes 786440 | tf_op jit(solution)/shard_map/ppermute | solution.py:598
  335.0 32.4 %collective-permute-start.44 = (f32[256,256]{1,0:T(8,128)S(1)}, f32[256,256]{1,0:T(8,128)S(1)}, u32[]{:S(2)}, u32[]{:S(2)}) collective-permute-start(f32[256,256]{1,0:T(8,128)S(1)} %get-tuple-element.76), channel_id=1, source_target_pairs={{0,1},{1,9},{2,5},{3,13},{4,0},{5,8},{6,4},{7,12},{8,3},{9,11},{10... | collective-permute-start | bytes 786440 | tf_op jit(solution)/shard_map/ppermute | solution.py:598
  (26 other events, 280.6 us)

commit v2 on v1

--- a/solution.py
+++ b/solution.py
@@ -340,16 +340,24 @@
     ]
 
 
-def read_screen(screen_ref, a):
-    return screen_ref[0, 0, :, lane_block(a)], screen_ref[0, 1, :, lane_block(a)]
-
-
-def turn_kernel(keeps_field, *refs):
+def read_screen(scale_ref, slowness_ref, a):
+    layer = slowness_ref[a // 2, 0, 0, :, lane_block(a % 2)]
+    phase = scale_ref[0] * ((layer - reference_slowness) * depth_interval)
+    square = phase * phase
+    cosine, sine = 1.0 / 40320.0, 1.0 / 362880.0
+    for term in (-1.0 / 720.0, 1.0 / 24.0, -0.5, 1.0):
+        cosine = cosine * square + term
+    for term in (-1.0 / 5040.0, 1.0 / 120.0, -1.0 / 6.0, 1.0):
+        sine = sine * square + term
+    return cosine, sine * phase
+
+
+def turn_kernel(keeps_field, scale_ref, *refs):
     blocks, rest = refs[:4], refs[4:]
     screen_ref, table_ref, inv_upper, inv_lower, upper_ref, lower_ref = rest[:6]
     outs = rest[6:]
     terms = inverse_y(read_y_blocks(blocks), table_ref, inv_upper, inv_lower)
-    terms = [multiply(terms[a], read_screen(screen_ref, a)) for a in range(y_radix)]
+    terms = [multiply(terms[a], read_screen(scale_ref, screen_ref, a)) for a in range(y_radix)]
     if keeps_field:
         for a in range(y_radix):
             for part in range(2):
@@ -360,7 +368,7 @@
             outs[k // 2][part, :, lane_block(k % 2)] = spectrum[k][part]
 
 
-def image_kernel(own_ready, place_ref, *refs):
+def image_kernel(own_ready, place_ref, scale_ref, *refs):
     own_count = 1 if own_ready else 4
     own, refs = refs[:own_count], refs[own_count:]
     blocks, refs = refs[:4], refs[4:]
@@ -370,7 +378,7 @@
     if not own_ready:
         mine = inverse_y(read_y_blocks(own), table_ref, inv_upper, inv_lower)
     for a in range(y_radix):
-        screen = read_screen(screen_ref, a)
+        screen = read_screen(scale_ref, screen_ref, a)
         if own_ready:
             near = (own[0][0, :, lane_block(a)], own[0][1, :, lane_block(a)])
         else:
@@ -378,19 +386,22 @@
         far = multiply(other[a], conjugate(screen))
         quarters[a // 2, :, lane_block(a % 2)] = near[0] * far[0] + near[1] * far[1]
     for r in range(4):
-        outs[r][...] = quarters[lax.bitwise_xor(place_ref[1], r)]
-
-
-def x_kernel(
-    swap_ref, b0, b1, b2, b3, table_in, table_out, move_ref,
-    upper_ref, lower_ref, inv_upper, inv_lower, o0, o1, o2, o3, high, low, held,
-):
-    blocks, outs = (b0, b1, b2, b3), (o0, o1, o2, o3)
-    rows = b0.shape[1]
+        outs[r][...] = quarters[lax.bitwise_xor(2 * place_ref[2] + place_ref[1] // 2, r)]
+
+
+def x_kernel(pieces, swap_ref, *refs):
+    blocks, refs = refs[: x_radix * pieces], refs[x_radix * pieces :]
+    table_in, table_out, move_ref, upper_ref, lower_ref, inv_upper, inv_lower = refs[:7]
+    outs, (high, low, held) = refs[7:11], refs[11:]
+    rows = blocks[0].shape[1]
 
     def wide(table, k, part, span):
         values = table[k, part, span, :]
-        return jnp.concatenate([values] * (b0.shape[2] // lanes), axis=1)
+        return jnp.concatenate([values] * (held.shape[2] // lanes), axis=1)
+
+    def read(q, part, span):
+        values = [block[part, span, :] for block in blocks[q * pieces : (q + 1) * pieces]]
+        return values[0] if pieces == 1 else jnp.concatenate(values, axis=1)
 
     def actual(k, swaps):
         return k if k % 2 == 0 else lax.bitwise_xor(k, 2 * swaps)
@@ -398,7 +409,7 @@
     def gather_rows(step, carry):
         span = pl.ds(pl.multiple_of(step * strip, strip), strip)
         lower_span = pl.ds(pl.multiple_of(step * strip + rows, strip), strip)
-        terms = dft4([(block[0, span, :], block[1, span, :]) for block in blocks], -1.0)
+        terms = dft4([(read(q, 0, span), read(q, 1, span)) for q in range(x_radix)], -1.0)
         for k in range(x_radix):
             factor = (wide(table_in, k, 0, span), wide(table_in, k, 1, span))
             real, imag = multiply(terms[k], factor)
@@ -444,9 +455,9 @@
 vmem_limit = 40 * 1024 * 1024
 
 
-def parameters(steps):
+def parameters(steps, limit=vmem_limit):
     return pltpu.CompilerParams(
-        vmem_limit_bytes=vmem_limit, dimension_semantics=("arbitrary",) * steps
+        vmem_limit_bytes=limit, dimension_semantics=("arbitrary",) * steps
     )
 
 
@@ -460,27 +471,39 @@
     parts, freqs, rows, y_cols = field.shape
     width = y_cols // 4
     out = jax.ShapeDtypeStruct((freqs, parts, rows, width), jnp.float32)
+
+    def fixed(array):
+        return pl.BlockSpec(array.shape, lambda j, i, place: (0,) * array.ndim)
+
     return pl.pallas_call(
         origin_kernel,
-        grid=(freqs, rows // row_block),
-        in_specs=[
-            smem,
-            pl.BlockSpec((parts, 1, row_block, y_cols), lambda j, i: (0, j, i, 0)),
-            whole(table),
-            whole(matrices[0]),
-            whole(matrices[1]),
-        ],
-        out_specs=[pl.BlockSpec((1, parts, row_block, width), lambda j, i: (j, 0, i, 0))] * 4,
+        grid_spec=pltpu.PrefetchScalarGridSpec(
+            num_scalar_prefetch=1,
+            grid=(freqs, rows // row_block),
+            in_specs=[
+                pl.BlockSpec((parts, 1, row_block, y_cols), lambda j, i, place: (0, j, i, 0)),
+                fixed(table),
+                fixed(matrices[0]),
+                fixed(matrices[1]),
+            ],
+            out_specs=[
+                pl.BlockSpec(
+                    (1, parts, row_block, width),
+                    lambda j, i, place: (lax.bitwise_xor(j, place[1] // 2), 0, i, 0),
+                )
+            ]
+            * 4,
+        ),
         out_shape=[out] * 4,
-        compiler_params=parameters(2),
+        compiler_params=parameters(2, 60 * 1024 * 1024),
         cost_estimate=estimate(6),
         name="origin_rows",
     )(place, field, table, *matrices)
 
 
-def turn_rows(keeps_field, slot, blocks, screen, table, inverse, forward):
+def turn_rows(keeps_field, depth_step, slot, scale, blocks, screen, table, inverse, forward):
     parts, rows, width = blocks[0].shape
-    y_cols = screen.shape[-1]
+    y_cols = screen.shape[0] * screen.shape[-1]
     block = pl.BlockSpec((parts, row_block, width), lambda i: (0, i, 0))
     full = pl.BlockSpec((parts, row_block, y_cols), lambda i: (0, i, 0))
     out = [jax.ShapeDtypeStruct((parts, rows, width), jnp.float32)] * 4
@@ -491,30 +514,31 @@
     return pl.pallas_call(
         functools.partial(turn_kernel, keeps_field),
         grid=(rows // row_block,),
-        in_specs=[block] * 4
-        + [pl.BlockSpec((1, 2, row_block, y_cols), lambda i: (slot, 0, i, 0))]
+        in_specs=[smem]
+        + [block] * 4
+        + [pl.BlockSpec((4, 1, 1, row_block, width), lambda i: (0, depth_step, slot, i, 0))]
         + [whole(array) for array in (table, *inverse, *forward)],
         out_specs=out_specs,
         out_shape=out,
         compiler_params=parameters(1),
         cost_estimate=estimate(5),
         name="turn_rows",
-    )(*blocks, screen, table, *inverse, *forward)
-
-
-def image_rows(place, own, blocks, screen, table, inverse):
+    )(scale, *blocks, screen, table, *inverse, *forward)
+
+
+def image_rows(depth_step, place, scale, own, blocks, screen, table, inverse):
     parts, rows, width = blocks[0].shape
-    y_cols = screen.shape[-1]
+    y_cols = screen.shape[0] * screen.shape[-1]
     own_ready = len(own) == 1
     block = pl.BlockSpec((parts, row_block, width), lambda i: (0, i, 0))
     full = pl.BlockSpec((parts, row_block, y_cols), lambda i: (0, i, 0))
     return pl.pallas_call(
         functools.partial(image_kernel, own_ready),
         grid=(rows // row_block,),
-        in_specs=[smem]
+        in_specs=[smem, smem]
         + ([full] if own_ready else [block] * 4)
         + [block] * 4
-        + [pl.BlockSpec((1, 2, row_block, y_cols), lambda i: (0, 0, i, 0))]
+        + [pl.BlockSpec((4, 1, 1, row_block, width), lambda i: (0, depth_step, 0, i, 0))]
         + [whole(array) for array in (table, *inverse)],
         out_specs=[pl.BlockSpec((row_block, width), lambda i: (i, 0))] * 4,
         out_shape=[jax.ShapeDtypeStruct((rows, width), jnp.float32)] * 4,
@@ -522,19 +546,20 @@
         compiler_params=parameters(1),
         cost_estimate=estimate(4),
         name="image_rows",
-    )(place, *own, *blocks, screen, table, *inverse)
+    )(place, scale, *own, *blocks, screen, table, *inverse)
 
 
 def move_columns(chunk, swaps, blocks, table_in, table_out, move, forward, inverse):
-    parts, rows, width = blocks[0].shape
-    move_block = pl.BlockSpec(
-        (x_radix, parts, rows, width), lambda i: (0, 0, 0, chunk)
-    )
-    block = whole(blocks[0])
+    pieces = len(blocks[0])
+    parts, rows, width = blocks[0][0].shape
+    width = pieces * width
+    move_block = pl.BlockSpec((x_radix, parts, rows, width), lambda i: (0, 0, 0, chunk))
+    blocks = [piece for block in blocks for piece in block]
+    block = pl.BlockSpec((parts, rows, width), lambda i: (0, 0, 0))
     return pl.pallas_call(
-        x_kernel,
+        functools.partial(x_kernel, pieces),
         grid=(1,),
-        in_specs=[smem] + [block] * 4 + [whole(table_in), whole(table_out), move_block]
+        in_specs=[smem] + [whole(piece) for piece in blocks] + [whole(table_in), whole(table_out), move_block]
         + [whole(array) for array in (*forward, *inverse)],
         out_specs=[block] * 4,
         out_shape=[jax.ShapeDtypeStruct((parts, rows, width), jnp.float32)] * 4,
@@ -588,6 +613,11 @@
     return jnp.stack([amplitude * jnp.cos(angles), amplitude * jnp.sin(angles)], axis=1)
 
 
+def zero_after(*others):
+    corners = sum(other[(0,) * other.ndim] for other in others)
+    return (corners * 0.0).astype(jnp.int32)
+
+
 def per_device_fields(sizes, wavefields, slowness, freq_index):
     s, z, x, c = (lax.axis_index(axis) for axis in axes)
     rows, y_cols = wavefields.shape[3:]
@@ -601,10 +631,13 @@
         return send(array, lambda s, z, x, c: (s, z, x, 1 - c))
 
     def to_partner(array):
+        return send(array, lambda s, z, x, c: (s, z ^ 1, x, c))
+
+    def to_partner_core(array):
+        return send(array, lambda s, z, x, c: (s, z ^ 1, x, 1 - c))
+
+    def to_freq(array):
         return send(array, lambda s, z, x, c: (s, z, 1 - x, c))
-
-    def to_partner_core(array):
-        return send(array, lambda s, z, x, c: (s, z, 1 - x, 1 - c))
 
     def to_shot(array):
         return send(array, lambda s, z, x, c: (1 - s, z, x, c))
@@ -617,53 +650,55 @@
     column_forward = column_matrix(rows, -1.0)
     column_inverse = column_matrix(rows, 1.0)
 
+    width = y_cols // 8
+    piece = lax.dynamic_slice_in_dim(slowness, (4 * s + 2 * x + c) * width, width, 2)
+    pieces = [piece] + [along_z(piece, r) for r in (2, 3, 1)]
+
+    def all_columns(late):
+        stacked = jnp.stack([pieces[k] for k in (0, 3, 1, 2)], axis=1)
+        mine = lax.dynamic_slice_in_dim(stacked, 2 * ((z // 2) ^ c) + late, 2, 1)
+        theirs = to_core(
+            lax.dynamic_slice_in_dim(stacked, 2 * ((z // 2) ^ (1 - c)) + late, 2, 1)
+        )
+        both = jnp.where(
+            c == 0, jnp.concatenate([mine, theirs], 3), jnp.concatenate([theirs, mine], 3)
+        )
+        other = to_freq(both)
+        pair = jnp.where(x == 0, jnp.stack([both, other]), jnp.stack([other, both]))
+        far = to_shot(pair)
+        return jnp.where(s == 0, jnp.concatenate([pair, far]), jnp.concatenate([far, pair]))
+
     y_steps = y_table(c, y_cols)
     spectra = origin_rows(wavefields[0], place, y_steps, row_forward)
-    own_field = c == x
+    kept_is_odd = (z ^ c) % 2 == 1
     arrived = []
     for chunk in range(2):
         kept, crossed = spectra[chunk], to_core(spectra[2 + chunk])
-        stays = jnp.where(own_field, kept, crossed)
-        moved = to_partner(jnp.where(own_field, crossed, kept))
-        blocks = []
-        for r in range(4):
-            goal = z ^ r
-            choice = jnp.where(goal % 2 == x, stays, moved)
-            block = lax.dynamic_index_in_dim(choice, goal // 2, 0, keepdims=False)
-            blocks.append(block if r == 0 else along_z(block, r))
-        arrived.append(blocks)
-
-    other_index = to_partner(freq_index)
-    indices = jnp.where(z % 2 == x, freq_index, other_index)
-    omega = omega_unit * lax.dynamic_index_in_dim(indices, z // 2, 0, keepdims=False).astype(jnp.float32)
-    polarity = (2 * x - 1).astype(jnp.float32)
-    order = 2 * c + x
+        even = jnp.where(kept_is_odd, crossed, kept)
+        odd = jnp.where(kept_is_odd, kept, crossed)
+        far = along_z(even[1], 2)
+        farthest = along_z(odd[1], 3)
+        arrived.append([[even[0]], [along_z(odd[0], 1)], [far], [farthest]])
+
+    late = zero_after(arrived[0][1][0])
+    layers = all_columns(late)
+
+    z_late = z + late
+    side = z_late % 2
+    index = lax.dynamic_index_in_dim(freq_index, z_late // 2, 0, keepdims=False)
+    omega = omega_unit * index.astype(jnp.float32)
+    polarity = (2 * side - 1).astype(jnp.float32)
+    order = 2 * c + side
     move = move_table(omega, polarity, c, x_total, y_cols)
-    table_z = x_table(z, x_total)
+    table_z = x_table(z_late, x_total)
     table_order = x_table(order, x_total)
-
-    width = y_cols // 4
-
-    def screens_of(layer):
-        piece = lax.dynamic_slice_in_dim(layer, (2 * s + c) * width, width, 1)
-        pieces = jnp.stack([piece] + [along_z(piece, r) for r in range(1, 4)])
-        mine = lax.dynamic_slice_in_dim(pieces, 2 * ((z // 2) ^ c), 2, 0)
-        theirs = to_core(lax.dynamic_slice_in_dim(pieces, 2 * ((z // 2) ^ (1 - c)), 2, 0))
-        half = jnp.where(
-            c == 0, jnp.concatenate([mine, theirs], 2), jnp.concatenate([theirs, mine], 2)
-        )
-        far = to_shot(half)
-        both = jnp.where(s == 0, jnp.concatenate([half, far], 2), jnp.concatenate([far, half], 2))
-        both = jnp.where((z % 2) == x, both, both[::-1])
-        phases = (polarity * omega) * ((both - reference_slowness) * depth_interval)
-        return jnp.stack([jnp.cos(phases), jnp.sin(phases)], axis=1)
+    scale = (polarity * omega).reshape(1)
 
     images = []
-    blocks_in, order_in, table_in = arrived, z, table_z
+    blocks_in, order_in, table_in, hold = arrived, z, table_z, 0
     for depth_step in range(DEPTH):
         last = depth_step == DEPTH - 1
-        swaps = jnp.stack([order_in & 1, order & 1]).astype(jnp.int32)
-        screen = screens_of(slowness[depth_step])
+        swaps = jnp.stack([order_in & 1, order & 1]).astype(jnp.int32) + hold
         near, partner = [], []
         for chunk in range(2):
             out = move_columns(
@@ -678,25 +713,36 @@
             return [pairs[0][0], pairs[1][0], pairs[0][1], pairs[1][1]]
 
         own = y_blocks([near[0][0], near[1][0]])
+        far_blocks = y_blocks(partner)
         if not last:
             turned = [None, None]
+            waits = [zero_after(*partner[0]).astype(jnp.float32), 0.0]
             for slot in (1, 0):
                 blocks = y_blocks([near[0][slot], near[1][slot]])
                 turned[slot] = turn_rows(
-                    slot == 0, slot, blocks, screen, y_steps, row_inverse, row_forward
+                    slot == 0, depth_step, slot, scale + waits[slot], blocks, layers, y_steps,
+                    row_inverse, row_forward,
                 )
             blocks_in = [
-                [turned[0][k], turned[1][k], to_core(turned[0][2 + k]), to_core(turned[1][2 + k])]
+                [
+                    [turned[0][k]],
+                    [turned[1][k]],
+                    [to_core(turned[0][2 + k])],
+                    [to_core(turned[1][2 + k])],
+                ]
                 for k in range(2)
             ]
+            hold = zero_after(*partner[1])
             order_in, table_in = order, table_order
             own = [turned[0][4]]
-        terms = image_rows(place, own, y_blocks(partner), screen, y_steps, row_inverse)
+        terms = image_rows(
+            depth_step, place, scale, own, far_blocks, layers, y_steps, row_inverse
+        )
 
         def gather(r):
             def target(s, z, x, c):
-                quarter = z ^ r
-                return s, 2 * c + x, quarter // 2, quarter % 2
+                quarter = (2 * x + z // 2) ^ r
+                return s, 2 * c + z % 2, quarter // 2, quarter % 2
 
             return send(terms[r], target)
 

time: 369 us -> 287 us (0.78)
  waiting for transfers between devices: 160 us -> 113 us
  starting transfers between devices: 75.7 us -> 42.4 us
  other arithmetic: 49.4 us -> 28.2 us
  Pallas kernels: 62.2 us -> 71 us
  local copies, waits for them, and re-layouts: 19 us -> 27.1 us
    ppermute x47 -> x40, waiting for transfers between devices: 160 us -> 113 us  [send(): return lax.ppermute(array, axes, route(sizes, target))]
    ppermute x47 -> x40, starting transfers between devices: 75.7 us -> 42.4 us  [send(): return lax.ppermute(array, axes, route(sizes, target))]
    another operation x8 -> x2, other arithmetic: 20.2 us -> 2.23 us  [the longest x1 2.16 us: all_columns(): stacked = jnp.stack([pieces[k] for k in (0, 3, 1, 2)], axis=1)]
    unnamed x54 -> x92, local copies, waits for them, and re-layouts: 6.62 us -> 15.1 us
    pallas_call x5, Pallas kernels: 43.6 us -> 48.9 us  [the longest x4 40.1 us: move_columns(): pl.pallas_call(functools.partial(x_kernel, pieces), grid=(1,), in_specs=[...]
    dynamic_slice x7 -> x3, local copies, waits for them, and re-layouts: 7.38 us -> 3.62 us  [the longest x1 2.26 us: all_columns(): mine = lax.dynamic_slice_in_dim(stacked, 2 * (z // 2 ^ c) + late, 2, 1)]
    select_n x7 -> x6, other arithmetic: 12.9 us -> 13.8 us  [the longest x1 4 us: all_columns(): jnp.where(s == 0, jnp.concatenate([pair, far]), jnp.concatenate([far, pai...]
  transfers between devices with their start and end apart: 47 -> 40, of which waited for: 16 -> 12; matrix products, arithmetic and copies ran while one was open for 16% -> 13% of each run, Pallas kernels for 17% -> 22%
where the time goes in v2:
time: 287 us; the launch traced here: 286 us
  waiting for transfers between devices  113 us (39%)
  Pallas kernels  71 us (25%)
  starting transfers between devices  42.4 us (15%)
  other arithmetic  28.2 us (10%)
  local copies, waits for them, and re-layouts  27.1 us (9%)
  between operations  4.77 us (2%)
    ppermute x40, waiting for transfers between devices, send(): return lax.ppermute(array, axes, route(sizes, target))  113 us
    ppermute x40, starting transfers between devices, send(): return lax.ppermute(array, axes, route(sizes, target))  42.4 us
    pallas_call x4, Pallas kernels, move_columns(): pl.pallas_call(functools.partial(x_kernel, pieces), grid=(1,), in_specs=[...  40.1 us
    unnamed x92, local copies, waits for them, and re-layouts  15.1 us
    pallas_call x2, Pallas kernels, turn_rows(): pl.pallas_call(functools.partial(turn_kernel, keeps_field), grid=(rows //...  13.2 us
    pallas_call x2, Pallas kernels, image_rows(): pl.pallas_call(functools.partial(image_kernel, own_ready), grid=(rows //...  8.92 us
    pallas_call x1, Pallas kernels, origin_rows(): pl.pallas_call(origin_kernel, grid_spec=pltpu.PrefetchScalarGridSpec(num_...  8.77 us
    mul x1, other arithmetic, move_table(): amplitude * jnp.cos(angles)  8.59 us
  transfers between devices with their start and end apart: 40, of which 12 were waited for; matrix products, arithmetic and copies ran while one was open for 13% of the time, Pallas kernels for 22%

profile of v2, /device:TPU:0, one launch (start us, length us, event | category | flops | bytes accessed | tf_op | source)
XLA Modules:
  0.0 286.2 jit_solution(14785274482505374910)
XLA Ops:
  1.5 8.8 %origin_rows.1 = (f32[2,2,256,256]{3,2,1,0:T(8,128)}, f32[2,2,256,256]{3,2,1,0:T(8,128)}, f32[2,2,256,256]{3,2,1,0:T(8,128)}, f32[2,2,256,256]{3,2,1,0:T(8,128)}) custom-call(s32[4]{0:T(128)} %pad_add_fusion.place_ref, f32[2,2,256,1024]{3,2,1,0:T(8,128)} %bitcast.54, f32[8,2,128]{2,1,0:T(2,128)} %pad_maximum_fusion.3.table_ref.refs_5_.refs_6_.refs_9_, ...), custom_call_target="tpu_custom_call" | custom-call | flops 6000000000 | bytes 18000000 | tf_op jit(solution)/shard_map/origin_rows/pallas_call | solution.py:478
  11.5 2.6 collective-permute-start.12
  14.1 2.6 collective-permute-start.13
  16.9 9.7 %collective-permute-done.12 = f32[2,256,128]{2,1,0:T(8,128)} collective-permute-done((f32[2,256,128]{2,1,0:T(8,128)}, f32[2,256,128]{2,1,0:T(8,128)}, u32[]{:S(2)}, u32[]{:S(2)}) %collective-permute-start.12) | collective-permute-done | bytes 262176 | tf_op jit(solution)/shard_map/ppermute | solution.py:628
  26.5 9.2 %collective-permute-done.13 = f32[2,256,128]{2,1,0:T(8,128)} collective-permute-done((f32[2,256,128]{2,1,0:T(8,128)}, f32[2,256,128]{2,1,0:T(8,128)}, u32[]{:S(2)}, u32[]{:S(2)}) %collective-permute-start.13) | collective-permute-done | bytes 262176 | tf_op jit(solution)/shard_map/ppermute | solution.py:628
  35.8 2.2 pad_maximum_fusion.1
  37.9 1.4 broadcast_select_fusion.2
  40.2 5.4 %collective-permute-start.1 = (f32[2,256,256]{2,1,0:T(8,128)S(1)}, f32[2,256,256]{2,1,0:T(8,128)S(1)}, u32[]{:S(2)}, u32[]{:S(2)}) collective-permute-start(f32[2,256,256]{2,1,0:T(8,128)S(1)} %get-tuple-element.86), channel_id=1, source_target_pairs={{0,4},{1,5},{2,6},{3,7},{4,0},{5,1},{6,2},{7,3},{8,12},{9,13},{10,... | collective-permute-start | bytes 1572872 | tf_op jit(solution)/shard_map/ppermute | solution.py:628
  47.4 1.5 collective-permute-start.3
  48.9 1.4 broadcast_select_fusion
  50.3 1.1 slice_bitcast_fusion
  51.4 1.0 collective-permute-start.7
  53.3 1.9 collective-permute-start.8
  55.2 12.9 %collective-permute-done.1.refs_1_ = f32[2,256,256]{2,1,0:T(8,128)S(1)} collective-permute-done((f32[2,256,256]{2,1,0:T(8,128)S(1)}, f32[2,256,256]{2,1,0:T(8,128)S(1)}, u32[]{:S(2)}, u32[]{:S(2)}) %collective-permute-start.1) | collective-permute-done | bytes 524320 | tf_op jit(solution)/shard_map/ppermute | solution.py:628
  69.5 2.3 constant_dynamic-slice_fusion.1
  72.6 1.4 collective-permute-done.15
  74.0 2.6 maximum_select_fusion.3
  76.6 1.5 collective-permute-start.16
  80.2 8.6 %cosine_multiply_fusion = (f32[4,1,256,512]{3,2,1,0:T(8,128)S(1)}, f32[4,1,256,512]{3,2,1,0:T(8,128)S(1)}) fusion(f32[]{:T(128)S(6)} %convert_element_type.86, f32[512]{0:T(512)S(1)} %fusion.17, f32[4,256]{1,0:T(4,128)S(1)} %fusion.11, f32[]{:T(128)} %bitcast.17), kind=kLoop, calls=%fused_computation.6 | loop fusion | flops 5767168 | bytes 4200456 | tf_op jit(solution)/shard_map/mul | solution.py:613
  88.8 1.3 maximum_select_fusion.2
  90.2 12.0 %collective-permute-done.16 = f32[2,2,256,256]{3,2,1,0:T(8,128)} collective-permute-done((f32[2,2,256,256]{3,2,1,0:T(8,128)}, f32[2,2,256,256]{3,2,1,0:T(8,128)}, u32[]{:S(2)}, u32[]{:S(2)}) %collective-permute-start.16) | collective-permute-done | bytes 1048608 | tf_op jit(solution)/shard_map/ppermute | solution.py:628
  102.1 3.1 %maximum_select_fusion.1 = f32[2,2,2,256,256]{4,3,2,1,0:T(8,128)} fusion(f32[1,2,2,256,256]{4,3,2,1,0:T(8,128)} %bitcast.32, f32[1,2,2,256,256]{4,3,2,1,0:T(8,128)S(1)} %maximum_select_fusion.2, pred[]{:T(512)S(6)} %eq.78), kind=kLoop, calls=%fused_computation.4 | loop fusion | flops 1572864 | bytes 4194305 | tf_op jit(solution)/shard_map/jit(_where)/select_n | solution.py:667
  105.2 1.5 collective-permute-start.17
  108.3 1.7 collective-permute-start.9
  112.6 10.5 %move_columns.4 = (f32[2,256,256]{2,1,0:T(8,128)S(1)}, f32[2,256,256]{2,1,0:T(8,128)}, f32[2,256,256]{2,1,0:T(8,128)S(1)}, f32[2,256,256]{2,1,0:T(8,128)}) custom-call(s32[2]{0:T(128)S(1)} %pad_add_fusion.1.swap_ref, f32[2,256,256]{2,1,0:T(8,128)S(1)} %get-tuple-element.88.refs_0_, f32[2,256,256]{2,1,0:T(8,128)S(1)} %collective-permute-done.1.refs_1_, ...), custom_call_target="tpu_custom_call" | custom-call | flops 8000000000 | bytes 24000000 | tf_op jit(solution)/shard_map/move_columns/pallas_call | solution.py:559
  124.0 6.0 %collective-permute-done.8.refs_2_ = f32[2,256,256]{2,1,0:T(8,128)} collective-permute-done((f32[2,256,256]{2,1,0:T(8,128)}, f32[2,256,256]{2,1,0:T(8,128)}, u32[]{:S(2)}, u32[]{:S(2)}) %collective-permute-start.8) | collective-permute-done | bytes 524320 | tf_op jit(solution)/shard_map/ppermute | solution.py:628
  130.0 10.8 %move_columns.5 = (f32[2,256,256]{2,1,0:T(8,128)S(1)}, f32[2,256,256]{2,1,0:T(8,128)S(1)}, f32[2,256,256]{2,1,0:T(8,128)S(1)}, f32[2,256,256]{2,1,0:T(8,128)}) custom-call(s32[2]{0:T(128)S(1)} %pad_add_fusion.1.swap_ref, f32[2,256,256]{2,1,0:T(8,128)S(1)} %get-tuple-element.92.refs_0_, f32[2,256,256]{2,1,0:T(8,128)S(1)} %collective-permute-done.7.refs_1_, ...), custom_call_target="tpu_custom_call" | custom-call | flops 8000000000 | bytes 24000000 | tf_op jit(solution)/shard_map/move_columns/pallas_call | solution.py:559
  143.2 6.8 %collective-permute-done.4.refs_1_ = f32[2,256,256]{2,1,0:T(8,128)S(1)} collective-permute-done((f32[2,256,256]{2,1,0:T(8,128)}, f32[2,256,256]{2,1,0:T(8,128)S(1)}, u32[]{:S(2)}, u32[]{:S(2)}) %collective-permute-start.4) | collective-permute-done | bytes 524320 | tf_op jit(solution)/shard_map/ppermute | solution.py:628
  149.9 3.1 %collective-permute-start.19 = (f32[2,256,256]{2,1,0:T(8,128)}, f32[2,256,256]{2,1,0:T(8,128)S(1)}, u32[]{:S(2)}, u32[]{:S(2)}) collective-permute-start(f32[2,256,256]{2,1,0:T(8,128)} %get-tuple-element.54), channel_id=1, source_target_pairs={{0,5},{1,4},{2,7},{3,6},{4,1},{5,0},{6,3},{7,2},{8,13},{9,12},{10,... | collective-permute-start | bytes 1572872 | tf_op jit(solution)/shard_map/ppermute | solution.py:628
  156.1 4.0 %maximum_select_fusion.refs_4_.refs_5_.refs_8_ = f32[4,2,2,256,256]{4,3,2,1,0:T(8,128)S(1)} fusion(f32[2,2,2,256,256]{4,3,2,1,0:T(8,128)} %collective-permute-done.17, f32[2,2,2,256,256]{4,3,2,1,0:T(8,128)} %maximum_select_fusion.1, pred[]{:T(512)S(6)} %eq.77), kind=kLoop, calls=%fused_computation.3 | loop fusion | flops 3145728 | bytes 8388609 | tf_op jit(solution)/shard_map/jit(_where)/select_n | solution.py:669
  160.2 7.0 %turn_rows.3 = (f32[2,256,256]{2,1,0:T(8,128)S(1)}, f32[2,256,256]{2,1,0:T(8,128)S(1)}, f32[2,256,256]{2,1,0:T(8,128)S(1)}, f32[2,256,256]{2,1,0:T(8,128)S(1)}) custom-call(f32[1]{0:T(128)} %bitcast.9.scale_ref, f32[2,256,256]{2,1,0:T(8,128)} %get-tuple-element.44.refs_0_, f32[2,256,256]{2,1,0:T(8,128)S(1)} %copy-done.12, ...), custom_call_target="tpu_custom_call" | custom-call | flops 5000000000 | bytes 15000000 | tf_op jit(solution)/shard_map/turn_rows/pallas_call | solution.py:514
  169.0 6.2 %turn_rows.2 = (f32[2,256,256]{2,1,0:T(8,128)S(1)}, f32[2,256,256]{2,1,0:T(8,128)S(1)}, f32[2,256,256]{2,1,0:T(8,128)S(1)}, f32[2,256,256]{2,1,0:T(8,128)S(1)}, f32[2,256,1024]{2,1,0:T(8,128)S(1)}) custom-call(f32[1]{0:T(128)S(6)} %add.328.scale_ref, f32[2,256,256]{2,1,0:T(8,128)S(1)} %copy-done.29, f32[2,256,256]{2,1,0:T(8,128)S(1)} %copy-done.33, ...), custom_call_target="tpu_custom_call" | custom-call | flops 5000000000 | bytes 15000000 | tf_op jit(solution)/shard_map/turn_rows/pallas_call | solution.py:514
  183.4 9.4 %move_columns.7 = (f32[2,256,256]{2,1,0:T(8,128)S(1)}, f32[2,256,256]{2,1,0:T(8,128)S(1)}, f32[2,256,256]{2,1,0:T(8,128)S(1)}, f32[2,256,256]{2,1,0:T(8,128)S(1)}) custom-call(s32[2]{0:T(128)S(1)} %add_add_fusion.swap_ref, f32[2,256,256]{2,1,0:T(8,128)S(1)} %copy-done.39, f32[2,256,256]{2,1,0:T(8,128)S(1)} %copy-done.37, ...), custom_call_target="tpu_custom_call" | custom-call | flops 8000000000 | bytes 24000000 | tf_op jit(solution)/shard_map/move_columns/pallas_call | solution.py:559
  193.8 1.9 collective-permute-start.33
  197.8 9.4 %move_columns.6 = (f32[2,256,256]{2,1,0:T(8,128)S(1)}, f32[2,256,256]{2,1,0:T(8,128)S(1)}, f32[2,256,256]{2,1,0:T(8,128)S(1)}, f32[2,256,256]{2,1,0:T(8,128)S(1)}) custom-call(s32[2]{0:T(128)S(1)} %add_add_fusion.swap_ref, f32[2,256,256]{2,1,0:T(8,128)S(1)} %copy-done.35, f32[2,256,256]{2,1,0:T(8,128)S(1)} %copy-done.31, ...), custom_call_target="tpu_custom_call" | custom-call | flops 8000000000 | bytes 24000000 | tf_op jit(solution)/shard_map/move_columns/pallas_call | solution.py:559
  207.5 1.9 collective-permute-start.32
  209.4 3.7 %image_rows.2 = (f32[256,256]{1,0:T(8,128)S(1)}, f32[256,256]{1,0:T(8,128)S(1)}, f32[256,256]{1,0:T(8,128)S(1)}, f32[256,256]{1,0:T(8,128)S(1)}) custom-call(s32[4]{0:T(128)S(1)} %copy-done.5, f32[1]{0:T(128)} %bitcast.9.scale_ref, f32[2,256,1024]{2,1,0:T(8,128)S(1)} %get-tuple-element.52.refs_0_, f32[2,256,256]{2,1,0:T(8,128)S(1)} %collective-permute-done.4.refs_1_, ...), custom_call_target="tpu_custom_call" | custom-call | flops 4000000000 | bytes 12000000 | tf_op jit(solution)/shard_map/image_rows/pallas_call | solution.py:535
  213.8 5.3 %collective-permute-done.35.refs_7_ = f32[2,256,256]{2,1,0:T(8,128)S(1)} collective-permute-done((f32[2,256,256]{2,1,0:T(8,128)S(1)}, f32[2,256,256]{2,1,0:T(8,128)S(1)}, u32[]{:S(2)}, u32[]{:S(2)}) %collective-permute-start.35) | collective-permute-done | bytes 524320 | tf_op jit(solution)/shard_map/ppermute | solution.py:628
  219.1 3.2 %collective-permute-start.21 = (f32[256,256]{1,0:T(8,128)S(1)}, f32[256,256]{1,0:T(8,128)S(1)}, u32[]{:S(2)}, u32[]{:S(2)}) collective-permute-start(f32[256,256]{1,0:T(8,128)S(1)} %get-tuple-element.56), channel_id=1, source_target_pairs={{0,1},{1,9},{2,3},{3,11},{4,5},{5,13},{6,7},{7,15},{8,0},{9,8},{10... | collective-permute-start | bytes 786440 | tf_op jit(solution)/shard_map/ppermute | solution.py:628
  222.4 1.5 collective-permute-start.22
  223.8 15.5 %collective-permute-done.32.refs_4_ = f32[2,256,256]{2,1,0:T(8,128)S(1)} collective-permute-done((f32[2,256,256]{2,1,0:T(8,128)S(1)}, f32[2,256,256]{2,1,0:T(8,128)S(1)}, u32[]{:S(2)}, u32[]{:S(2)}) %collective-permute-start.32) | collective-permute-done | bytes 524320 | tf_op jit(solution)/shard_map/ppermute | solution.py:628
  240.0 10.1 %collective-permute-done.34.refs_6_ = f32[2,256,256]{2,1,0:T(8,128)S(1)} collective-permute-done((f32[2,256,256]{2,1,0:T(8,128)S(1)}, f32[2,256,256]{2,1,0:T(8,128)S(1)}, u32[]{:S(2)}, u32[]{:S(2)}) %collective-permute-start.34) | collective-permute-done | bytes 524320 | tf_op jit(solution)/shard_map/ppermute | solution.py:628
  250.1 5.2 %image_rows.3 = (f32[256,256]{1,0:T(8,128)S(1)}, f32[256,256]{1,0:T(8,128)S(1)}, f32[256,256]{1,0:T(8,128)S(1)}, f32[256,256]{1,0:T(8,128)S(1)}) custom-call(s32[4]{0:T(128)S(1)} %copy-done.5, f32[1]{0:T(128)} %bitcast.9.scale_ref, f32[2,256,256]{2,1,0:T(8,128)S(1)} %get-tuple-element.63.refs_0_, f32[2,256,256]{2,1,0:T(8,128)S(1)} %copy-done.27, ...), custom_call_target="tpu_custom_call" | custom-call | flops 4000000000 | bytes 12000000 | tf_op jit(solution)/shard_map/image_rows/pallas_call | solution.py:535
  256.0 2.3 collective-permute-start.37
  258.3 2.1 collective-permute-start.38
  260.4 1.1 collective-permute-start.39
  261.6 16.5 %collective-permute-done.37 = f32[256,256]{1,0:T(8,128)S(1)} collective-permute-done((f32[256,256]{1,0:T(8,128)S(1)}, f32[256,256]{1,0:T(8,128)S(1)}, u32[]{:S(2)}, u32[]{:S(2)}) %collective-permute-start.37) | collective-permute-done | bytes 262176 | tf_op jit(solution)/shard_map/ppermute | solution.py:628
  278.1 7.1 %collective-permute-done.39 = f32[256,256]{1,0:T(8,128)S(1)} collective-permute-done((f32[256,256]{1,0:T(8,128)S(1)}, f32[256,256]{1,0:T(8,128)S(1)}, u32[]{:S(2)}, u32[]{:S(2)}) %collective-permute-start.39) | collective-permute-done | bytes 262176 | tf_op jit(solution)/shard_map/ppermute | solution.py:628
  (186 shorter events, 33.2 us)
Async XLA Ops:
  10.3 27.7 %copy-start.43 = (f32[2,2,256,256]{3,2,1,0:T(8,128)S(1)}, f32[2,2,256,256]{3,2,1,0:T(8,128)}, u32[]{:S(2)}) copy-start(f32[2,2,256,256]{3,2,1,0:T(8,128)} %get-tuple-element.42) | copy-start | bytes 3145732
  10.3 27.7 %collective-permute-start = (f32[2,2,256,256]{3,2,1,0:T(8,128)}, f32[2,2,256,256]{3,2,1,0:T(8,128)}, u32[]{:S(2)}, u32[]{:S(2)}) collective-permute-start(f32[2,2,256,256]{3,2,1,0:T(8,128)} %get-tuple-element.43), channel_id=1, source_target_pairs={{0,1},{1,0},{2,3},{3,2},{4,5},{5,4},{6,7},{7,6},{8,9},{9,8},{10,11... | collective-permute-start | bytes 3145736 | tf_op jit(solution)/shard_map/ppermute | solution.py:628
  11.5 15.0 %collective-permute-start.12 = (f32[2,256,128]{2,1,0:T(8,128)}, f32[2,256,128]{2,1,0:T(8,128)}, u32[]{:S(2)}, u32[]{:S(2)}) collective-permute-start(f32[2,256,128]{2,1,0:T(8,128)} %constant_dynamic-slice_fusion.2), channel_id=1, source_target_pairs={{0,4},{1,5},{2,6},{3,7},{4,0},{5,1},{6,2},{7,3},{8,12},{9,13},{10,... | collective-permute-start | bytes 786440 | tf_op jit(solution)/shard_map/ppermute | solution.py:628
  14.1 21.6 %collective-permute-start.13 = (f32[2,256,128]{2,1,0:T(8,128)}, f32[2,256,128]{2,1,0:T(8,128)}, u32[]{:S(2)}, u32[]{:S(2)}) collective-permute-start(f32[2,256,128]{2,1,0:T(8,128)} %constant_dynamic-slice_fusion.2), channel_id=1, source_target_pairs={{0,8},{1,9},{2,10},{3,11},{4,12},{5,13},{6,14},{7,15},{8,0},{9,1},... | collective-permute-start | bytes 786440 | tf_op jit(solution)/shard_map/ppermute | solution.py:628
  16.7 19.1 %collective-permute-start.14 = (f32[2,256,128]{2,1,0:T(8,128)}, f32[2,256,128]{2,1,0:T(8,128)}, u32[]{:S(2)}, u32[]{:S(2)}) collective-permute-start(f32[2,256,128]{2,1,0:T(8,128)} %constant_dynamic-slice_fusion.2), channel_id=1, source_target_pairs={{0,12},{1,13},{2,14},{3,15},{4,8},{5,9},{6,10},{7,11},{8,4},{9,5},... | collective-permute-start | bytes 786440 | tf_op jit(solution)/shard_map/ppermute | solution.py:628
  16.7 32.2 %collective-permute-start.6 = (f32[2,2,256,256]{3,2,1,0:T(8,128)}, f32[2,2,256,256]{3,2,1,0:T(8,128)}, u32[]{:S(2)}, u32[]{:S(2)}) collective-permute-start(f32[2,2,256,256]{3,2,1,0:T(8,128)} %get-tuple-element.47), channel_id=1, source_target_pairs={{0,1},{1,0},{2,3},{3,2},{4,5},{5,4},{6,7},{7,6},{8,9},{9,8},{10,11... | collective-permute-start | bytes 3145736 | tf_op jit(solution)/shard_map/ppermute | solution.py:628
  40.2 27.9 %collective-permute-start.1 = (f32[2,256,256]{2,1,0:T(8,128)S(1)}, f32[2,256,256]{2,1,0:T(8,128)S(1)}, u32[]{:S(2)}, u32[]{:S(2)}) collective-permute-start(f32[2,256,256]{2,1,0:T(8,128)S(1)} %get-tuple-element.86), channel_id=1, source_target_pairs={{0,4},{1,5},{2,6},{3,7},{4,0},{5,1},{6,2},{7,3},{8,12},{9,13},{10,... | collective-permute-start | bytes 1572872 | tf_op jit(solution)/shard_map/ppermute | solution.py:628
  46.5 61.0 %collective-permute-start.2 = (f32[2,256,256]{2,1,0:T(8,128)}, f32[2,256,256]{2,1,0:T(8,128)S(1)}, u32[]{:S(2)}, u32[]{:S(2)}) collective-permute-start(f32[2,256,256]{2,1,0:T(8,128)} %get-tuple-element.87), channel_id=1, source_target_pairs={{0,8},{1,9},{2,10},{3,11},{4,12},{5,13},{6,14},{7,15},{8,0},{9,1},... | collective-permute-start | bytes 1572872 | tf_op jit(solution)/shard_map/ppermute | solution.py:628
  47.4 62.6 %collective-permute-start.3 = (f32[2,256,256]{2,1,0:T(8,128)}, f32[2,256,256]{2,1,0:T(8,128)S(1)}, u32[]{:S(2)}, u32[]{:S(2)}) collective-permute-start(f32[2,256,256]{2,1,0:T(8,128)} %get-tuple-element.85), channel_id=1, source_target_pairs={{0,12},{1,13},{2,14},{3,15},{4,8},{5,9},{6,10},{7,11},{8,4},{9,5},... | collective-permute-start | bytes 1572872 | tf_op jit(solution)/shard_map/ppermute | solution.py:628
  51.4 72.5 %collective-permute-start.7 = (f32[2,256,256]{2,1,0:T(8,128)}, f32[2,256,256]{2,1,0:T(8,128)S(1)}, u32[]{:S(2)}, u32[]{:S(2)}) collective-permute-start(f32[2,256,256]{2,1,0:T(8,128)} %get-tuple-element.90), channel_id=1, source_target_pairs={{0,4},{1,5},{2,6},{3,7},{4,0},{5,1},{6,2},{7,3},{8,12},{9,13},{10,... | collective-permute-start | bytes 1572872 | tf_op jit(solution)/shard_map/ppermute | solution.py:628
  52.4 19.4 %copy-start.40 = (s32[4]{0:T(128)S(1)}, s32[4]{0:T(128)}, u32[]{:S(2)}) copy-start(s32[4]{0:T(128)} %constant.169.clone) | copy-start | bytes 52
  53.3 76.7 %collective-permute-start.8 = (f32[2,256,256]{2,1,0:T(8,128)}, f32[2,256,256]{2,1,0:T(8,128)}, u32[]{:S(2)}, u32[]{:S(2)}) collective-permute-start(f32[2,256,256]{2,1,0:T(8,128)} %get-tuple-element.91), channel_id=1, source_target_pairs={{0,8},{1,9},{2,10},{3,11},{4,12},{5,13},{6,14},{7,15},{8,0},{9,1},... | collective-permute-start | bytes 1572872 | tf_op jit(solution)/shard_map/ppermute | solution.py:628
  71.7 2.3 collective-permute-start.15
  76.6 25.5 %collective-permute-start.16 = (f32[2,2,256,256]{3,2,1,0:T(8,128)}, f32[2,2,256,256]{3,2,1,0:T(8,128)}, u32[]{:S(2)}, u32[]{:S(2)}) collective-permute-start(f32[2,2,256,256]{3,2,1,0:T(8,128)} %maximum_select_fusion.3), channel_id=1, source_target_pairs={{0,2},{1,3},{2,0},{3,1},{4,6},{5,7},{6,4},{7,5},{8,10},{9,11},{10,... | collective-permute-start | bytes 3145736 | tf_op jit(solution)/shard_map/ppermute | solution.py:628
  105.2 50.2 %collective-permute-start.17 = (f32[2,2,2,256,256]{4,3,2,1,0:T(8,128)}, f32[2,2,2,256,256]{4,3,2,1,0:T(8,128)}, u32[]{:S(2)}, u32[]{:S(2)}) collective-permute-start(f32[2,2,2,256,256]{4,3,2,1,0:T(8,128)} %maximum_select_fusion.1), channel_id=1, source_target_pairs={{0,16},{1,17},{2,18},{3,19},{4,20},{5,21},{6,22},{7,23},{8,24},{9,... | collective-permute-start | bytes 6291464 | tf_op jit(solution)/shard_map/ppermute | solution.py:628
  107.4 22.6 %copy-start.2 = (f32[4,2,256,512]{3,2,1,0:T(8,128)}, f32[4,2,256,512]{3,2,1,0:T(8,128)S(1)}, u32[]{:S(2)}) copy-start(f32[4,2,256,512]{3,2,1,0:T(8,128)S(1)} %pad_maximum_fusion.refs_6_) | copy-start | bytes 12582916
  108.3 21.7 %collective-permute-start.9 = (f32[2,256,256]{2,1,0:T(8,128)S(1)}, f32[2,256,256]{2,1,0:T(8,128)S(1)}, u32[]{:S(2)}, u32[]{:S(2)}) collective-permute-start(f32[2,256,256]{2,1,0:T(8,128)S(1)} %copy-done.44), channel_id=1, source_target_pairs={{0,12},{1,13},{2,14},{3,15},{4,8},{5,9},{6,10},{7,11},{8,4},{9,5},... | collective-permute-start | bytes 1572872 | tf_op jit(solution)/shard_map/ppermute | solution.py:628
  123.9 16.9 %copy-start.28 = (f32[2,256,256]{2,1,0:T(8,128)}, f32[2,256,256]{2,1,0:T(8,128)S(1)}, u32[]{:S(2)}) copy-start(f32[2,256,256]{2,1,0:T(8,128)S(1)} %get-tuple-element.46.refs_0_) | copy-start | bytes 1572868
  123.9 29.7 %collective-permute-start.5 = (f32[2,256,256]{2,1,0:T(8,128)}, f32[2,256,256]{2,1,0:T(8,128)S(1)}, u32[]{:S(2)}, u32[]{:S(2)}) collective-permute-start(f32[2,256,256]{2,1,0:T(8,128)} %get-tuple-element.45), channel_id=1, source_target_pairs={{0,5},{1,4},{2,7},{3,6},{4,1},{5,0},{6,3},{7,2},{8,13},{9,12},{10,... | collective-permute-start | bytes 1572872 | tf_op jit(solution)/shard_map/ppermute | solution.py:628
  123.9 36.2 %collective-permute-start.24 = (f32[2,256,256]{2,1,0:T(8,128)}, f32[2,256,256]{2,1,0:T(8,128)}, u32[]{:S(2)}, u32[]{:S(2)}) collective-permute-start(f32[2,256,256]{2,1,0:T(8,128)} %get-tuple-element.45), channel_id=1, source_target_pairs={{0,1},{1,0},{2,3},{3,2},{4,5},{5,4},{6,7},{7,6},{8,9},{9,8},{10,11... | collective-permute-start | bytes 1572872 | tf_op jit(solution)/shard_map/ppermute | solution.py:628
  130.0 19.9 %collective-permute-start.4 = (f32[2,256,256]{2,1,0:T(8,128)}, f32[2,256,256]{2,1,0:T(8,128)S(1)}, u32[]{:S(2)}, u32[]{:S(2)}) collective-permute-start(f32[2,256,256]{2,1,0:T(8,128)} %get-tuple-element.44.refs_0_), channel_id=1, source_target_pairs={{0,4},{1,5},{2,6},{3,7},{4,0},{5,1},{6,2},{7,3},{8,12},{9,13},{10,... | collective-permute-start | bytes 1572872 | tf_op jit(solution)/shard_map/ppermute | solution.py:628
  143.2 17.0 %collective-permute-start.25 = (f32[2,256,256]{2,1,0:T(8,128)}, f32[2,256,256]{2,1,0:T(8,128)}, u32[]{:S(2)}, u32[]{:S(2)}) collective-permute-start(f32[2,256,256]{2,1,0:T(8,128)} %get-tuple-element.54), channel_id=1, source_target_pairs={{0,1},{1,0},{2,3},{3,2},{4,5},{5,4},{6,7},{7,6},{8,9},{9,8},{10,11... | collective-permute-start | bytes 1572872 | tf_op jit(solution)/shard_map/ppermute | solution.py:628
  149.9 27.9 %collective-permute-start.19 = (f32[2,256,256]{2,1,0:T(8,128)}, f32[2,256,256]{2,1,0:T(8,128)S(1)}, u32[]{:S(2)}, u32[]{:S(2)}) collective-permute-start(f32[2,256,256]{2,1,0:T(8,128)} %get-tuple-element.54), channel_id=1, source_target_pairs={{0,5},{1,4},{2,7},{3,6},{4,1},{5,0},{6,3},{7,2},{8,13},{9,12},{10,... | collective-permute-start | bytes 1572872 | tf_op jit(solution)/shard_map/ppermute | solution.py:628
  153.6 15.3 %collective-permute-start.10 = (f32[2,256,256]{2,1,0:T(8,128)}, f32[2,256,256]{2,1,0:T(8,128)S(1)}, u32[]{:S(2)}, u32[]{:S(2)}) collective-permute-start(f32[2,256,256]{2,1,0:T(8,128)} %copy-done.10), channel_id=1, source_target_pairs={{0,1},{1,0},{2,3},{3,2},{4,5},{5,4},{6,7},{7,6},{8,9},{9,8},{10,11... | collective-permute-start | bytes 1572872 | tf_op jit(solution)/shard_map/ppermute | solution.py:628
  155.5 13.4 %collective-permute-start.11 = (f32[2,256,256]{2,1,0:T(8,128)}, f32[2,256,256]{2,1,0:T(8,128)S(1)}, u32[]{:S(2)}, u32[]{:S(2)}) collective-permute-start(f32[2,256,256]{2,1,0:T(8,128)} %copy-done.13), channel_id=1, source_target_pairs={{0,1},{1,0},{2,3},{3,2},{4,5},{5,4},{6,7},{7,6},{8,9},{9,8},{10,11... | collective-permute-start | bytes 1572872 | tf_op jit(solution)/shard_map/ppermute | solution.py:628
  160.1 17.1 %collective-permute-start.18 = (f32[2,256,256]{2,1,0:T(8,128)S(1)}, f32[2,256,256]{2,1,0:T(8,128)S(1)}, u32[]{:S(2)}, u32[]{:S(2)}) collective-permute-start(f32[2,256,256]{2,1,0:T(8,128)S(1)} %copy-done.12), channel_id=1, source_target_pairs={{0,4},{1,5},{2,6},{3,7},{4,0},{5,1},{6,2},{7,3},{8,12},{9,13},{10,... | collective-permute-start | bytes 1572872 | tf_op jit(solution)/shard_map/ppermute | solution.py:628
  168.8 11.4 %collective-permute-start.29 = (f32[2,256,256]{2,1,0:T(8,128)S(1)}, f32[2,256,256]{2,1,0:T(8,128)S(1)}, u32[]{:S(2)}, u32[]{:S(2)}) collective-permute-start(f32[2,256,256]{2,1,0:T(8,128)S(1)} %get-tuple-element.67), channel_id=1, source_target_pairs={{0,1},{1,0},{2,3},{3,2},{4,5},{5,4},{6,7},{7,6},{8,9},{9,8},{10,11... | collective-permute-start | bytes 1572872 | tf_op jit(solution)/shard_map/ppermute | solution.py:628
  169.0 11.3 %copy-start.3 = (f32[4,2,256,512]{3,2,1,0:T(8,128)S(1)}, f32[4,2,256,512]{3,2,1,0:T(8,128)}, u32[]{:S(2)}) copy-start(f32[4,2,256,512]{3,2,1,0:T(8,128)} %copy-done.2) | copy-start | bytes 12582916
  176.8 3.5 %collective-permute-start.28 = (f32[2,256,256]{2,1,0:T(8,128)S(1)}, f32[2,256,256]{2,1,0:T(8,128)S(1)}, u32[]{:S(2)}, u32[]{:S(2)}) collective-permute-start(f32[2,256,256]{2,1,0:T(8,128)S(1)} %get-tuple-element.66), channel_id=1, source_target_pairs={{0,1},{1,0},{2,3},{3,2},{4,5},{5,4},{6,7},{7,6},{8,9},{9,8},{10,11... | collective-permute-start | bytes 1572872 | tf_op jit(solution)/shard_map/ppermute | solution.py:628
  179.7 16.0 %collective-permute-start.27 = (f32[2,256,256]{2,1,0:T(8,128)S(1)}, f32[2,256,256]{2,1,0:T(8,128)S(1)}, u32[]{:S(2)}, u32[]{:S(2)}) collective-permute-start(f32[2,256,256]{2,1,0:T(8,128)S(1)} %get-tuple-element.62), channel_id=1, source_target_pairs={{0,1},{1,0},{2,3},{3,2},{4,5},{5,4},{6,7},{7,6},{8,9},{9,8},{10,11... | collective-permute-start | bytes 1572872 | tf_op jit(solution)/shard_map/ppermute | solution.py:628
  179.9 15.9 %collective-permute-start.26 = (f32[2,256,256]{2,1,0:T(8,128)S(1)}, f32[2,256,256]{2,1,0:T(8,128)S(1)}, u32[]{:S(2)}, u32[]{:S(2)}) collective-permute-start(f32[2,256,256]{2,1,0:T(8,128)S(1)} %get-tuple-element.61), channel_id=1, source_target_pairs={{0,1},{1,0},{2,3},{3,2},{4,5},{5,4},{6,7},{7,6},{8,9},{9,8},{10,11... | collective-permute-start | bytes 1572872 | tf_op jit(solution)/shard_map/ppermute | solution.py:628
  193.7 15.7 %collective-permute-start.31 = (f32[2,256,256]{2,1,0:T(8,128)S(1)}, f32[2,256,256]{2,1,0:T(8,128)S(1)}, u32[]{:S(2)}, u32[]{:S(2)}) collective-permute-start(f32[2,256,256]{2,1,0:T(8,128)S(1)} %get-tuple-element.70), channel_id=1, source_target_pairs={{0,1},{1,0},{2,3},{3,2},{4,5},{5,4},{6,7},{7,6},{8,9},{9,8},{10,11... | collective-permute-start | bytes 1572872 | tf_op jit(solution)/shard_map/ppermute | solution.py:628
  193.8 19.4 %collective-permute-start.33 = (f32[2,256,256]{2,1,0:T(8,128)S(1)}, f32[2,256,256]{2,1,0:T(8,128)S(1)}, u32[]{:S(2)}, u32[]{:S(2)}) collective-permute-start(f32[2,256,256]{2,1,0:T(8,128)S(1)} %get-tuple-element.72), channel_id=1, source_target_pairs={{0,4},{1,5},{2,6},{3,7},{4,0},{5,1},{6,2},{7,3},{8,12},{9,13},{10,... | collective-permute-start | bytes 1572872 | tf_op jit(solution)/shard_map/ppermute | solution.py:628
  195.7 23.5 %collective-permute-start.35 = (f32[2,256,256]{2,1,0:T(8,128)S(1)}, f32[2,256,256]{2,1,0:T(8,128)S(1)}, u32[]{:S(2)}, u32[]{:S(2)}) collective-permute-start(f32[2,256,256]{2,1,0:T(8,128)S(1)} %get-tuple-element.74), channel_id=1, source_target_pairs={{0,5},{1,4},{2,7},{3,6},{4,1},{5,0},{6,3},{7,2},{8,13},{9,12},{10,... | collective-permute-start | bytes 1572872 | tf_op jit(solution)/shard_map/ppermute | solution.py:628
  197.8 11.6 %copy-start.5 = (s32[4]{0:T(128)S(1)}, s32[4]{0:T(128)}, u32[]{:S(2)}) copy-start(s32[4]{0:T(128)} %pad_add_fusion.place_ref) | copy-start | bytes 52
  207.3 15.1 %collective-permute-start.30 = (f32[2,256,256]{2,1,0:T(8,128)S(1)}, f32[2,256,256]{2,1,0:T(8,128)S(1)}, u32[]{:S(2)}, u32[]{:S(2)}) collective-permute-start(f32[2,256,256]{2,1,0:T(8,128)S(1)} %get-tuple-element.69), channel_id=1, source_target_pairs={{0,1},{1,0},{2,3},{3,2},{4,5},{5,4},{6,7},{7,6},{8,9},{9,8},{10,11... | collective-permute-start | bytes 1572872 | tf_op jit(solution)/shard_map/ppermute | solution.py:628
  207.5 31.9 %collective-permute-start.32 = (f32[2,256,256]{2,1,0:T(8,128)S(1)}, f32[2,256,256]{2,1,0:T(8,128)S(1)}, u32[]{:S(2)}, u32[]{:S(2)}) collective-permute-start(f32[2,256,256]{2,1,0:T(8,128)S(1)} %get-tuple-element.71), channel_id=1, source_target_pairs={{0,4},{1,5},{2,6},{3,7},{4,0},{5,1},{6,2},{7,3},{8,12},{9,13},{10,... | collective-permute-start | bytes 1572872 | tf_op jit(solution)/shard_map/ppermute | solution.py:628
  209.4 40.7 %collective-permute-start.34 = (f32[2,256,256]{2,1,0:T(8,128)S(1)}, f32[2,256,256]{2,1,0:T(8,128)S(1)}, u32[]{:S(2)}, u32[]{:S(2)}) collective-permute-start(f32[2,256,256]{2,1,0:T(8,128)S(1)} %get-tuple-element.73), channel_id=1, source_target_pairs={{0,5},{1,4},{2,7},{3,6},{4,1},{5,0},{6,3},{7,2},{8,13},{9,12},{10,... | collective-permute-start | bytes 1572872 | tf_op jit(solution)/shard_map/ppermute | solution.py:628
  209.4 40.7 %copy-start.27 = (f32[2,256,256]{2,1,0:T(8,128)S(1)}, f32[2,256,256]{2,1,0:T(8,128)}, u32[]{:S(2)}) copy-start(f32[2,256,256]{2,1,0:T(8,128)} %copy-done.26) | copy-start | bytes 1572868
  213.1 42.9 %collective-permute-start.20 = (f32[256,256]{1,0:T(8,128)S(1)}, f32[256,256]{1,0:T(8,128)S(1)}, u32[]{:S(2)}, u32[]{:S(2)}) collective-permute-start(f32[256,256]{1,0:T(8,128)S(1)} %get-tuple-element.55), channel_id=1, source_target_pairs={{0,0},{1,8},{2,2},{3,10},{4,4},{5,12},{6,6},{7,14},{8,1},{9,9},{10... | collective-permute-start | bytes 786440 | tf_op jit(solution)/shard_map/ppermute | solution.py:628
  219.1 39.2 %collective-permute-start.21 = (f32[256,256]{1,0:T(8,128)S(1)}, f32[256,256]{1,0:T(8,128)S(1)}, u32[]{:S(2)}, u32[]{:S(2)}) collective-permute-start(f32[256,256]{1,0:T(8,128)S(1)} %get-tuple-element.56), channel_id=1, source_target_pairs={{0,1},{1,9},{2,3},{3,11},{4,5},{5,13},{6,7},{7,15},{8,0},{9,8},{10... | collective-permute-start | bytes 786440 | tf_op jit(solution)/shard_map/ppermute | solution.py:628
  222.4 38.1 %collective-permute-start.22 = (f32[256,256]{1,0:T(8,128)S(1)}, f32[256,256]{1,0:T(8,128)S(1)}, u32[]{:S(2)}, u32[]{:S(2)}) collective-permute-start(f32[256,256]{1,0:T(8,128)S(1)} %get-tuple-element.57), channel_id=1, source_target_pairs={{0,2},{1,10},{2,0},{3,8},{4,6},{5,14},{6,4},{7,12},{8,3},{9,11},{1... | collective-permute-start | bytes 786440 | tf_op jit(solution)/shard_map/ppermute | solution.py:628
  239.4 22.2 %collective-permute-start.23 = (f32[256,256]{1,0:T(8,128)S(1)}, f32[256,256]{1,0:T(8,128)S(1)}, u32[]{:S(2)}, u32[]{:S(2)}) collective-permute-start(f32[256,256]{1,0:T(8,128)S(1)} %get-tuple-element.58), channel_id=1, source_target_pairs={{0,3},{1,11},{2,1},{3,9},{4,7},{5,15},{6,5},{7,13},{8,2},{9,10},{1... | collective-permute-start | bytes 786440 | tf_op jit(solution)/shard_map/ppermute | solution.py:628
  250.1 36.1 %copy-start.1 = (f32[2,256,1024]{2,1,0:T(8,128)S(1)}, f32[2,256,1024]{2,1,0:T(8,128)}, u32[]{:S(2)}) copy-start(f32[2,256,1024]{2,1,0:T(8,128)} %param.14) | copy-start | bytes 6291460
  255.3 6.3 %collective-permute-start.36 = (f32[256,256]{1,0:T(8,128)S(1)}, f32[256,256]{1,0:T(8,128)S(1)}, u32[]{:S(2)}, u32[]{:S(2)}) collective-permute-start(f32[256,256]{1,0:T(8,128)S(1)} %get-tuple-element.75), channel_id=1, source_target_pairs={{0,0},{1,8},{2,2},{3,10},{4,4},{5,12},{6,6},{7,14},{8,1},{9,9},{10... | collective-permute-start | bytes 786440 | tf_op jit(solution)/shard_map/ppermute | solution.py:628
  256.0 22.1 %collective-permute-start.37 = (f32[256,256]{1,0:T(8,128)S(1)}, f32[256,256]{1,0:T(8,128)S(1)}, u32[]{:S(2)}, u32[]{:S(2)}) collective-permute-start(f32[256,256]{1,0:T(8,128)S(1)} %get-tuple-element.76), channel_id=1, source_target_pairs={{0,1},{1,9},{2,3},{3,11},{4,5},{5,13},{6,7},{7,15},{8,0},{9,8},{10... | collective-permute-start | bytes 786440 | tf_op jit(solution)/shard_map/ppermute | solution.py:628
  258.3 19.8 %collective-permute-start.38 = (f32[256,256]{1,0:T(8,128)S(1)}, f32[256,256]{1,0:T(8,128)S(1)}, u32[]{:S(2)}, u32[]{:S(2)}) collective-permute-start(f32[256,256]{1,0:T(8,128)S(1)} %get-tuple-element.77), channel_id=1, source_target_pairs={{0,2},{1,10},{2,0},{3,8},{4,6},{5,14},{6,4},{7,12},{8,3},{9,11},{1... | collective-permute-start | bytes 786440 | tf_op jit(solution)/shard_map/ppermute | solution.py:628
  260.4 24.8 %collective-permute-start.39 = (f32[256,256]{1,0:T(8,128)S(1)}, f32[256,256]{1,0:T(8,128)S(1)}, u32[]{:S(2)}, u32[]{:S(2)}) collective-permute-start(f32[256,256]{1,0:T(8,128)S(1)} %get-tuple-element.78), channel_id=1, source_target_pairs={{0,3},{1,11},{2,1},{3,9},{4,7},{5,15},{6,5},{7,13},{8,2},{9,10},{1... | collective-permute-start | bytes 786440 | tf_op jit(solution)/shard_map/ppermute | solution.py:628
  (38 other events, 154.3 us)

commit v3 on v2

--- a/solution.py
+++ b/solution.py
@@ -165,7 +165,7 @@
 lanes = 128
 y_radix = 8
 x_radix = 4
-row_block = 64
+row_group = 32
 strip = 16
 
 
@@ -176,7 +176,7 @@
         and sizes["fld"] == 2
         and shape[2] == 2
         and shape[4] == y_radix * lanes
-        and shape[3] % row_block == 0
+        and shape[3] % row_group == 0
         and shape[3] * 4 == shape[4]
     )
 
@@ -321,27 +321,35 @@
     return slice(index * lanes, (index + 1) * lanes)
 
 
+def row_groups(rows):
+    return [slice(first, first + row_group) for first in range(0, rows, row_group)]
+
+
 def origin_kernel(place_ref, field_ref, table_ref, upper_ref, lower_ref, *outs):
     sign = (1 - 2 * place_ref[3]).astype(jnp.float32)
-    terms = []
-    for a in range(y_radix):
-        term = (field_ref[0, 0, :, lane_block(a)], field_ref[1, 0, :, lane_block(a)])
-        terms.append((term[0] * sign, term[1] * sign) if a % 2 else term)
-    spectrum = forward_y(terms, table_ref, upper_ref, lower_ref)
-    for k in range(y_radix):
-        for part in range(2):
-            outs[k // 2][0, part, :, lane_block(k % 2)] = spectrum[k][part]
-
-
-def read_y_blocks(blocks):
+    for rows in row_groups(field_ref.shape[2]):
+        terms = []
+        for a in range(y_radix):
+            term = (field_ref[0, 0, rows, lane_block(a)], field_ref[1, 0, rows, lane_block(a)])
+            terms.append((term[0] * sign, term[1] * sign) if a % 2 else term)
+        spectrum = forward_y(terms, table_ref, upper_ref, lower_ref)
+        for k in range(y_radix):
+            for part in range(2):
+                outs[k // 2][0, part, rows, lane_block(k % 2)] = spectrum[k][part]
+
+
+def read_y_blocks(blocks, rows):
     return [
-        tuple(blocks[k // 2][part, :, lane_block(k % 2)] for part in range(2))
+        tuple(blocks[k // 2][part, rows, lane_block(k % 2)] for part in range(2))
         for k in range(y_radix)
     ]
 
 
-def read_screen(scale_ref, slowness_ref, a):
-    layer = slowness_ref[a // 2, 0, 0, :, lane_block(a % 2)]
+def read_layer(ref, at, rows):
+    return [ref[a // 2, at[0], at[1], rows, lane_block(a % 2)] for a in range(y_radix)]
+
+
+def screen_of(scale_ref, layer):
     phase = scale_ref[0] * ((layer - reference_slowness) * depth_interval)
     square = phase * phase
     cosine, sine = 1.0 / 40320.0, 1.0 / 362880.0
@@ -352,113 +360,120 @@
     return cosine, sine * phase
 
 
-def turn_kernel(keeps_field, scale_ref, *refs):
-    blocks, rest = refs[:4], refs[4:]
-    screen_ref, table_ref, inv_upper, inv_lower, upper_ref, lower_ref = rest[:6]
-    outs = rest[6:]
-    terms = inverse_y(read_y_blocks(blocks), table_ref, inv_upper, inv_lower)
-    terms = [multiply(terms[a], read_screen(scale_ref, screen_ref, a)) for a in range(y_radix)]
-    if keeps_field:
-        for a in range(y_radix):
+def turn_kernel(keeps_field, at, scale_ref, *refs):
+    blocks, layer_ref, refs = refs[:4], refs[4], refs[5:]
+    table_ref, inv_upper, inv_lower, upper_ref, lower_ref = refs[:5]
+    outs = refs[5:]
+    for rows in row_groups(blocks[0].shape[1]):
+        terms = inverse_y(read_y_blocks(blocks, rows), table_ref, inv_upper, inv_lower)
+        layer = read_layer(layer_ref, at, rows)
+        terms = [multiply(terms[a], screen_of(scale_ref, layer[a])) for a in range(y_radix)]
+        if keeps_field:
+            for a in range(y_radix):
+                for part in range(2):
+                    outs[4][part, rows, lane_block(a)] = terms[a][part]
+        spectrum = forward_y(terms, table_ref, upper_ref, lower_ref)
+        for k in range(y_radix):
             for part in range(2):
-                outs[4][part, :, lane_block(a)] = terms[a][part]
-    spectrum = forward_y(terms, table_ref, upper_ref, lower_ref)
-    for k in range(y_radix):
-        for part in range(2):
-            outs[k // 2][part, :, lane_block(k % 2)] = spectrum[k][part]
-
-
-def image_kernel(own_ready, place_ref, scale_ref, *refs):
+                outs[k // 2][part, rows, lane_block(k % 2)] = spectrum[k][part]
+
+
+def image_kernel(own_ready, at, place_ref, scale_ref, *refs):
     own_count = 1 if own_ready else 4
     own, refs = refs[:own_count], refs[own_count:]
-    blocks, refs = refs[:4], refs[4:]
-    screen_ref, table_ref, inv_upper, inv_lower = refs[:4]
-    outs, quarters = refs[4:8], refs[8]
-    other = inverse_y(read_y_blocks(blocks), table_ref, inv_upper, inv_lower)
-    if not own_ready:
-        mine = inverse_y(read_y_blocks(own), table_ref, inv_upper, inv_lower)
-    for a in range(y_radix):
-        screen = read_screen(scale_ref, screen_ref, a)
-        if own_ready:
-            near = (own[0][0, :, lane_block(a)], own[0][1, :, lane_block(a)])
-        else:
-            near = multiply(mine[a], screen)
-        far = multiply(other[a], conjugate(screen))
-        quarters[a // 2, :, lane_block(a % 2)] = near[0] * far[0] + near[1] * far[1]
+    blocks, layer_ref, refs = refs[:4], refs[4], refs[5:]
+    table_ref, inv_upper, inv_lower = refs[:3]
+    outs, quarters = refs[3:7], refs[7]
+    for rows in row_groups(blocks[0].shape[1]):
+        layer = read_layer(layer_ref, at, rows)
+        other = inverse_y(read_y_blocks(blocks, rows), table_ref, inv_upper, inv_lower)
+        if not own_ready:
+            mine = inverse_y(read_y_blocks(own, rows), table_ref, inv_upper, inv_lower)
+        for a in range(y_radix):
+            screen = screen_of(scale_ref, layer[a])
+            if own_ready:
+                near = (own[0][0, rows, lane_block(a)], own[0][1, rows, lane_block(a)])
+            else:
+                near = multiply(mine[a], screen)
+            far = multiply(other[a], conjugate(screen))
+            quarters[a // 2, rows, lane_block(a % 2)] = near[0] * far[0] + near[1] * far[1]
     for r in range(4):
         outs[r][...] = quarters[lax.bitwise_xor(2 * place_ref[2] + place_ref[1] // 2, r)]
 
 
-def x_kernel(pieces, swap_ref, *refs):
-    blocks, refs = refs[: x_radix * pieces], refs[x_radix * pieces :]
-    table_in, table_out, move_ref, upper_ref, lower_ref, inv_upper, inv_lower = refs[:7]
-    outs, (high, low, held) = refs[7:11], refs[11:]
-    rows = blocks[0].shape[1]
-
-    def wide(table, k, part, span):
-        values = table[k, part, span, :]
+def x_kernel(swap_ref, *refs):
+    blocks, refs = refs[:x_radix], refs[x_radix:]
+    table_in, table_out, half_ref, move_ref, upper_ref, lower_ref, inv_upper, inv_lower = refs[:8]
+    outs, (high, low, held) = refs[8:12], refs[12:]
+    inner = blocks[0].shape[1] // 2
+
+    def wide(table, *at):
+        values = table[at]
         return jnp.concatenate([values] * (held.shape[2] // lanes), axis=1)
-
-    def read(q, part, span):
-        values = [block[part, span, :] for block in blocks[q * pieces : (q + 1) * pieces]]
-        return values[0] if pieces == 1 else jnp.concatenate(values, axis=1)
 
     def actual(k, swaps):
         return k if k % 2 == 0 else lax.bitwise_xor(k, 2 * swaps)
 
+    def spans(step):
+        first = pl.multiple_of(step * strip, strip)
+        return pl.ds(first, strip), pl.ds(pl.multiple_of(first + inner, strip), strip)
+
     def gather_rows(step, carry):
-        span = pl.ds(pl.multiple_of(step * strip, strip), strip)
-        lower_span = pl.ds(pl.multiple_of(step * strip + rows, strip), strip)
-        terms = dft4([(read(q, 0, span), read(q, 1, span)) for q in range(x_radix)], -1.0)
+        span, second = spans(step)
+        halves = []
+        for rows in (span, second):
+            terms = dft4([(block[0, rows, :], block[1, rows, :]) for block in blocks], -1.0)
+            halves.append(
+                [
+                    multiply(terms[k], (wide(table_in, k, 0, rows), wide(table_in, k, 1, rows)))
+                    for k in range(x_radix)
+                ]
+            )
+        turn = (wide(half_ref, 0, span), wide(half_ref, 1, span))
         for k in range(x_radix):
-            factor = (wide(table_in, k, 0, span), wide(table_in, k, 1, span))
-            real, imag = multiply(terms[k], factor)
-            goal = actual(k, swap_ref[0])
-            high[goal, span, :], low[goal, span, :] = two_parts(real)
-            high[goal, lower_span, :], low[goal, lower_span, :] = two_parts(imag)
+            goal = 2 * actual(k, swap_ref[0])
+            pair = (
+                add(halves[0][k], halves[1][k]),
+                multiply(subtract(halves[0][k], halves[1][k]), turn),
+            )
+            for e in range(2):
+                high[goal + e, span, :], low[goal + e, span, :] = two_parts(pair[e][0])
+                high[goal + e, second, :], low[goal + e, second, :] = two_parts(pair[e][1])
         return carry
 
-    lax.fori_loop(0, rows // strip, gather_rows, 0)
-
-    def one_block(k, carry):
+    lax.fori_loop(0, inner // strip, gather_rows, 0, unroll=2)
+
+    for k in range(2 * x_radix):
         values = columns_product(upper_ref, lower_ref, high[k], low[k])
-        moved = multiply((values[:rows], values[rows:]), (move_ref[k, 0], move_ref[k, 1]))
+        moved = multiply((values[:inner], values[inner:]), (move_ref[k, 0], move_ref[k, 1]))
         upper, lower = two_parts(jnp.concatenate(moved, axis=0))
         held[k] = columns_product(inv_upper, inv_lower, upper, lower)
+
+    def scatter_rows(step, carry):
+        span, second = spans(step)
+        turn = (wide(half_ref, 0, span), -wide(half_ref, 1, span))
+        halves = [[], []]
+        for k in range(x_radix):
+            source = 2 * actual(k, swap_ref[1])
+            even = (held[source, span, :], held[source, second, :])
+            odd = multiply((held[source + 1, span, :], held[source + 1, second, :]), turn)
+            for half, rows, term in ((0, span, add(even, odd)), (1, second, subtract(even, odd))):
+                factor = (wide(table_out, k, 0, rows), -wide(table_out, k, 1, rows))
+                halves[half].append(multiply(term, factor))
+        for half, rows in ((0, span), (1, second)):
+            terms = dft4(halves[half], 1.0)
+            for q in range(x_radix):
+                for part in range(2):
+                    outs[q][part, rows, :] = terms[q][part]
         return carry
 
-    lax.fori_loop(0, x_radix, one_block, 0)
-
-    def scatter_rows(step, carry):
-        span = pl.ds(pl.multiple_of(step * strip, strip), strip)
-        lower_span = pl.ds(pl.multiple_of(step * strip + rows, strip), strip)
-        terms = []
-        for k in range(x_radix):
-            source = actual(k, swap_ref[1])
-            factor = (wide(table_out, k, 0, span), -wide(table_out, k, 1, span))
-            terms.append(multiply((held[source, span, :], held[source, lower_span, :]), factor))
-        terms = dft4(terms, 1.0)
-        for q in range(x_radix):
-            for part in range(2):
-                outs[q][part, span, :] = terms[q][part]
-        return carry
-
-    lax.fori_loop(0, rows // strip, scatter_rows, 0)
-
-
-def whole(array):
-    return pl.BlockSpec(array.shape, lambda *step: (0,) * array.ndim)
+    lax.fori_loop(0, inner // strip, scatter_rows, 0, unroll=2)
 
 
 smem = pl.BlockSpec(memory_space=pltpu.SMEM)
 vmem = pl.BlockSpec(memory_space=pltpu.VMEM)
-vmem_limit = 40 * 1024 * 1024
-
-
-def parameters(steps, limit=vmem_limit):
-    return pltpu.CompilerParams(
-        vmem_limit_bytes=limit, dimension_semantics=("arbitrary",) * steps
-    )
+column_limit = 24 * 1024 * 1024
+row_limit = 24 * 1024 * 1024
 
 
 def estimate(microseconds):
@@ -473,105 +488,83 @@
     out = jax.ShapeDtypeStruct((freqs, parts, rows, width), jnp.float32)
 
     def fixed(array):
-        return pl.BlockSpec(array.shape, lambda j, i, place: (0,) * array.ndim)
+        return pl.BlockSpec(array.shape, lambda j, place: (0,) * array.ndim)
 
     return pl.pallas_call(
         origin_kernel,
         grid_spec=pltpu.PrefetchScalarGridSpec(
             num_scalar_prefetch=1,
-            grid=(freqs, rows // row_block),
+            grid=(freqs,),
             in_specs=[
-                pl.BlockSpec((parts, 1, row_block, y_cols), lambda j, i, place: (0, j, i, 0)),
+                pl.BlockSpec((parts, 1, rows, y_cols), lambda j, place: (0, j, 0, 0)),
                 fixed(table),
                 fixed(matrices[0]),
                 fixed(matrices[1]),
             ],
             out_specs=[
                 pl.BlockSpec(
-                    (1, parts, row_block, width),
-                    lambda j, i, place: (lax.bitwise_xor(j, place[1] // 2), 0, i, 0),
+                    (1, parts, rows, width),
+                    lambda j, place: (lax.bitwise_xor(j, place[1] // 2), 0, 0, 0),
                 )
             ]
             * 4,
         ),
         out_shape=[out] * 4,
-        compiler_params=parameters(2, 60 * 1024 * 1024),
+        compiler_params=pltpu.CompilerParams(
+            vmem_limit_bytes=60 * 1024 * 1024, dimension_semantics=("arbitrary",)
+        ),
         cost_estimate=estimate(6),
         name="origin_rows",
     )(place, field, table, *matrices)
 
 
-def turn_rows(keeps_field, depth_step, slot, scale, blocks, screen, table, inverse, forward):
+def turn_rows(keeps_field, at, scale, blocks, layers, table, inverse, forward):
     parts, rows, width = blocks[0].shape
-    y_cols = screen.shape[0] * screen.shape[-1]
-    block = pl.BlockSpec((parts, row_block, width), lambda i: (0, i, 0))
-    full = pl.BlockSpec((parts, row_block, y_cols), lambda i: (0, i, 0))
     out = [jax.ShapeDtypeStruct((parts, rows, width), jnp.float32)] * 4
-    out_specs = [block] * 4
     if keeps_field:
-        out = out + [jax.ShapeDtypeStruct((parts, rows, y_cols), jnp.float32)]
-        out_specs = out_specs + [full]
+        out = out + [jax.ShapeDtypeStruct((parts, rows, 4 * width), jnp.float32)]
     return pl.pallas_call(
-        functools.partial(turn_kernel, keeps_field),
-        grid=(rows // row_block,),
-        in_specs=[smem]
-        + [block] * 4
-        + [pl.BlockSpec((4, 1, 1, row_block, width), lambda i: (0, depth_step, slot, i, 0))]
-        + [whole(array) for array in (table, *inverse, *forward)],
-        out_specs=out_specs,
+        functools.partial(turn_kernel, keeps_field, at),
+        in_specs=[smem] + [vmem] * 10,
+        out_specs=[vmem] * len(out),
         out_shape=out,
-        compiler_params=parameters(1),
-        cost_estimate=estimate(5),
+        compiler_params=pltpu.CompilerParams(vmem_limit_bytes=row_limit),
+        cost_estimate=estimate(4),
         name="turn_rows",
-    )(scale, *blocks, screen, table, *inverse, *forward)
-
-
-def image_rows(depth_step, place, scale, own, blocks, screen, table, inverse):
+    )(scale, *blocks, layers, table, *inverse, *forward)
+
+
+def image_rows(at, place, scale, own, blocks, layers, table, inverse):
     parts, rows, width = blocks[0].shape
-    y_cols = screen.shape[0] * screen.shape[-1]
-    own_ready = len(own) == 1
-    block = pl.BlockSpec((parts, row_block, width), lambda i: (0, i, 0))
-    full = pl.BlockSpec((parts, row_block, y_cols), lambda i: (0, i, 0))
     return pl.pallas_call(
-        functools.partial(image_kernel, own_ready),
-        grid=(rows // row_block,),
-        in_specs=[smem, smem]
-        + ([full] if own_ready else [block] * 4)
-        + [block] * 4
-        + [pl.BlockSpec((4, 1, 1, row_block, width), lambda i: (0, depth_step, 0, i, 0))]
-        + [whole(array) for array in (table, *inverse)],
-        out_specs=[pl.BlockSpec((row_block, width), lambda i: (i, 0))] * 4,
+        functools.partial(image_kernel, len(own) == 1, at),
+        in_specs=[smem, smem] + [vmem] * (len(own) + 8),
+        out_specs=[vmem] * 4,
         out_shape=[jax.ShapeDtypeStruct((rows, width), jnp.float32)] * 4,
-        scratch_shapes=[pltpu.VMEM((4, row_block, width), jnp.float32)],
-        compiler_params=parameters(1),
-        cost_estimate=estimate(4),
+        scratch_shapes=[pltpu.VMEM((4, rows, width), jnp.float32)],
+        compiler_params=pltpu.CompilerParams(vmem_limit_bytes=row_limit),
+        cost_estimate=estimate(3),
         name="image_rows",
-    )(place, scale, *own, *blocks, screen, table, *inverse)
-
-
-def move_columns(chunk, swaps, blocks, table_in, table_out, move, forward, inverse):
-    pieces = len(blocks[0])
-    parts, rows, width = blocks[0][0].shape
-    width = pieces * width
-    move_block = pl.BlockSpec((x_radix, parts, rows, width), lambda i: (0, 0, 0, chunk))
-    blocks = [piece for block in blocks for piece in block]
-    block = pl.BlockSpec((parts, rows, width), lambda i: (0, 0, 0))
+    )(place, scale, *own, *blocks, layers, table, *inverse)
+
+
+def move_columns(swaps, blocks, tables, move, forward, inverse):
+    parts, rows, width = blocks[0].shape
+    inner = parts * rows // 2
     return pl.pallas_call(
-        functools.partial(x_kernel, pieces),
-        grid=(1,),
-        in_specs=[smem] + [whole(piece) for piece in blocks] + [whole(table_in), whole(table_out), move_block]
-        + [whole(array) for array in (*forward, *inverse)],
-        out_specs=[block] * 4,
-        out_shape=[jax.ShapeDtypeStruct((parts, rows, width), jnp.float32)] * 4,
+        x_kernel,
+        in_specs=[smem] + [vmem] * (x_radix + 8),
+        out_specs=[vmem] * x_radix,
+        out_shape=[jax.ShapeDtypeStruct((parts, rows, width), jnp.float32)] * x_radix,
         scratch_shapes=[
-            pltpu.VMEM((x_radix, parts * rows, width), jnp.bfloat16),
-            pltpu.VMEM((x_radix, parts * rows, width), jnp.bfloat16),
-            pltpu.VMEM((x_radix, parts * rows, width), jnp.float32),
+            pltpu.VMEM((2 * x_radix, inner, width), jnp.bfloat16),
+            pltpu.VMEM((2 * x_radix, inner, width), jnp.bfloat16),
+            pltpu.VMEM((2 * x_radix, inner, width), jnp.float32),
         ],
-        compiler_params=parameters(1),
-        cost_estimate=estimate(8),
+        compiler_params=pltpu.CompilerParams(vmem_limit_bytes=column_limit),
+        cost_estimate=estimate(6),
         name="move_columns",
-    )(swaps, *blocks, table_in, table_out, move, *forward, *inverse)
+    )(swaps, *blocks, *tables, move, *forward, *inverse)
 
 
 def y_table(core, y_cols):
@@ -596,11 +589,30 @@
     return jnp.broadcast_to(table[..., None], table.shape + (lanes,))
 
 
-def move_table(omega, polarity, core, x_total, y_total):
-    k = jnp.arange(x_radix, dtype=jnp.int32)[:, None]
-    inner = jnp.arange(x_total // x_radix, dtype=jnp.int32)[None, :]
-    x_waves = wave_number(k + x_radix * inner, x_total)
-    ky = jnp.arange(y_radix // 2, dtype=jnp.int32)[:, None] + y_radix // 2 * core
+def cosine_sine(angles):
+    half = 0.5 * angles
+    square = half * half
+    cosine, sine = 1.0 / math.factorial(12), -1.0 / math.factorial(11)
+    for order in (10, 8, 6, 4, 2, 0):
+        sign = -1.0 if order % 4 else 1.0
+        cosine = cosine * square + sign / math.factorial(order)
+        if order:
+            sine = sine * square - sign / math.factorial(order - 1)
+    sine = sine * half
+    return 1.0 - 2.0 * sine * sine, 2.0 * sine * cosine
+
+
+def half_table(rows):
+    angles = -2.0 * np.pi / rows * np.arange(rows // 2)
+    table = np.stack([np.cos(angles), np.sin(angles)]).astype(np.float32)
+    return jnp.asarray(np.ascontiguousarray(np.broadcast_to(table[..., None], table.shape + (lanes,))))
+
+
+def move_table(chunk, omega, polarity, core, x_total, y_total):
+    step = jnp.arange(2 * x_radix, dtype=jnp.int32)[:, None]
+    inner = jnp.arange(x_total // (2 * x_radix), dtype=jnp.int32)[None, :]
+    x_waves = wave_number(step // 2 + x_radix * (2 * inner + step % 2), x_total)
+    ky = jnp.arange(2, dtype=jnp.int32)[:, None] + 2 * chunk + y_radix // 2 * core
     inner = jnp.arange(lanes, dtype=jnp.int32)[None, :]
     y_waves = wave_number((ky + y_radix * inner).reshape(-1), y_total)
     lateral = x_waves[:, :, None] ** 2 + y_waves[None, None, :] ** 2
@@ -610,7 +622,8 @@
     amplitude = jnp.where(travels, 1.0, jnp.exp(-kz_root * depth_interval))
     amplitude = amplitude / (x_total * y_total)
     angles = jnp.where(travels, polarity * kz_root * depth_interval, 0.0)
-    return jnp.stack([amplitude * jnp.cos(angles), amplitude * jnp.sin(angles)], axis=1)
+    cosine, sine = cosine_sine(angles)
+    return jnp.stack([amplitude * cosine, amplitude * sine], axis=1)
 
 
 def zero_after(*others):
@@ -647,8 +660,8 @@
 
     row_forward = row_matrix(lanes, -1.0)
     row_inverse = row_matrix(lanes, 1.0)
-    column_forward = column_matrix(rows, -1.0)
-    column_inverse = column_matrix(rows, 1.0)
+    column_forward = column_matrix(rows // 2, -1.0)
+    column_inverse = column_matrix(rows // 2, 1.0)
 
     width = y_cols // 8
     piece = lax.dynamic_slice_in_dim(slowness, (4 * s + 2 * x + c) * width, width, 2)
@@ -678,9 +691,9 @@
         odd = jnp.where(kept_is_odd, kept, crossed)
         far = along_z(even[1], 2)
         farthest = along_z(odd[1], 3)
-        arrived.append([[even[0]], [along_z(odd[0], 1)], [far], [farthest]])
-
-    late = zero_after(arrived[0][1][0])
+        arrived.append([even[0], along_z(odd[0], 1), far, farthest])
+
+    late = zero_after(arrived[0][1])
     layers = all_columns(late)
 
     z_late = z + late
@@ -689,7 +702,8 @@
     omega = omega_unit * index.astype(jnp.float32)
     polarity = (2 * side - 1).astype(jnp.float32)
     order = 2 * c + side
-    move = move_table(omega, polarity, c, x_total, y_cols)
+    moves = [move_table(chunk, omega, polarity, c, x_total, y_cols) for chunk in range(2)]
+    half = half_table(rows)
     table_z = x_table(z_late, x_total)
     table_order = x_table(order, x_total)
     scale = (polarity * omega).reshape(1)
@@ -702,7 +716,7 @@
         near, partner = [], []
         for chunk in range(2):
             out = move_columns(
-                chunk, swaps, blocks_in[chunk], table_in, table_order, move,
+                swaps, blocks_in[chunk], (table_in, table_order, half), moves[chunk],
                 column_forward, column_inverse,
             )
             crossed = [to_core(out[2]), None if last else to_core(out[3])]
@@ -720,23 +734,18 @@
             for slot in (1, 0):
                 blocks = y_blocks([near[0][slot], near[1][slot]])
                 turned[slot] = turn_rows(
-                    slot == 0, depth_step, slot, scale + waits[slot], blocks, layers, y_steps,
+                    slot == 0, (depth_step, slot), scale + waits[slot], blocks, layers, y_steps,
                     row_inverse, row_forward,
                 )
             blocks_in = [
-                [
-                    [turned[0][k]],
-                    [turned[1][k]],
-                    [to_core(turned[0][2 + k])],
-                    [to_core(turned[1][2 + k])],
-                ]
+                [turned[0][k], turned[1][k], to_core(turned[0][2 + k]), to_core(turned[1][2 + k])]
                 for k in range(2)
             ]
             hold = zero_after(*partner[1])
             order_in, table_in = order, table_order
             own = [turned[0][4]]
         terms = image_rows(
-            depth_step, place, scale, own, far_blocks, layers, y_steps, row_inverse
+            (depth_step, 0), place, scale, own, far_blocks, layers, y_steps, row_inverse
         )
 
         def gather(r):

time: 287 us -> 265 us (0.923)
  Pallas kernels: 71 us -> 41.2 us
  waiting for transfers between devices: 113 us -> 138 us
  other arithmetic: 28.2 us -> 21.2 us
  local copies, waits for them, and re-layouts: 27.1 us -> 20.9 us
  starting transfers between devices: 42.4 us -> 38.8 us
    pallas_call x8, Pallas kernels: 62.2 us -> 35 us  [the longest x4 20.4 us: move_columns(): pl.pallas_call(x_kernel, in_specs=[smem] + [vmem] * (x_radix + 8), out_sp...]
    ppermute x40, waiting for transfers between devices: 113 us -> 138 us  [send(): return lax.ppermute(array, axes, route(sizes, target))]
    unnamed x92 -> x70, local copies, waits for them, and re-layouts: 15.1 us -> 8.38 us
    mul x2, other arithmetic: 8.6 us -> 3.37 us  [the longest x1 3.36 us: move_table(): return jnp.stack([amplitude * cosine, amplitude * sine], axis=1)]
    ppermute x40, starting transfers between devices: 42.4 us -> 38.8 us  [send(): return lax.ppermute(array, axes, route(sizes, target))]
  transfers between devices with their start and end apart: 40 -> 40, of which waited for: 12 -> 14; matrix products, arithmetic and copies ran while one was open for 13% -> 12% of each run, Pallas kernels for 22% -> 16%
where the time goes in v3:
time: 265 us; the launch traced here: 264 us
  waiting for transfers between devices  138 us (52%)
  Pallas kernels  41.2 us (16%)
  starting transfers between devices  38.8 us (15%)
  other arithmetic  21.2 us (8%)
  local copies, waits for them, and re-layouts  20.9 us (8%)
  between operations  4.38 us (2%)
    ppermute x40, waiting for transfers between devices, send(): return lax.ppermute(array, axes, route(sizes, target))  138 us
    ppermute x40, starting transfers between devices, send(): return lax.ppermute(array, axes, route(sizes, target))  38.8 us
    pallas_call x4, Pallas kernels, move_columns(): pl.pallas_call(x_kernel, in_specs=[smem] + [vmem] * (x_radix + 8), out_sp...  20.4 us
    unnamed x70, local copies, waits for them, and re-layouts  8.38 us
    pallas_call x2, Pallas kernels, image_rows(): pl.pallas_call(functools.partial(image_kernel, len(own) == 1, at), in_spe...  7.33 us
    pallas_call x2, Pallas kernels, turn_rows(): pl.pallas_call(functools.partial(turn_kernel, keeps_field, at), in_specs=...  7.31 us
    pallas_call x1, Pallas kernels, origin_rows(): pl.pallas_call(origin_kernel, grid_spec=pltpu.PrefetchScalarGridSpec(num_...  6.15 us
  transfers between devices with their start and end apart: 40, of which 14 were waited for; matrix products, arithmetic and copies ran while one was open for 12% of the time, Pallas kernels for 16%

profile of v3, /device:TPU:0, one launch (start us, length us, event | category | flops | bytes accessed | tf_op | source)
XLA Modules:
  0.0 264.1 jit_solution(1705309287534380294)
XLA Ops:
  0.0 1.6 copy-done
  2.3 3.0 %collective-permute-start.12 = (f32[2,256,128]{2,1,0:T(8,128)}, f32[2,256,128]{2,1,0:T(8,128)}, u32[]{:S(2)}, u32[]{:S(2)}) collective-permute-start(f32[2,256,128]{2,1,0:T(8,128)} %constant_dynamic-slice_fusion.2), channel_id=1, source_target_pairs={{0,4},{1,5},{2,6},{3,7},{4,0},{5,1},{6,2},{7,3},{8,12},{9,13},{10,... | collective-permute-start | bytes 786440 | tf_op jit(solution)/shard_map/ppermute | solution.py:641
  5.4 2.6 collective-permute-start.13
  9.4 6.2 %origin_rows.1 = (f32[2,2,256,256]{3,2,1,0:T(8,128)}, f32[2,2,256,256]{3,2,1,0:T(8,128)}, f32[2,2,256,256]{3,2,1,0:T(8,128)}, f32[2,2,256,256]{3,2,1,0:T(8,128)}) custom-call(s32[4]{0:T(128)} %pad_add_fusion.place_ref, f32[2,2,256,1024]{3,2,1,0:T(8,128)} %bitcast.57, f32[8,2,128]{2,1,0:T(2,128)} %pad_maximum_fusion.4.table_ref.refs_5_.refs_6_.refs_9_, ...), custom_call_target="tpu_custom_call" | custom-call | flops 6000000000 | bytes 18000000 | tf_op jit(solution)/shard_map/origin_rows/pallas_call | solution.py:493
  16.8 10.2 %collective-permute-done.13 = f32[2,256,128]{2,1,0:T(8,128)} collective-permute-done((f32[2,256,128]{2,1,0:T(8,128)}, f32[2,256,128]{2,1,0:T(8,128)}, u32[]{:S(2)}, u32[]{:S(2)}) %collective-permute-start.13) | collective-permute-done | bytes 262176 | tf_op jit(solution)/shard_map/ppermute | solution.py:641
  27.0 2.1 pad_maximum_fusion.2
  29.2 1.4 broadcast_select_fusion.2
  31.5 4.8 %collective-permute-start.1 = (f32[2,256,256]{2,1,0:T(8,128)S(1)}, f32[2,256,256]{2,1,0:T(8,128)S(1)}, u32[]{:S(2)}, u32[]{:S(2)}) collective-permute-start(f32[2,256,256]{2,1,0:T(8,128)S(1)} %get-tuple-element.86), channel_id=1, source_target_pairs={{0,4},{1,5},{2,6},{3,7},{4,0},{5,1},{6,2},{7,3},{8,12},{9,13},{10,... | collective-permute-start | bytes 1572872 | tf_op jit(solution)/shard_map/ppermute | solution.py:641
  38.3 1.5 collective-permute-start.3
  39.8 1.4 broadcast_select_fusion
  44.3 1.9 collective-permute-start.8
  46.2 12.2 %collective-permute-done.1.refs_1_ = f32[2,256,256]{2,1,0:T(8,128)S(1)} collective-permute-done((f32[2,256,256]{2,1,0:T(8,128)S(1)}, f32[2,256,256]{2,1,0:T(8,128)S(1)}, u32[]{:S(2)}, u32[]{:S(2)}) %collective-permute-start.1) | collective-permute-done | bytes 524320 | tf_op jit(solution)/shard_map/ppermute | solution.py:641
  60.3 1.3 constant_dynamic-slice_fusion.1
  63.6 1.1 maximum_select_fusion.3
  64.7 1.5 collective-permute-start.16
  67.5 3.4 %fusion.1 = (f32[8,1,128,256]{3,2,1,0:T(8,128)S(1)}, f32[8,1,128,256]{3,2,1,0:T(8,128)S(1)}, f32[8,1,128,256]{3,2,1,0:T(8,128)S(1)}, f32[8,1,128,256]{3,2,1,0:T(8,128)S(1)}) fusion(f32[256]{0:T(256)S(1)} %get-tuple-element.105, f32[8,128]{1,0:T(8,128)S(1)} %fusion.24, f32[]{:T(128)} %bitcast.17, f32[]{:T(128)S(6)} %convert_element_type.96, ...), kind=kLoop, calls=%fused_computation.11 | loop fusion | flops 20971520 | bytes 4200456 | tf_op jit(solution)/shard_map/mul | solution.py:626
  70.9 1.3 maximum_select_fusion.2
  72.2 18.0 %collective-permute-done.16 = f32[2,2,256,256]{3,2,1,0:T(8,128)} collective-permute-done((f32[2,2,256,256]{3,2,1,0:T(8,128)}, f32[2,2,256,256]{3,2,1,0:T(8,128)}, u32[]{:S(2)}, u32[]{:S(2)}) %collective-permute-start.16) | collective-permute-done | bytes 1048608 | tf_op jit(solution)/shard_map/ppermute | solution.py:641
  90.3 3.1 %maximum_select_fusion.1 = f32[2,2,2,256,256]{4,3,2,1,0:T(8,128)} fusion(f32[1,2,2,256,256]{4,3,2,1,0:T(8,128)} %bitcast.33, f32[1,2,2,256,256]{4,3,2,1,0:T(8,128)S(1)} %maximum_select_fusion.2, pred[]{:T(512)S(6)} %eq.81), kind=kLoop, calls=%fused_computation.5 | loop fusion | flops 1572864 | bytes 4194305 | tf_op jit(solution)/shard_map/jit(_where)/select_n | solution.py:680
  93.3 1.5 collective-permute-start.17
  96.0 2.4 collective-permute-start.9
  101.0 5.3 %move_columns.4 = (f32[2,256,256]{2,1,0:T(8,128)S(1)}, f32[2,256,256]{2,1,0:T(8,128)}, f32[2,256,256]{2,1,0:T(8,128)S(1)}, f32[2,256,256]{2,1,0:T(8,128)}) custom-call(s32[2]{0:T(128)S(1)} %pad_add_fusion.1.swap_ref, f32[2,256,256]{2,1,0:T(8,128)S(1)} %copy-done.5, f32[2,256,256]{2,1,0:T(8,128)S(1)} %copy-done.9, f32[2,256,256]{2,1,0:T(8,128)S(1)} %copy-done.11, ...), custom_call_target="tpu_custom_call" | custom-call | flops 6000000000 | bytes 18000000 | tf_op jit(solution)/shard_map/move_columns/pallas_call | solution.py:554
  107.5 13.4 %collective-permute-done.8.refs_2_ = f32[2,256,256]{2,1,0:T(8,128)} collective-permute-done((f32[2,256,256]{2,1,0:T(8,128)}, f32[2,256,256]{2,1,0:T(8,128)}, u32[]{:S(2)}, u32[]{:S(2)}) %collective-permute-start.8) | collective-permute-done | bytes 524320 | tf_op jit(solution)/shard_map/ppermute | solution.py:641
  120.9 6.0 %move_columns.5 = (f32[2,256,256]{2,1,0:T(8,128)S(1)}, f32[2,256,256]{2,1,0:T(8,128)S(1)}, f32[2,256,256]{2,1,0:T(8,128)S(1)}, f32[2,256,256]{2,1,0:T(8,128)}) custom-call(s32[2]{0:T(128)S(1)} %pad_add_fusion.1.swap_ref, f32[2,256,256]{2,1,0:T(8,128)S(1)} %copy-done.4, f32[2,256,256]{2,1,0:T(8,128)} %collective-permute-done.7.refs_1_, ...), custom_call_target="tpu_custom_call" | custom-call | flops 6000000000 | bytes 18000000 | tf_op jit(solution)/shard_map/move_columns/pallas_call | solution.py:554
  129.4 11.3 %collective-permute-done.4.refs_1_ = f32[2,256,256]{2,1,0:T(8,128)} collective-permute-done((f32[2,256,256]{2,1,0:T(8,128)}, f32[2,256,256]{2,1,0:T(8,128)}, u32[]{:S(2)}, u32[]{:S(2)}) %collective-permute-start.4) | collective-permute-done | bytes 524320 | tf_op jit(solution)/shard_map/ppermute | solution.py:641
  140.7 1.2 slice.61
  142.0 1.2 slice.62
  144.9 4.0 %maximum_select_fusion.refs_4_.refs_5_.refs_8_ = f32[4,2,2,256,256]{4,3,2,1,0:T(8,128)S(1)} fusion(f32[2,2,2,256,256]{4,3,2,1,0:T(8,128)} %collective-permute-done.17, f32[2,2,2,256,256]{4,3,2,1,0:T(8,128)} %maximum_select_fusion.1, pred[]{:T(512)S(6)} %eq.80), kind=kLoop, calls=%fused_computation.2 | loop fusion | flops 3145728 | bytes 8388609 | tf_op jit(solution)/shard_map/jit(_where)/select_n | solution.py:682
  148.9 1.8 collective-permute-start.18
  150.8 4.3 %turn_rows.3 = (f32[2,256,256]{2,1,0:T(8,128)S(1)}, f32[2,256,256]{2,1,0:T(8,128)S(1)}, f32[2,256,256]{2,1,0:T(8,128)S(1)}, f32[2,256,256]{2,1,0:T(8,128)S(1)}) custom-call(f32[1]{0:T(128)} %bitcast.9.scale_ref, f32[2,256,256]{2,1,0:T(8,128)} %get-tuple-element.44.refs_0_, f32[2,256,256]{2,1,0:T(8,128)S(1)} %copy-done.16, ...), custom_call_target="tpu_custom_call" | custom-call | flops 4000000000 | bytes 12000000 | tf_op jit(solution)/shard_map/turn_rows/pallas_call | solution.py:526
  155.3 3.0 %turn_rows.2 = (f32[2,256,256]{2,1,0:T(8,128)S(1)}, f32[2,256,256]{2,1,0:T(8,128)S(1)}, f32[2,256,256]{2,1,0:T(8,128)S(1)}, f32[2,256,256]{2,1,0:T(8,128)S(1)}, f32[2,256,1024]{2,1,0:T(8,128)S(1)}) custom-call(f32[1]{0:T(128)S(6)} %add.698.scale_ref, f32[2,256,256]{2,1,0:T(8,128)S(1)} %copy-done.26, f32[2,256,256]{2,1,0:T(8,128)S(1)} %copy-done.28, ...), custom_call_target="tpu_custom_call" | custom-call | flops 4000000000 | bytes 12000000 | tf_op jit(solution)/shard_map/turn_rows/pallas_call | solution.py:526
  158.8 7.6 %collective-permute-done.18.refs_2_ = f32[2,256,256]{2,1,0:T(8,128)S(1)} collective-permute-done((f32[2,256,256]{2,1,0:T(8,128)S(1)}, f32[2,256,256]{2,1,0:T(8,128)S(1)}, u32[]{:S(2)}, u32[]{:S(2)}) %collective-permute-start.18) | collective-permute-done | bytes 524320 | tf_op jit(solution)/shard_map/ppermute | solution.py:641
  169.3 4.4 %move_columns.7 = (f32[2,256,256]{2,1,0:T(8,128)S(1)}, f32[2,256,256]{2,1,0:T(8,128)S(1)}, f32[2,256,256]{2,1,0:T(8,128)S(1)}, f32[2,256,256]{2,1,0:T(8,128)S(1)}) custom-call(s32[2]{0:T(128)S(1)} %add_add_fusion.swap_ref, f32[2,256,256]{2,1,0:T(8,128)S(1)} %get-tuple-element.64.refs_0_, f32[2,256,256]{2,1,0:T(8,128)S(1)} %get-tuple-element.65.refs_1_, ...), custom_call_target="tpu_custom_call" | custom-call | flops 6000000000 | bytes 18000000 | tf_op jit(solution)/shard_map/move_columns/pallas_call | solution.py:554
  173.9 1.8 collective-permute-start.35
  175.7 4.6 %move_columns.6 = (f32[2,256,256]{2,1,0:T(8,128)S(1)}, f32[2,256,256]{2,1,0:T(8,128)S(1)}, f32[2,256,256]{2,1,0:T(8,128)S(1)}, f32[2,256,256]{2,1,0:T(8,128)S(1)}) custom-call(s32[2]{0:T(128)S(1)} %add_add_fusion.swap_ref, f32[2,256,256]{2,1,0:T(8,128)S(1)} %get-tuple-element.59.refs_0_, f32[2,256,256]{2,1,0:T(8,128)S(1)} %get-tuple-element.60.refs_1_, ...), custom_call_target="tpu_custom_call" | custom-call | flops 6000000000 | bytes 18000000 | tf_op jit(solution)/shard_map/move_columns/pallas_call | solution.py:554
  180.8 1.4 collective-permute-start.34
  182.3 3.4 %image_rows.2 = (f32[256,256]{1,0:T(8,128)S(1)}, f32[256,256]{1,0:T(8,128)S(1)}, f32[256,256]{1,0:T(8,128)S(1)}, f32[256,256]{1,0:T(8,128)S(1)}) custom-call(s32[4]{0:T(128)S(1)} %copy-done.7, f32[1]{0:T(128)} %bitcast.9.scale_ref, f32[2,256,1024]{2,1,0:T(8,128)S(1)} %get-tuple-element.52.refs_0_, f32[2,256,256]{2,1,0:T(8,128)} %collective-permute-done.4.refs_1_, ...), custom_call_target="tpu_custom_call" | custom-call | flops 3000000000 | bytes 9000000 | tf_op jit(solution)/shard_map/image_rows/pallas_call | solution.py:539
  185.7 2.9 %collective-permute-done.33.refs_5_ = f32[2,256,256]{2,1,0:T(8,128)S(1)} collective-permute-done((f32[2,256,256]{2,1,0:T(8,128)S(1)}, f32[2,256,256]{2,1,0:T(8,128)S(1)}, u32[]{:S(2)}, u32[]{:S(2)}) %collective-permute-start.33) | collective-permute-done | bytes 524320 | tf_op jit(solution)/shard_map/ppermute | solution.py:641
  189.3 12.5 %collective-permute-done.35.refs_7_ = f32[2,256,256]{2,1,0:T(8,128)S(1)} collective-permute-done((f32[2,256,256]{2,1,0:T(8,128)S(1)}, f32[2,256,256]{2,1,0:T(8,128)S(1)}, u32[]{:S(2)}, u32[]{:S(2)}) %collective-permute-start.35) | collective-permute-done | bytes 524320 | tf_op jit(solution)/shard_map/ppermute | solution.py:641
  202.5 1.5 collective-permute-start.22
  204.0 15.5 %collective-permute-done.32.refs_4_ = f32[2,256,256]{2,1,0:T(8,128)S(1)} collective-permute-done((f32[2,256,256]{2,1,0:T(8,128)S(1)}, f32[2,256,256]{2,1,0:T(8,128)S(1)}, u32[]{:S(2)}, u32[]{:S(2)}) %collective-permute-start.32) | collective-permute-done | bytes 524320 | tf_op jit(solution)/shard_map/ppermute | solution.py:641
  219.8 10.1 %collective-permute-done.34.refs_6_ = f32[2,256,256]{2,1,0:T(8,128)S(1)} collective-permute-done((f32[2,256,256]{2,1,0:T(8,128)S(1)}, f32[2,256,256]{2,1,0:T(8,128)S(1)}, u32[]{:S(2)}, u32[]{:S(2)}) %collective-permute-start.34) | collective-permute-done | bytes 524320 | tf_op jit(solution)/shard_map/ppermute | solution.py:641
  229.9 3.9 %image_rows.3 = (f32[256,256]{1,0:T(8,128)S(1)}, f32[256,256]{1,0:T(8,128)S(1)}, f32[256,256]{1,0:T(8,128)S(1)}, f32[256,256]{1,0:T(8,128)S(1)}) custom-call(s32[4]{0:T(128)S(1)} %copy-done.7, f32[1]{0:T(128)} %bitcast.9.scale_ref, f32[2,256,256]{2,1,0:T(8,128)S(1)} %get-tuple-element.63.refs_0_, f32[2,256,256]{2,1,0:T(8,128)S(1)} %get-tuple-element.68.refs_1_, ...), custom_call_target="tpu_custom_call" | custom-call | flops 3000000000 | bytes 9000000 | tf_op jit(solution)/shard_map/image_rows/pallas_call | solution.py:539
  234.5 2.5 collective-permute-start.37
  237.0 1.5 collective-permute-start.38
  238.5 1.7 collective-permute-start.39
  240.3 16.4 %collective-permute-done.37 = f32[256,256]{1,0:T(8,128)S(1)} collective-permute-done((f32[256,256]{1,0:T(8,128)S(1)}, f32[256,256]{1,0:T(8,128)S(1)}, u32[]{:S(2)}, u32[]{:S(2)}) %collective-permute-start.37) | collective-permute-done | bytes 262176 | tf_op jit(solution)/shard_map/ppermute | solution.py:641
  256.7 6.5 %collective-permute-done.39 = f32[256,256]{1,0:T(8,128)S(1)} collective-permute-done((f32[256,256]{1,0:T(8,128)S(1)}, f32[256,256]{1,0:T(8,128)S(1)}, u32[]{:S(2)}, u32[]{:S(2)}) %collective-permute-start.39) | collective-permute-done | bytes 262176 | tf_op jit(solution)/shard_map/ppermute | solution.py:641
  (166 shorter events, 27.5 us)
Async XLA Ops:
  2.3 14.5 %collective-permute-start.12 = (f32[2,256,128]{2,1,0:T(8,128)}, f32[2,256,128]{2,1,0:T(8,128)}, u32[]{:S(2)}, u32[]{:S(2)}) collective-permute-start(f32[2,256,128]{2,1,0:T(8,128)} %constant_dynamic-slice_fusion.2), channel_id=1, source_target_pairs={{0,4},{1,5},{2,6},{3,7},{4,0},{5,1},{6,2},{7,3},{8,12},{9,13},{10,... | collective-permute-start | bytes 786440 | tf_op jit(solution)/shard_map/ppermute | solution.py:641
  5.4 21.7 %collective-permute-start.13 = (f32[2,256,128]{2,1,0:T(8,128)}, f32[2,256,128]{2,1,0:T(8,128)}, u32[]{:S(2)}, u32[]{:S(2)}) collective-permute-start(f32[2,256,128]{2,1,0:T(8,128)} %constant_dynamic-slice_fusion.2), channel_id=1, source_target_pairs={{0,8},{1,9},{2,10},{3,11},{4,12},{5,13},{6,14},{7,15},{8,0},{9,1},... | collective-permute-start | bytes 786440 | tf_op jit(solution)/shard_map/ppermute | solution.py:641
  7.9 19.1 %collective-permute-start.14 = (f32[2,256,128]{2,1,0:T(8,128)}, f32[2,256,128]{2,1,0:T(8,128)}, u32[]{:S(2)}, u32[]{:S(2)}) collective-permute-start(f32[2,256,128]{2,1,0:T(8,128)} %constant_dynamic-slice_fusion.2), channel_id=1, source_target_pairs={{0,12},{1,13},{2,14},{3,15},{4,8},{5,9},{6,10},{7,11},{8,4},{9,5},... | collective-permute-start | bytes 786440 | tf_op jit(solution)/shard_map/ppermute | solution.py:641
  15.6 13.6 %copy-start.32 = (f32[2,2,256,256]{3,2,1,0:T(8,128)S(1)}, f32[2,2,256,256]{3,2,1,0:T(8,128)}, u32[]{:S(2)}) copy-start(f32[2,2,256,256]{3,2,1,0:T(8,128)} %get-tuple-element.42) | copy-start | bytes 3145732
  15.6 13.6 %collective-permute-start = (f32[2,2,256,256]{3,2,1,0:T(8,128)}, f32[2,2,256,256]{3,2,1,0:T(8,128)}, u32[]{:S(2)}, u32[]{:S(2)}) collective-permute-start(f32[2,2,256,256]{3,2,1,0:T(8,128)} %get-tuple-element.43), channel_id=1, source_target_pairs={{0,1},{1,0},{2,3},{3,2},{4,5},{5,4},{6,7},{7,6},{8,9},{9,8},{10,11... | collective-permute-start | bytes 3145736 | tf_op jit(solution)/shard_map/ppermute | solution.py:641
  15.6 24.2 %collective-permute-start.6 = (f32[2,2,256,256]{3,2,1,0:T(8,128)}, f32[2,2,256,256]{3,2,1,0:T(8,128)}, u32[]{:S(2)}, u32[]{:S(2)}) collective-permute-start(f32[2,2,256,256]{3,2,1,0:T(8,128)} %get-tuple-element.47), channel_id=1, source_target_pairs={{0,1},{1,0},{2,3},{3,2},{4,5},{5,4},{6,7},{7,6},{8,9},{9,8},{10,11... | collective-permute-start | bytes 3145736 | tf_op jit(solution)/shard_map/ppermute | solution.py:641
  30.6 9.2 %copy-start.31 = (f32[2,2,256,256]{3,2,1,0:T(8,128)S(1)}, f32[2,2,256,256]{3,2,1,0:T(8,128)}, u32[]{:S(2)}) copy-start(f32[2,2,256,256]{3,2,1,0:T(8,128)} %get-tuple-element.48) | copy-start | bytes 3145732
  31.5 27.0 %collective-permute-start.1 = (f32[2,256,256]{2,1,0:T(8,128)S(1)}, f32[2,256,256]{2,1,0:T(8,128)S(1)}, u32[]{:S(2)}, u32[]{:S(2)}) collective-permute-start(f32[2,256,256]{2,1,0:T(8,128)S(1)} %get-tuple-element.86), channel_id=1, source_target_pairs={{0,4},{1,5},{2,6},{3,7},{4,0},{5,1},{6,2},{7,3},{8,12},{9,13},{10,... | collective-permute-start | bytes 1572872 | tf_op jit(solution)/shard_map/ppermute | solution.py:641
  37.3 57.9 %collective-permute-start.2 = (f32[2,256,256]{2,1,0:T(8,128)}, f32[2,256,256]{2,1,0:T(8,128)S(1)}, u32[]{:S(2)}, u32[]{:S(2)}) collective-permute-start(f32[2,256,256]{2,1,0:T(8,128)} %get-tuple-element.87), channel_id=1, source_target_pairs={{0,8},{1,9},{2,10},{3,11},{4,12},{5,13},{6,14},{7,15},{8,0},{9,1},... | collective-permute-start | bytes 1572872 | tf_op jit(solution)/shard_map/ppermute | solution.py:641
  38.3 60.1 %collective-permute-start.3 = (f32[2,256,256]{2,1,0:T(8,128)}, f32[2,256,256]{2,1,0:T(8,128)S(1)}, u32[]{:S(2)}, u32[]{:S(2)}) collective-permute-start(f32[2,256,256]{2,1,0:T(8,128)} %get-tuple-element.85), channel_id=1, source_target_pairs={{0,12},{1,13},{2,14},{3,15},{4,8},{5,9},{6,10},{7,11},{8,4},{9,5},... | collective-permute-start | bytes 1572872 | tf_op jit(solution)/shard_map/ppermute | solution.py:641
  42.3 65.1 %collective-permute-start.7 = (f32[2,256,256]{2,1,0:T(8,128)}, f32[2,256,256]{2,1,0:T(8,128)}, u32[]{:S(2)}, u32[]{:S(2)}) collective-permute-start(f32[2,256,256]{2,1,0:T(8,128)} %get-tuple-element.90), channel_id=1, source_target_pairs={{0,4},{1,5},{2,6},{3,7},{4,0},{5,1},{6,2},{7,3},{8,12},{9,13},{10,... | collective-permute-start | bytes 1572872 | tf_op jit(solution)/shard_map/ppermute | solution.py:641
  43.3 18.5 %copy-start.29 = (s32[4]{0:T(128)S(1)}, s32[4]{0:T(128)}, u32[]{:S(2)}) copy-start(s32[4]{0:T(128)} %constant.231.clone) | copy-start | bytes 52
  44.3 76.6 %collective-permute-start.8 = (f32[2,256,256]{2,1,0:T(8,128)}, f32[2,256,256]{2,1,0:T(8,128)}, u32[]{:S(2)}, u32[]{:S(2)}) collective-permute-start(f32[2,256,256]{2,1,0:T(8,128)} %get-tuple-element.91), channel_id=1, source_target_pairs={{0,8},{1,9},{2,10},{3,11},{4,12},{5,13},{6,14},{7,15},{8,0},{9,1},... | collective-permute-start | bytes 1572872 | tf_op jit(solution)/shard_map/ppermute | solution.py:641
  61.6 2.0 collective-permute-start.15
  64.7 25.5 %collective-permute-start.16 = (f32[2,2,256,256]{3,2,1,0:T(8,128)}, f32[2,2,256,256]{3,2,1,0:T(8,128)}, u32[]{:S(2)}, u32[]{:S(2)}) collective-permute-start(f32[2,2,256,256]{3,2,1,0:T(8,128)} %maximum_select_fusion.3), channel_id=1, source_target_pairs={{0,2},{1,3},{2,0},{3,1},{4,6},{5,7},{6,4},{7,5},{8,10},{9,11},{10,... | collective-permute-start | bytes 3145736 | tf_op jit(solution)/shard_map/ppermute | solution.py:641
  93.3 51.1 %collective-permute-start.17 = (f32[2,2,2,256,256]{4,3,2,1,0:T(8,128)}, f32[2,2,2,256,256]{4,3,2,1,0:T(8,128)}, u32[]{:S(2)}, u32[]{:S(2)}) collective-permute-start(f32[2,2,2,256,256]{4,3,2,1,0:T(8,128)} %maximum_select_fusion.1), channel_id=1, source_target_pairs={{0,16},{1,17},{2,18},{3,19},{4,20},{5,21},{6,22},{7,23},{8,24},{9,... | collective-permute-start | bytes 6291464 | tf_op jit(solution)/shard_map/ppermute | solution.py:641
  96.0 24.9 %collective-permute-start.9 = (f32[2,256,256]{2,1,0:T(8,128)S(1)}, f32[2,256,256]{2,1,0:T(8,128)S(1)}, u32[]{:S(2)}, u32[]{:S(2)}) collective-permute-start(f32[2,256,256]{2,1,0:T(8,128)S(1)} %copy-done.33), channel_id=1, source_target_pairs={{0,12},{1,13},{2,14},{3,15},{4,8},{5,9},{6,10},{7,11},{8,4},{9,5},... | collective-permute-start | bytes 1572872 | tf_op jit(solution)/shard_map/ppermute | solution.py:641
  106.4 35.5 %collective-permute-start.5 = (f32[2,256,256]{2,1,0:T(8,128)}, f32[2,256,256]{2,1,0:T(8,128)}, u32[]{:S(2)}, u32[]{:S(2)}) collective-permute-start(f32[2,256,256]{2,1,0:T(8,128)} %get-tuple-element.45), channel_id=1, source_target_pairs={{0,5},{1,4},{2,7},{3,6},{4,1},{5,0},{6,3},{7,2},{8,13},{9,12},{10,... | collective-permute-start | bytes 1572872 | tf_op jit(solution)/shard_map/ppermute | solution.py:641
  107.2 13.7 %copy-start.4 = (f32[2,256,256]{2,1,0:T(8,128)S(1)}, f32[2,256,256]{2,1,0:T(8,128)}, u32[]{:S(2)}) copy-start(f32[2,256,256]{2,1,0:T(8,128)} %get-tuple-element.92.refs_0_) | copy-start | bytes 1572868
  107.4 19.6 %copy-start.2 = (f32[8,2,128,256]{3,2,1,0:T(8,128)}, f32[8,2,128,256]{3,2,1,0:T(8,128)S(1)}, u32[]{:S(2)}) copy-start(f32[8,2,128,256]{3,2,1,0:T(8,128)S(1)} %pad_maximum_fusion.1.refs_7_) | copy-start | bytes 6291460
  107.4 41.5 %collective-permute-start.24 = (f32[2,256,256]{2,1,0:T(8,128)}, f32[2,256,256]{2,1,0:T(8,128)}, u32[]{:S(2)}, u32[]{:S(2)}) collective-permute-start(f32[2,256,256]{2,1,0:T(8,128)} %get-tuple-element.45), channel_id=1, source_target_pairs={{0,1},{1,0},{2,3},{3,2},{4,5},{5,4},{6,7},{7,6},{8,9},{9,8},{10,11... | collective-permute-start | bytes 1572872 | tf_op jit(solution)/shard_map/ppermute | solution.py:641
  120.9 19.8 %collective-permute-start.4 = (f32[2,256,256]{2,1,0:T(8,128)}, f32[2,256,256]{2,1,0:T(8,128)}, u32[]{:S(2)}, u32[]{:S(2)}) collective-permute-start(f32[2,256,256]{2,1,0:T(8,128)} %get-tuple-element.44.refs_0_), channel_id=1, source_target_pairs={{0,4},{1,5},{2,6},{3,7},{4,0},{5,1},{6,2},{7,3},{8,12},{9,13},{10,... | collective-permute-start | bytes 1572872 | tf_op jit(solution)/shard_map/ppermute | solution.py:641
  129.4 21.4 %collective-permute-start.25 = (f32[2,256,256]{2,1,0:T(8,128)}, f32[2,256,256]{2,1,0:T(8,128)}, u32[]{:S(2)}, u32[]{:S(2)}) collective-permute-start(f32[2,256,256]{2,1,0:T(8,128)} %get-tuple-element.54), channel_id=1, source_target_pairs={{0,1},{1,0},{2,3},{3,2},{4,5},{5,4},{6,7},{7,6},{8,9},{9,8},{10,11... | collective-permute-start | bytes 1572872 | tf_op jit(solution)/shard_map/ppermute | solution.py:641
  140.7 26.2 %collective-permute-start.19 = (f32[2,256,256]{2,1,0:T(8,128)}, f32[2,256,256]{2,1,0:T(8,128)S(1)}, u32[]{:S(2)}, u32[]{:S(2)}) collective-permute-start(f32[2,256,256]{2,1,0:T(8,128)} %get-tuple-element.54), channel_id=1, source_target_pairs={{0,5},{1,4},{2,7},{3,6},{4,1},{5,0},{6,3},{7,2},{8,13},{9,12},{10,... | collective-permute-start | bytes 1572872 | tf_op jit(solution)/shard_map/ppermute | solution.py:641
  141.9 13.4 %collective-permute-start.10 = (f32[2,256,256]{2,1,0:T(8,128)}, f32[2,256,256]{2,1,0:T(8,128)S(1)}, u32[]{:S(2)}, u32[]{:S(2)}) collective-permute-start(f32[2,256,256]{2,1,0:T(8,128)} %copy-done.14), channel_id=1, source_target_pairs={{0,1},{1,0},{2,3},{3,2},{4,5},{5,4},{6,7},{7,6},{8,9},{9,8},{10,11... | collective-permute-start | bytes 1572872 | tf_op jit(solution)/shard_map/ppermute | solution.py:641
  144.4 10.8 %collective-permute-start.11 = (f32[2,256,256]{2,1,0:T(8,128)}, f32[2,256,256]{2,1,0:T(8,128)S(1)}, u32[]{:S(2)}, u32[]{:S(2)}) collective-permute-start(f32[2,256,256]{2,1,0:T(8,128)} %copy-done.17), channel_id=1, source_target_pairs={{0,1},{1,0},{2,3},{3,2},{4,5},{5,4},{6,7},{7,6},{8,9},{9,8},{10,11... | collective-permute-start | bytes 1572872 | tf_op jit(solution)/shard_map/ppermute | solution.py:641
  148.9 17.4 %collective-permute-start.18 = (f32[2,256,256]{2,1,0:T(8,128)S(1)}, f32[2,256,256]{2,1,0:T(8,128)S(1)}, u32[]{:S(2)}, u32[]{:S(2)}) collective-permute-start(f32[2,256,256]{2,1,0:T(8,128)S(1)} %copy-done.16), channel_id=1, source_target_pairs={{0,4},{1,5},{2,6},{3,7},{4,0},{5,1},{6,2},{7,3},{8,12},{9,13},{10,... | collective-permute-start | bytes 1572872 | tf_op jit(solution)/shard_map/ppermute | solution.py:641
  155.1 14.2 %collective-permute-start.29 = (f32[2,256,256]{2,1,0:T(8,128)S(1)}, f32[2,256,256]{2,1,0:T(8,128)S(1)}, u32[]{:S(2)}, u32[]{:S(2)}) collective-permute-start(f32[2,256,256]{2,1,0:T(8,128)S(1)} %get-tuple-element.67), channel_id=1, source_target_pairs={{0,1},{1,0},{2,3},{3,2},{4,5},{5,4},{6,7},{7,6},{8,9},{9,8},{10,11... | collective-permute-start | bytes 1572872 | tf_op jit(solution)/shard_map/ppermute | solution.py:641
  155.3 14.0 %copy-start.3 = (f32[8,2,128,256]{3,2,1,0:T(8,128)S(1)}, f32[8,2,128,256]{3,2,1,0:T(8,128)}, u32[]{:S(2)}) copy-start(f32[8,2,128,256]{3,2,1,0:T(8,128)} %copy-done.2) | copy-start | bytes 6291460
  155.3 14.0 %copy-start.24 = (f32[2,128,128]{2,1,0:T(8,128)S(1)}, f32[2,128,128]{2,1,0:T(8,128)}, u32[]{:S(2)}) copy-start(f32[2,128,128]{2,1,0:T(8,128)} %constant.230.clone.refs_6_) | copy-start | bytes 393220
  158.4 10.9 %collective-permute-start.28 = (f32[2,256,256]{2,1,0:T(8,128)S(1)}, f32[2,256,256]{2,1,0:T(8,128)S(1)}, u32[]{:S(2)}, u32[]{:S(2)}) collective-permute-start(f32[2,256,256]{2,1,0:T(8,128)S(1)} %get-tuple-element.66), channel_id=1, source_target_pairs={{0,1},{1,0},{2,3},{3,2},{4,5},{5,4},{6,7},{7,6},{8,9},{9,8},{10,11... | collective-permute-start | bytes 1572872 | tf_op jit(solution)/shard_map/ppermute | solution.py:641
  168.8 6.9 %collective-permute-start.27 = (f32[2,256,256]{2,1,0:T(8,128)S(1)}, f32[2,256,256]{2,1,0:T(8,128)S(1)}, u32[]{:S(2)}, u32[]{:S(2)}) collective-permute-start(f32[2,256,256]{2,1,0:T(8,128)S(1)} %get-tuple-element.62), channel_id=1, source_target_pairs={{0,1},{1,0},{2,3},{3,2},{4,5},{5,4},{6,7},{7,6},{8,9},{9,8},{10,11... | collective-permute-start | bytes 1572872 | tf_op jit(solution)/shard_map/ppermute | solution.py:641
  168.8 6.9 %collective-permute-start.26 = (f32[2,256,256]{2,1,0:T(8,128)S(1)}, f32[2,256,256]{2,1,0:T(8,128)S(1)}, u32[]{:S(2)}, u32[]{:S(2)}) collective-permute-start(f32[2,256,256]{2,1,0:T(8,128)S(1)} %get-tuple-element.61), channel_id=1, source_target_pairs={{0,1},{1,0},{2,3},{3,2},{4,5},{5,4},{6,7},{7,6},{8,9},{9,8},{10,11... | collective-permute-start | bytes 1572872 | tf_op jit(solution)/shard_map/ppermute | solution.py:641
  173.7 7.1 %collective-permute-start.31 = (f32[2,256,256]{2,1,0:T(8,128)S(1)}, f32[2,256,256]{2,1,0:T(8,128)S(1)}, u32[]{:S(2)}, u32[]{:S(2)}) collective-permute-start(f32[2,256,256]{2,1,0:T(8,128)S(1)} %get-tuple-element.70), channel_id=1, source_target_pairs={{0,1},{1,0},{2,3},{3,2},{4,5},{5,4},{6,7},{7,6},{8,9},{9,8},{10,11... | collective-permute-start | bytes 1572872 | tf_op jit(solution)/shard_map/ppermute | solution.py:641
  173.9 14.7 %collective-permute-start.33 = (f32[2,256,256]{2,1,0:T(8,128)S(1)}, f32[2,256,256]{2,1,0:T(8,128)S(1)}, u32[]{:S(2)}, u32[]{:S(2)}) collective-permute-start(f32[2,256,256]{2,1,0:T(8,128)S(1)} %get-tuple-element.72), channel_id=1, source_target_pairs={{0,4},{1,5},{2,6},{3,7},{4,0},{5,1},{6,2},{7,3},{8,12},{9,13},{10,... | collective-permute-start | bytes 1572872 | tf_op jit(solution)/shard_map/ppermute | solution.py:641
  173.9 27.9 %collective-permute-start.35 = (f32[2,256,256]{2,1,0:T(8,128)S(1)}, f32[2,256,256]{2,1,0:T(8,128)S(1)}, u32[]{:S(2)}, u32[]{:S(2)}) collective-permute-start(f32[2,256,256]{2,1,0:T(8,128)S(1)} %get-tuple-element.74), channel_id=1, source_target_pairs={{0,5},{1,4},{2,7},{3,6},{4,1},{5,0},{6,3},{7,2},{8,13},{9,12},{10,... | collective-permute-start | bytes 1572872 | tf_op jit(solution)/shard_map/ppermute | solution.py:641
  180.3 22.2 %collective-permute-start.30 = (f32[2,256,256]{2,1,0:T(8,128)S(1)}, f32[2,256,256]{2,1,0:T(8,128)S(1)}, u32[]{:S(2)}, u32[]{:S(2)}) collective-permute-start(f32[2,256,256]{2,1,0:T(8,128)S(1)} %get-tuple-element.69), channel_id=1, source_target_pairs={{0,1},{1,0},{2,3},{3,2},{4,5},{5,4},{6,7},{7,6},{8,9},{9,8},{10,11... | collective-permute-start | bytes 1572872 | tf_op jit(solution)/shard_map/ppermute | solution.py:641
  180.7 38.8 %collective-permute-start.32 = (f32[2,256,256]{2,1,0:T(8,128)S(1)}, f32[2,256,256]{2,1,0:T(8,128)S(1)}, u32[]{:S(2)}, u32[]{:S(2)}) collective-permute-start(f32[2,256,256]{2,1,0:T(8,128)S(1)} %get-tuple-element.71), channel_id=1, source_target_pairs={{0,4},{1,5},{2,6},{3,7},{4,0},{5,1},{6,2},{7,3},{8,12},{9,13},{10,... | collective-permute-start | bytes 1572872 | tf_op jit(solution)/shard_map/ppermute | solution.py:641
  180.8 49.1 %collective-permute-start.34 = (f32[2,256,256]{2,1,0:T(8,128)S(1)}, f32[2,256,256]{2,1,0:T(8,128)S(1)}, u32[]{:S(2)}, u32[]{:S(2)}) collective-permute-start(f32[2,256,256]{2,1,0:T(8,128)S(1)} %get-tuple-element.73), channel_id=1, source_target_pairs={{0,5},{1,4},{2,7},{3,6},{4,1},{5,0},{6,3},{7,2},{8,13},{9,12},{10,... | collective-permute-start | bytes 1572872 | tf_op jit(solution)/shard_map/ppermute | solution.py:641
  188.6 45.9 %collective-permute-start.20 = (f32[256,256]{1,0:T(8,128)S(1)}, f32[256,256]{1,0:T(8,128)S(1)}, u32[]{:S(2)}, u32[]{:S(2)}) collective-permute-start(f32[256,256]{1,0:T(8,128)S(1)} %get-tuple-element.55), channel_id=1, source_target_pairs={{0,0},{1,8},{2,2},{3,10},{4,4},{5,12},{6,6},{7,14},{8,1},{9,9},{10... | collective-permute-start | bytes 786440 | tf_op jit(solution)/shard_map/ppermute | solution.py:641
  201.7 35.3 %collective-permute-start.21 = (f32[256,256]{1,0:T(8,128)S(1)}, f32[256,256]{1,0:T(8,128)S(1)}, u32[]{:S(2)}, u32[]{:S(2)}) collective-permute-start(f32[256,256]{1,0:T(8,128)S(1)} %get-tuple-element.56), channel_id=1, source_target_pairs={{0,1},{1,9},{2,3},{3,11},{4,5},{5,13},{6,7},{7,15},{8,0},{9,8},{10... | collective-permute-start | bytes 786440 | tf_op jit(solution)/shard_map/ppermute | solution.py:641
  202.5 36.0 %collective-permute-start.22 = (f32[256,256]{1,0:T(8,128)S(1)}, f32[256,256]{1,0:T(8,128)S(1)}, u32[]{:S(2)}, u32[]{:S(2)}) collective-permute-start(f32[256,256]{1,0:T(8,128)S(1)} %get-tuple-element.57), channel_id=1, source_target_pairs={{0,2},{1,10},{2,0},{3,8},{4,6},{5,14},{6,4},{7,12},{8,3},{9,11},{1... | collective-permute-start | bytes 786440 | tf_op jit(solution)/shard_map/ppermute | solution.py:641
  219.5 20.7 %collective-permute-start.23 = (f32[256,256]{1,0:T(8,128)S(1)}, f32[256,256]{1,0:T(8,128)S(1)}, u32[]{:S(2)}, u32[]{:S(2)}) collective-permute-start(f32[256,256]{1,0:T(8,128)S(1)} %get-tuple-element.58), channel_id=1, source_target_pairs={{0,3},{1,11},{2,1},{3,9},{4,7},{5,15},{6,5},{7,13},{8,2},{9,10},{1... | collective-permute-start | bytes 786440 | tf_op jit(solution)/shard_map/ppermute | solution.py:641
  229.9 34.2 %copy-start.1 = (f32[2,256,1024]{2,1,0:T(8,128)S(1)}, f32[2,256,1024]{2,1,0:T(8,128)}, u32[]{:S(2)}) copy-start(f32[2,256,1024]{2,1,0:T(8,128)} %param.15) | copy-start | bytes 6291460
  233.8 6.4 %collective-permute-start.36 = (f32[256,256]{1,0:T(8,128)S(1)}, f32[256,256]{1,0:T(8,128)S(1)}, u32[]{:S(2)}, u32[]{:S(2)}) collective-permute-start(f32[256,256]{1,0:T(8,128)S(1)} %get-tuple-element.75), channel_id=1, source_target_pairs={{0,0},{1,8},{2,2},{3,10},{4,4},{5,12},{6,6},{7,14},{8,1},{9,9},{10... | collective-permute-start | bytes 786440 | tf_op jit(solution)/shard_map/ppermute | solution.py:641
  234.5 22.1 %collective-permute-start.37 = (f32[256,256]{1,0:T(8,128)S(1)}, f32[256,256]{1,0:T(8,128)S(1)}, u32[]{:S(2)}, u32[]{:S(2)}) collective-permute-start(f32[256,256]{1,0:T(8,128)S(1)} %get-tuple-element.76), channel_id=1, source_target_pairs={{0,1},{1,9},{2,3},{3,11},{4,5},{5,13},{6,7},{7,15},{8,0},{9,8},{10... | collective-permute-start | bytes 786440 | tf_op jit(solution)/shard_map/ppermute | solution.py:641
  237.0 19.7 %collective-permute-start.38 = (f32[256,256]{1,0:T(8,128)S(1)}, f32[256,256]{1,0:T(8,128)S(1)}, u32[]{:S(2)}, u32[]{:S(2)}) collective-permute-start(f32[256,256]{1,0:T(8,128)S(1)} %get-tuple-element.77), channel_id=1, source_target_pairs={{0,2},{1,10},{2,0},{3,8},{4,6},{5,14},{6,4},{7,12},{8,3},{9,11},{1... | collective-permute-start | bytes 786440 | tf_op jit(solution)/shard_map/ppermute | solution.py:641
  238.5 24.7 %collective-permute-start.39 = (f32[256,256]{1,0:T(8,128)S(1)}, f32[256,256]{1,0:T(8,128)S(1)}, u32[]{:S(2)}, u32[]{:S(2)}) collective-permute-start(f32[256,256]{1,0:T(8,128)S(1)} %get-tuple-element.78), channel_id=1, source_target_pairs={{0,3},{1,11},{2,1},{3,9},{4,7},{5,15},{6,5},{7,13},{8,2},{9,10},{1... | collective-permute-start | bytes 786440 | tf_op jit(solution)/shard_map/ppermute | solution.py:641
  (27 other events, 96.4 us)

commit v4 on v3

--- a/solution.py
+++ b/solution.py
@@ -511,7 +511,7 @@
         ),
         out_shape=[out] * 4,
         compiler_params=pltpu.CompilerParams(
-            vmem_limit_bytes=60 * 1024 * 1024, dimension_semantics=("arbitrary",)
+            vmem_limit_bytes=32 * 1024 * 1024, dimension_semantics=("arbitrary",)
         ),
         cost_estimate=estimate(6),
         name="origin_rows",
@@ -741,7 +741,7 @@
                 [turned[0][k], turned[1][k], to_core(turned[0][2 + k]), to_core(turned[1][2 + k])]
                 for k in range(2)
             ]
-            hold = zero_after(*partner[1])
+            hold = zero_after(partner[1][0])
             order_in, table_in = order, table_order
             own = [turned[0][4]]
         terms = image_rows(

time: 265 us -> 260 us (0.981)
  waiting for transfers between devices: 138 us -> 121 us
  starting transfers between devices: 38.8 us -> 52.8 us
  other arithmetic: 21.2 us -> 17.3 us
    ppermute x40, waiting for transfers between devices: 138 us -> 121 us  [send(): return lax.ppermute(array, axes, route(sizes, target))]
    ppermute x40, starting transfers between devices: 38.8 us -> 52.8 us  [send(): return lax.ppermute(array, axes, route(sizes, target))]
    unnamed x70 -> x64, local copies, waits for them, and re-layouts: 8.38 us -> 12.2 us
  transfers between devices with their start and end apart: 40 -> 40, of which waited for: 14 -> 12; matrix products, arithmetic and copies ran while one was open for 12% -> 10% of each run, Pallas kernels for 16% -> 16%
where the time goes in v4:
time: 260 us; the launch traced here: 259 us
  waiting for transfers between devices  121 us (47%)
  starting transfers between devices  52.8 us (20%)
  Pallas kernels  40.7 us (16%)
  local copies, waits for them, and re-layouts  23.2 us (9%)
  other arithmetic  17.3 us (7%)
  between operations  3.89 us (1%)
    ppermute x40, waiting for transfers between devices, send(): return lax.ppermute(array, axes, route(sizes, target))  121 us
    ppermute x40, starting transfers between devices, send(): return lax.ppermute(array, axes, route(sizes, target))  52.8 us
    pallas_call x4, Pallas kernels, move_columns(): pl.pallas_call(x_kernel, in_specs=[smem] + [vmem] * (x_radix + 8), out_sp...  21.2 us
    unnamed x64, local copies, waits for them, and re-layouts  12.2 us
    pallas_call x2, Pallas kernels, turn_rows(): pl.pallas_call(functools.partial(turn_kernel, keeps_field, at), in_specs=...  7.51 us
    pallas_call x2, Pallas kernels, image_rows(): pl.pallas_call(functools.partial(image_kernel, len(own) == 1, at), in_spe...  7.4 us
  transfers between devices with their start and end apart: 40, of which 12 were waited for; matrix products, arithmetic and copies ran while one was open for 10% of the time, Pallas kernels for 16%

profile of v4, /device:TPU:0, one launch (start us, length us, event | category | flops | bytes accessed | tf_op | source)
XLA Modules:
  0.0 259.1 jit_solution(11829985269919379267)
XLA Ops:
  0.0 1.6 copy-done
  2.3 3.0 %collective-permute-start.12 = (f32[2,256,128]{2,1,0:T(8,128)}, f32[2,256,128]{2,1,0:T(8,128)}, u32[]{:S(2)}, u32[]{:S(2)}) collective-permute-start(f32[2,256,128]{2,1,0:T(8,128)} %constant_dynamic-slice_fusion.2), channel_id=1, source_target_pairs={{0,4},{1,5},{2,6},{3,7},{4,0},{5,1},{6,2},{7,3},{8,12},{9,13},{10,... | collective-permute-start | bytes 786440 | tf_op jit(solution)/shard_map/ppermute | solution.py:641
  5.4 2.6 collective-permute-start.13
  8.3 2.2 copy-done.8
  12.3 4.6 %origin_rows.1 = (f32[2,2,256,256]{3,2,1,0:T(8,128)S(1)}, f32[2,2,256,256]{3,2,1,0:T(8,128)S(1)}, f32[2,2,256,256]{3,2,1,0:T(8,128)}, f32[2,2,256,256]{3,2,1,0:T(8,128)}) custom-call(s32[4]{0:T(128)S(1)} %pad_add_fusion.place_ref, f32[2,2,256,1024]{3,2,1,0:T(8,128)S(1)} %bitcast.54, f32[8,2,128]{2,1,0:T(2,128)S(1)} %pad_maximum_fusion.4.table_ref.refs_5_.refs_6_.refs_9_, ...), custom_call_target="tpu_custom_call" | custom-call | flops 6000000000 | bytes 18000000 | tf_op jit(solution)/shard_map/origin_rows/pallas_call | solution.py:493
  18.6 8.4 %collective-permute-done.13 = f32[2,256,128]{2,1,0:T(8,128)} collective-permute-done((f32[2,256,128]{2,1,0:T(8,128)}, f32[2,256,128]{2,1,0:T(8,128)}, u32[]{:S(2)}, u32[]{:S(2)}) %collective-permute-start.13) | collective-permute-done | bytes 262176 | tf_op jit(solution)/shard_map/ppermute | solution.py:641
  27.0 2.2 pad_maximum_fusion.2
  29.2 1.4 broadcast_select_fusion.2
  31.5 4.8 %collective-permute-start.1 = (f32[2,256,256]{2,1,0:T(8,128)S(1)}, f32[2,256,256]{2,1,0:T(8,128)S(1)}, u32[]{:S(2)}, u32[]{:S(2)}) collective-permute-start(f32[2,256,256]{2,1,0:T(8,128)S(1)} %get-tuple-element.86), channel_id=1, source_target_pairs={{0,4},{1,5},{2,6},{3,7},{4,0},{5,1},{6,2},{7,3},{8,12},{9,13},{10,... | collective-permute-start | bytes 1572872 | tf_op jit(solution)/shard_map/ppermute | solution.py:641
  36.3 1.0 slice_bitcast_fusion.5
  38.3 1.5 collective-permute-start.3
  39.8 1.5 broadcast_select_fusion
  41.3 1.1 slice_bitcast_fusion
  43.4 1.0 slice_bitcast_fusion.1
  44.4 1.9 collective-permute-start.8
  46.3 12.2 %collective-permute-done.1.refs_1_ = f32[2,256,256]{2,1,0:T(8,128)S(1)} collective-permute-done((f32[2,256,256]{2,1,0:T(8,128)S(1)}, f32[2,256,256]{2,1,0:T(8,128)S(1)}, u32[]{:S(2)}, u32[]{:S(2)}) %collective-permute-start.1) | collective-permute-done | bytes 524320 | tf_op jit(solution)/shard_map/ppermute | solution.py:641
  62.7 1.0 maximum_select_fusion.3
  63.8 1.5 collective-permute-start.16
  66.7 3.4 %fusion.1 = (f32[8,1,128,256]{3,2,1,0:T(8,128)S(1)}, f32[8,1,128,256]{3,2,1,0:T(8,128)S(1)}, f32[8,1,128,256]{3,2,1,0:T(8,128)S(1)}, f32[8,1,128,256]{3,2,1,0:T(8,128)S(1)}) fusion(f32[256]{0:T(256)S(1)} %get-tuple-element.105, f32[8,128]{1,0:T(8,128)S(1)} %fusion.24, f32[]{:T(128)} %bitcast.17, f32[]{:T(128)S(6)} %convert_element_type.96, ...), kind=kLoop, calls=%fused_computation.11 | loop fusion | flops 20971520 | bytes 4200456 | tf_op jit(solution)/shard_map/mul | solution.py:626
  70.2 19.0 %collective-permute-done.16 = f32[2,2,256,256]{3,2,1,0:T(8,128)S(1)} collective-permute-done((f32[2,2,256,256]{3,2,1,0:T(8,128)}, f32[2,2,256,256]{3,2,1,0:T(8,128)S(1)}, u32[]{:S(2)}, u32[]{:S(2)}) %collective-permute-start.16) | collective-permute-done | bytes 1048608 | tf_op jit(solution)/shard_map/ppermute | solution.py:641
  89.2 1.5 maximum_select_fusion.1
  90.7 1.5 collective-permute-start.17
  93.4 2.4 collective-permute-start.9
  96.5 6.0 %move_columns.4 = (f32[2,256,256]{2,1,0:T(8,128)S(1)}, f32[2,256,256]{2,1,0:T(8,128)}, f32[2,256,256]{2,1,0:T(8,128)S(1)}, f32[2,256,256]{2,1,0:T(8,128)}) custom-call(s32[2]{0:T(128)S(1)} %pad_add_fusion.1.swap_ref, f32[2,256,256]{2,1,0:T(8,128)S(1)} %copy-done.7, f32[2,256,256]{2,1,0:T(8,128)S(1)} %copy-done.10, ...), custom_call_target="tpu_custom_call" | custom-call | flops 6000000000 | bytes 18000000 | tf_op jit(solution)/shard_map/move_columns/pallas_call | solution.py:554
  104.2 13.9 %collective-permute-start.24 = (f32[2,256,256]{2,1,0:T(8,128)}, f32[2,256,256]{2,1,0:T(8,128)}, u32[]{:S(2)}, u32[]{:S(2)}) collective-permute-start(f32[2,256,256]{2,1,0:T(8,128)} %get-tuple-element.45), channel_id=1, source_target_pairs={{0,1},{1,0},{2,3},{3,2},{4,5},{5,4},{6,7},{7,6},{8,9},{9,8},{10,11... | collective-permute-start | bytes 1572872 | tf_op jit(solution)/shard_map/ppermute | solution.py:641
  118.2 2.7 %collective-permute-done.8.refs_2_ = f32[2,256,256]{2,1,0:T(8,128)} collective-permute-done((f32[2,256,256]{2,1,0:T(8,128)}, f32[2,256,256]{2,1,0:T(8,128)}, u32[]{:S(2)}, u32[]{:S(2)}) %collective-permute-start.8) | collective-permute-done | bytes 524320 | tf_op jit(solution)/shard_map/ppermute | solution.py:641
  120.9 6.1 %move_columns.5 = (f32[2,256,256]{2,1,0:T(8,128)S(1)}, f32[2,256,256]{2,1,0:T(8,128)S(1)}, f32[2,256,256]{2,1,0:T(8,128)S(1)}, f32[2,256,256]{2,1,0:T(8,128)}) custom-call(s32[2]{0:T(128)S(1)} %pad_add_fusion.1.swap_ref, f32[2,256,256]{2,1,0:T(8,128)S(1)} %copy-done.6, f32[2,256,256]{2,1,0:T(8,128)} %collective-permute-done.7.refs_1_, ...), custom_call_target="tpu_custom_call" | custom-call | flops 6000000000 | bytes 18000000 | tf_op jit(solution)/shard_map/move_columns/pallas_call | solution.py:554
  129.4 10.6 %collective-permute-done.4.refs_1_ = f32[2,256,256]{2,1,0:T(8,128)} collective-permute-done((f32[2,256,256]{2,1,0:T(8,128)}, f32[2,256,256]{2,1,0:T(8,128)}, u32[]{:S(2)}, u32[]{:S(2)}) %collective-permute-start.4) | collective-permute-done | bytes 524320 | tf_op jit(solution)/shard_map/ppermute | solution.py:641
  140.1 1.2 slice.57
  141.8 1.2 slice.58
  144.2 4.1 %maximum_select_fusion.refs_4_.refs_5_.refs_8_ = f32[4,2,2,256,256]{4,3,2,1,0:T(8,128)S(1)} fusion(f32[2,2,2,256,256]{4,3,2,1,0:T(8,128)} %collective-permute-done.17, f32[2,2,2,256,256]{4,3,2,1,0:T(8,128)} %maximum_select_fusion.1, pred[]{:T(512)S(6)} %eq.80), kind=kLoop, calls=%fused_computation.2 | loop fusion | flops 3145728 | bytes 8388609 | tf_op jit(solution)/shard_map/jit(_where)/select_n | solution.py:682
  148.4 4.4 %turn_rows.3 = (f32[2,256,256]{2,1,0:T(8,128)S(1)}, f32[2,256,256]{2,1,0:T(8,128)S(1)}, f32[2,256,256]{2,1,0:T(8,128)S(1)}, f32[2,256,256]{2,1,0:T(8,128)S(1)}) custom-call(f32[1]{0:T(128)} %bitcast.9.scale_ref, f32[2,256,256]{2,1,0:T(8,128)} %get-tuple-element.44.refs_0_, f32[2,256,256]{2,1,0:T(8,128)S(1)} %copy-done.13, ...), custom_call_target="tpu_custom_call" | custom-call | flops 4000000000 | bytes 12000000 | tf_op jit(solution)/shard_map/turn_rows/pallas_call | solution.py:526
  152.9 3.1 %turn_rows.2 = (f32[2,256,256]{2,1,0:T(8,128)S(1)}, f32[2,256,256]{2,1,0:T(8,128)S(1)}, f32[2,256,256]{2,1,0:T(8,128)S(1)}, f32[2,256,256]{2,1,0:T(8,128)S(1)}, f32[2,256,1024]{2,1,0:T(8,128)S(1)}) custom-call(f32[1]{0:T(128)S(6)} %add.694.scale_ref, f32[2,256,256]{2,1,0:T(8,128)S(1)} %copy-done.25, f32[2,256,256]{2,1,0:T(8,128)S(1)} %copy-done.27, ...), custom_call_target="tpu_custom_call" | custom-call | flops 4000000000 | bytes 12000000 | tf_op jit(solution)/shard_map/turn_rows/pallas_call | solution.py:526
  156.6 1.7 collective-permute-start.19
  160.0 4.5 %move_columns.7 = (f32[2,256,256]{2,1,0:T(8,128)S(1)}, f32[2,256,256]{2,1,0:T(8,128)S(1)}, f32[2,256,256]{2,1,0:T(8,128)S(1)}, f32[2,256,256]{2,1,0:T(8,128)S(1)}) custom-call(s32[2]{0:T(128)S(1)} %add_add_fusion.swap_ref, f32[2,256,256]{2,1,0:T(8,128)S(1)} %get-tuple-element.64.refs_0_, f32[2,256,256]{2,1,0:T(8,128)S(1)} %get-tuple-element.65.refs_1_, ...), custom_call_target="tpu_custom_call" | custom-call | flops 6000000000 | bytes 18000000 | tf_op jit(solution)/shard_map/move_columns/pallas_call | solution.py:554
  165.1 1.4 collective-permute-start.35
  166.5 4.6 %move_columns.6 = (f32[2,256,256]{2,1,0:T(8,128)S(1)}, f32[2,256,256]{2,1,0:T(8,128)S(1)}, f32[2,256,256]{2,1,0:T(8,128)S(1)}, f32[2,256,256]{2,1,0:T(8,128)S(1)}) custom-call(s32[2]{0:T(128)S(1)} %add_add_fusion.swap_ref, f32[2,256,256]{2,1,0:T(8,128)S(1)} %get-tuple-element.59.refs_0_, f32[2,256,256]{2,1,0:T(8,128)S(1)} %get-tuple-element.60.refs_1_, ...), custom_call_target="tpu_custom_call" | custom-call | flops 6000000000 | bytes 18000000 | tf_op jit(solution)/shard_map/move_columns/pallas_call | solution.py:554
  173.3 3.5 %image_rows.2 = (f32[256,256]{1,0:T(8,128)S(1)}, f32[256,256]{1,0:T(8,128)S(1)}, f32[256,256]{1,0:T(8,128)S(1)}, f32[256,256]{1,0:T(8,128)S(1)}) custom-call(s32[4]{0:T(128)S(1)} %pad_add_fusion.place_ref, f32[1]{0:T(128)} %bitcast.9.scale_ref, f32[2,256,1024]{2,1,0:T(8,128)S(1)} %get-tuple-element.52.refs_0_, ...), custom_call_target="tpu_custom_call" | custom-call | flops 3000000000 | bytes 9000000 | tf_op jit(solution)/shard_map/image_rows/pallas_call | solution.py:539
  176.8 5.9 %collective-permute-done.33.refs_5_ = f32[2,256,256]{2,1,0:T(8,128)S(1)} collective-permute-done((f32[2,256,256]{2,1,0:T(8,128)S(1)}, f32[2,256,256]{2,1,0:T(8,128)S(1)}, u32[]{:S(2)}, u32[]{:S(2)}) %collective-permute-start.33) | collective-permute-done | bytes 524320 | tf_op jit(solution)/shard_map/ppermute | solution.py:641
  183.4 12.4 %collective-permute-done.35.refs_7_ = f32[2,256,256]{2,1,0:T(8,128)S(1)} collective-permute-done((f32[2,256,256]{2,1,0:T(8,128)S(1)}, f32[2,256,256]{2,1,0:T(8,128)S(1)}, u32[]{:S(2)}, u32[]{:S(2)}) %collective-permute-start.35) | collective-permute-done | bytes 524320 | tf_op jit(solution)/shard_map/ppermute | solution.py:641
  196.6 1.5 collective-permute-start.22
  198.1 15.5 %collective-permute-done.32.refs_4_ = f32[2,256,256]{2,1,0:T(8,128)S(1)} collective-permute-done((f32[2,256,256]{2,1,0:T(8,128)S(1)}, f32[2,256,256]{2,1,0:T(8,128)S(1)}, u32[]{:S(2)}, u32[]{:S(2)}) %collective-permute-start.32) | collective-permute-done | bytes 524320 | tf_op jit(solution)/shard_map/ppermute | solution.py:641
  213.9 10.1 %collective-permute-done.34.refs_6_ = f32[2,256,256]{2,1,0:T(8,128)S(1)} collective-permute-done((f32[2,256,256]{2,1,0:T(8,128)S(1)}, f32[2,256,256]{2,1,0:T(8,128)S(1)}, u32[]{:S(2)}, u32[]{:S(2)}) %collective-permute-start.34) | collective-permute-done | bytes 524320 | tf_op jit(solution)/shard_map/ppermute | solution.py:641
  224.0 3.9 %image_rows.3 = (f32[256,256]{1,0:T(8,128)S(1)}, f32[256,256]{1,0:T(8,128)S(1)}, f32[256,256]{1,0:T(8,128)S(1)}, f32[256,256]{1,0:T(8,128)S(1)}) custom-call(s32[4]{0:T(128)S(1)} %pad_add_fusion.place_ref, f32[1]{0:T(128)} %bitcast.9.scale_ref, f32[2,256,256]{2,1,0:T(8,128)S(1)} %get-tuple-element.63.refs_0_, f32[2,256,256]{2,1,0:T(8,128)S(1)} %get-tuple-element.68.refs_1_, ...), custom_call_target="tpu_custom_call" | custom-call | flops 3000000000 | bytes 9000000 | tf_op jit(solution)/shard_map/image_rows/pallas_call | solution.py:539
  228.6 2.6 %collective-permute-start.37 = (f32[256,256]{1,0:T(8,128)S(1)}, f32[256,256]{1,0:T(8,128)S(1)}, u32[]{:S(2)}, u32[]{:S(2)}) collective-permute-start(f32[256,256]{1,0:T(8,128)S(1)} %get-tuple-element.76), channel_id=1, source_target_pairs={{0,1},{1,9},{2,3},{3,11},{4,5},{5,13},{6,7},{7,15},{8,0},{9,8},{10... | collective-permute-start | bytes 786440 | tf_op jit(solution)/shard_map/ppermute | solution.py:641
  231.2 2.4 collective-permute-start.38
  234.4 16.4 %collective-permute-done.37 = f32[256,256]{1,0:T(8,128)S(1)} collective-permute-done((f32[256,256]{1,0:T(8,128)S(1)}, f32[256,256]{1,0:T(8,128)S(1)}, u32[]{:S(2)}, u32[]{:S(2)}) %collective-permute-start.37) | collective-permute-done | bytes 262176 | tf_op jit(solution)/shard_map/ppermute | solution.py:641
  250.8 7.3 %collective-permute-done.39 = f32[256,256]{1,0:T(8,128)S(1)} collective-permute-done((f32[256,256]{1,0:T(8,128)S(1)}, f32[256,256]{1,0:T(8,128)S(1)}, u32[]{:S(2)}, u32[]{:S(2)}) %collective-permute-start.39) | collective-permute-done | bytes 262176 | tf_op jit(solution)/shard_map/ppermute | solution.py:641
  (159 shorter events, 26.8 us)
Async XLA Ops:
  2.3 16.3 %collective-permute-start.12 = (f32[2,256,128]{2,1,0:T(8,128)}, f32[2,256,128]{2,1,0:T(8,128)}, u32[]{:S(2)}, u32[]{:S(2)}) collective-permute-start(f32[2,256,128]{2,1,0:T(8,128)} %constant_dynamic-slice_fusion.2), channel_id=1, source_target_pairs={{0,4},{1,5},{2,6},{3,7},{4,0},{5,1},{6,2},{7,3},{8,12},{9,13},{10,... | collective-permute-start | bytes 786440 | tf_op jit(solution)/shard_map/ppermute | solution.py:641
  5.4 21.7 %collective-permute-start.13 = (f32[2,256,128]{2,1,0:T(8,128)}, f32[2,256,128]{2,1,0:T(8,128)}, u32[]{:S(2)}, u32[]{:S(2)}) collective-permute-start(f32[2,256,128]{2,1,0:T(8,128)} %constant_dynamic-slice_fusion.2), channel_id=1, source_target_pairs={{0,8},{1,9},{2,10},{3,11},{4,12},{5,13},{6,14},{7,15},{8,0},{9,1},... | collective-permute-start | bytes 786440 | tf_op jit(solution)/shard_map/ppermute | solution.py:641
  7.9 19.1 %collective-permute-start.14 = (f32[2,256,128]{2,1,0:T(8,128)}, f32[2,256,128]{2,1,0:T(8,128)}, u32[]{:S(2)}, u32[]{:S(2)}) collective-permute-start(f32[2,256,128]{2,1,0:T(8,128)} %constant_dynamic-slice_fusion.2), channel_id=1, source_target_pairs={{0,12},{1,13},{2,14},{3,15},{4,8},{5,9},{6,10},{7,11},{8,4},{9,5},... | collective-permute-start | bytes 786440 | tf_op jit(solution)/shard_map/ppermute | solution.py:641
  17.8 11.4 %collective-permute-start = (f32[2,2,256,256]{3,2,1,0:T(8,128)}, f32[2,2,256,256]{3,2,1,0:T(8,128)}, u32[]{:S(2)}, u32[]{:S(2)}) collective-permute-start(f32[2,2,256,256]{3,2,1,0:T(8,128)} %get-tuple-element.43), channel_id=1, source_target_pairs={{0,1},{1,0},{2,3},{3,2},{4,5},{5,4},{6,7},{7,6},{8,9},{9,8},{10,11... | collective-permute-start | bytes 3145736 | tf_op jit(solution)/shard_map/ppermute | solution.py:641
  17.8 22.0 %collective-permute-start.6 = (f32[2,2,256,256]{3,2,1,0:T(8,128)}, f32[2,2,256,256]{3,2,1,0:T(8,128)}, u32[]{:S(2)}, u32[]{:S(2)}) collective-permute-start(f32[2,2,256,256]{3,2,1,0:T(8,128)} %get-tuple-element.47), channel_id=1, source_target_pairs={{0,1},{1,0},{2,3},{3,2},{4,5},{5,4},{6,7},{7,6},{8,9},{9,8},{10,11... | collective-permute-start | bytes 3145736 | tf_op jit(solution)/shard_map/ppermute | solution.py:641
  18.5 10.7 %copy-start.5 = (f32[2,2,256,256]{3,2,1,0:T(8,128)S(1)}, f32[2,2,256,256]{3,2,1,0:T(8,128)}, u32[]{:S(2)}) copy-start(f32[2,2,256,256]{3,2,1,0:T(8,128)} %copy-done.4) | copy-start | bytes 3145732
  31.5 27.0 %collective-permute-start.1 = (f32[2,256,256]{2,1,0:T(8,128)S(1)}, f32[2,256,256]{2,1,0:T(8,128)S(1)}, u32[]{:S(2)}, u32[]{:S(2)}) collective-permute-start(f32[2,256,256]{2,1,0:T(8,128)S(1)} %get-tuple-element.86), channel_id=1, source_target_pairs={{0,4},{1,5},{2,6},{3,7},{4,0},{5,1},{6,2},{7,3},{8,12},{9,13},{10,... | collective-permute-start | bytes 1572872 | tf_op jit(solution)/shard_map/ppermute | solution.py:641
  37.3 55.2 %collective-permute-start.2 = (f32[2,256,256]{2,1,0:T(8,128)}, f32[2,256,256]{2,1,0:T(8,128)}, u32[]{:S(2)}, u32[]{:S(2)}) collective-permute-start(f32[2,256,256]{2,1,0:T(8,128)} %get-tuple-element.87), channel_id=1, source_target_pairs={{0,8},{1,9},{2,10},{3,11},{4,12},{5,13},{6,14},{7,15},{8,0},{9,1},... | collective-permute-start | bytes 1572872 | tf_op jit(solution)/shard_map/ppermute | solution.py:641
  38.3 57.5 %collective-permute-start.3 = (f32[2,256,256]{2,1,0:T(8,128)}, f32[2,256,256]{2,1,0:T(8,128)}, u32[]{:S(2)}, u32[]{:S(2)}) collective-permute-start(f32[2,256,256]{2,1,0:T(8,128)} %get-tuple-element.85), channel_id=1, source_target_pairs={{0,12},{1,13},{2,14},{3,15},{4,8},{5,9},{6,10},{7,11},{8,4},{9,5},... | collective-permute-start | bytes 1572872 | tf_op jit(solution)/shard_map/ppermute | solution.py:641
  41.3 19.4 %copy-start.29 = (f32[2,4,256,128]{3,2,1,0:T(8,128)S(1)}, f32[2,4,256,128]{3,2,1,0:T(8,128)}, u32[]{:S(2)}) copy-start(f32[2,4,256,128]{3,2,1,0:T(8,128)} %pad_maximum_fusion.2) | copy-start | bytes 3145732
  42.4 61.9 %collective-permute-start.7 = (f32[2,256,256]{2,1,0:T(8,128)}, f32[2,256,256]{2,1,0:T(8,128)}, u32[]{:S(2)}, u32[]{:S(2)}) collective-permute-start(f32[2,256,256]{2,1,0:T(8,128)} %get-tuple-element.90), channel_id=1, source_target_pairs={{0,4},{1,5},{2,6},{3,7},{4,0},{5,1},{6,2},{7,3},{8,12},{9,13},{10,... | collective-permute-start | bytes 1572872 | tf_op jit(solution)/shard_map/ppermute | solution.py:641
  43.4 17.5 %copy-start.28 = (s32[4]{0:T(128)S(1)}, s32[4]{0:T(128)}, u32[]{:S(2)}) copy-start(s32[4]{0:T(128)} %constant.231.clone) | copy-start | bytes 52
  44.4 76.4 %collective-permute-start.8 = (f32[2,256,256]{2,1,0:T(8,128)}, f32[2,256,256]{2,1,0:T(8,128)}, u32[]{:S(2)}, u32[]{:S(2)}) collective-permute-start(f32[2,256,256]{2,1,0:T(8,128)} %get-tuple-element.91), channel_id=1, source_target_pairs={{0,8},{1,9},{2,10},{3,11},{4,12},{5,13},{6,14},{7,15},{8,0},{9,1},... | collective-permute-start | bytes 1572872 | tf_op jit(solution)/shard_map/ppermute | solution.py:641
  60.7 2.0 collective-permute-start.15
  63.8 25.4 %collective-permute-start.16 = (f32[2,2,256,256]{3,2,1,0:T(8,128)}, f32[2,2,256,256]{3,2,1,0:T(8,128)S(1)}, u32[]{:S(2)}, u32[]{:S(2)}) collective-permute-start(f32[2,2,256,256]{3,2,1,0:T(8,128)} %maximum_select_fusion.3), channel_id=1, source_target_pairs={{0,2},{1,3},{2,0},{3,1},{4,6},{5,7},{6,4},{7,5},{8,10},{9,11},{10,... | collective-permute-start | bytes 3145736 | tf_op jit(solution)/shard_map/ppermute | solution.py:641
  90.7 53.4 %collective-permute-start.17 = (f32[2,2,2,256,256]{4,3,2,1,0:T(8,128)}, f32[2,2,2,256,256]{4,3,2,1,0:T(8,128)}, u32[]{:S(2)}, u32[]{:S(2)}) collective-permute-start(f32[2,2,2,256,256]{4,3,2,1,0:T(8,128)} %maximum_select_fusion.1), channel_id=1, source_target_pairs={{0,16},{1,17},{2,18},{3,19},{4,20},{5,21},{6,22},{7,23},{8,24},{9,... | collective-permute-start | bytes 6291464 | tf_op jit(solution)/shard_map/ppermute | solution.py:641
  93.4 27.5 %collective-permute-start.9 = (f32[2,256,256]{2,1,0:T(8,128)S(1)}, f32[2,256,256]{2,1,0:T(8,128)S(1)}, u32[]{:S(2)}, u32[]{:S(2)}) collective-permute-start(f32[2,256,256]{2,1,0:T(8,128)S(1)} %copy-done.30), channel_id=1, source_target_pairs={{0,12},{1,13},{2,14},{3,15},{4,8},{5,9},{6,10},{7,11},{8,4},{9,5},... | collective-permute-start | bytes 1572872 | tf_op jit(solution)/shard_map/ppermute | solution.py:641
  103.4 37.9 %collective-permute-start.5 = (f32[2,256,256]{2,1,0:T(8,128)}, f32[2,256,256]{2,1,0:T(8,128)}, u32[]{:S(2)}, u32[]{:S(2)}) collective-permute-start(f32[2,256,256]{2,1,0:T(8,128)} %get-tuple-element.45), channel_id=1, source_target_pairs={{0,5},{1,4},{2,7},{3,6},{4,1},{5,0},{6,3},{7,2},{8,13},{9,12},{10,... | collective-permute-start | bytes 1572872 | tf_op jit(solution)/shard_map/ppermute | solution.py:641
  103.4 17.5 %copy-start.6 = (f32[2,256,256]{2,1,0:T(8,128)S(1)}, f32[2,256,256]{2,1,0:T(8,128)}, u32[]{:S(2)}) copy-start(f32[2,256,256]{2,1,0:T(8,128)} %get-tuple-element.92.refs_0_) | copy-start | bytes 1572868
  104.2 22.7 %copy-start.2 = (f32[8,2,128,256]{3,2,1,0:T(8,128)}, f32[8,2,128,256]{3,2,1,0:T(8,128)S(1)}, u32[]{:S(2)}) copy-start(f32[8,2,128,256]{3,2,1,0:T(8,128)S(1)} %pad_maximum_fusion.1.refs_7_) | copy-start | bytes 6291460
  104.2 44.1 %collective-permute-start.24 = (f32[2,256,256]{2,1,0:T(8,128)}, f32[2,256,256]{2,1,0:T(8,128)}, u32[]{:S(2)}, u32[]{:S(2)}) collective-permute-start(f32[2,256,256]{2,1,0:T(8,128)} %get-tuple-element.45), channel_id=1, source_target_pairs={{0,1},{1,0},{2,3},{3,2},{4,5},{5,4},{6,7},{7,6},{8,9},{9,8},{10,11... | collective-permute-start | bytes 1572872 | tf_op jit(solution)/shard_map/ppermute | solution.py:641
  120.9 19.2 %collective-permute-start.4 = (f32[2,256,256]{2,1,0:T(8,128)}, f32[2,256,256]{2,1,0:T(8,128)}, u32[]{:S(2)}, u32[]{:S(2)}) collective-permute-start(f32[2,256,256]{2,1,0:T(8,128)} %get-tuple-element.44.refs_0_), channel_id=1, source_target_pairs={{0,4},{1,5},{2,6},{3,7},{4,0},{5,1},{6,2},{7,3},{8,12},{9,13},{10,... | collective-permute-start | bytes 1572872 | tf_op jit(solution)/shard_map/ppermute | solution.py:641
  129.4 18.9 %collective-permute-start.25 = (f32[2,256,256]{2,1,0:T(8,128)}, f32[2,256,256]{2,1,0:T(8,128)}, u32[]{:S(2)}, u32[]{:S(2)}) collective-permute-start(f32[2,256,256]{2,1,0:T(8,128)} %get-tuple-element.54), channel_id=1, source_target_pairs={{0,1},{1,0},{2,3},{3,2},{4,5},{5,4},{6,7},{7,6},{8,9},{9,8},{10,11... | collective-permute-start | bytes 1572872 | tf_op jit(solution)/shard_map/ppermute | solution.py:641
  140.1 12.8 %collective-permute-start.10 = (f32[2,256,256]{2,1,0:T(8,128)}, f32[2,256,256]{2,1,0:T(8,128)S(1)}, u32[]{:S(2)}, u32[]{:S(2)}) collective-permute-start(f32[2,256,256]{2,1,0:T(8,128)} %copy-done.11), channel_id=1, source_target_pairs={{0,1},{1,0},{2,3},{3,2},{4,5},{5,4},{6,7},{7,6},{8,9},{9,8},{10,11... | collective-permute-start | bytes 1572872 | tf_op jit(solution)/shard_map/ppermute | solution.py:641
  141.3 11.6 %collective-permute-start.11 = (f32[2,256,256]{2,1,0:T(8,128)}, f32[2,256,256]{2,1,0:T(8,128)S(1)}, u32[]{:S(2)}, u32[]{:S(2)}) collective-permute-start(f32[2,256,256]{2,1,0:T(8,128)} %copy-done.14), channel_id=1, source_target_pairs={{0,1},{1,0},{2,3},{3,2},{4,5},{5,4},{6,7},{7,6},{8,9},{9,8},{10,11... | collective-permute-start | bytes 1572872 | tf_op jit(solution)/shard_map/ppermute | solution.py:641
  144.2 14.1 %collective-permute-start.18 = (f32[2,256,256]{2,1,0:T(8,128)}, f32[2,256,256]{2,1,0:T(8,128)S(1)}, u32[]{:S(2)}, u32[]{:S(2)}) collective-permute-start(f32[2,256,256]{2,1,0:T(8,128)} %copy-done.12), channel_id=1, source_target_pairs={{0,4},{1,5},{2,6},{3,7},{4,0},{5,1},{6,2},{7,3},{8,12},{9,13},{10,... | collective-permute-start | bytes 1572872 | tf_op jit(solution)/shard_map/ppermute | solution.py:641
  152.8 7.2 %collective-permute-start.29 = (f32[2,256,256]{2,1,0:T(8,128)S(1)}, f32[2,256,256]{2,1,0:T(8,128)S(1)}, u32[]{:S(2)}, u32[]{:S(2)}) collective-permute-start(f32[2,256,256]{2,1,0:T(8,128)S(1)} %get-tuple-element.67), channel_id=1, source_target_pairs={{0,1},{1,0},{2,3},{3,2},{4,5},{5,4},{6,7},{7,6},{8,9},{9,8},{10,11... | collective-permute-start | bytes 1572872 | tf_op jit(solution)/shard_map/ppermute | solution.py:641
  152.9 7.1 %copy-start.3 = (f32[8,2,128,256]{3,2,1,0:T(8,128)S(1)}, f32[8,2,128,256]{3,2,1,0:T(8,128)}, u32[]{:S(2)}) copy-start(f32[8,2,128,256]{3,2,1,0:T(8,128)} %copy-done.2) | copy-start | bytes 6291460
  152.9 7.1 %copy-start.23 = (f32[2,128,128]{2,1,0:T(8,128)S(1)}, f32[2,128,128]{2,1,0:T(8,128)}, u32[]{:S(2)}) copy-start(f32[2,128,128]{2,1,0:T(8,128)} %constant.230.clone.refs_6_) | copy-start | bytes 393220
  156.0 4.0 %collective-permute-start.28 = (f32[2,256,256]{2,1,0:T(8,128)S(1)}, f32[2,256,256]{2,1,0:T(8,128)S(1)}, u32[]{:S(2)}, u32[]{:S(2)}) collective-permute-start(f32[2,256,256]{2,1,0:T(8,128)S(1)} %get-tuple-element.66), channel_id=1, source_target_pairs={{0,1},{1,0},{2,3},{3,2},{4,5},{5,4},{6,7},{7,6},{8,9},{9,8},{10,11... | collective-permute-start | bytes 1572872 | tf_op jit(solution)/shard_map/ppermute | solution.py:641
  156.6 15.3 %collective-permute-start.19 = (f32[2,256,256]{2,1,0:T(8,128)}, f32[2,256,256]{2,1,0:T(8,128)S(1)}, u32[]{:S(2)}, u32[]{:S(2)}) collective-permute-start(f32[2,256,256]{2,1,0:T(8,128)} %get-tuple-element.54), channel_id=1, source_target_pairs={{0,5},{1,4},{2,7},{3,6},{4,1},{5,0},{6,3},{7,2},{8,13},{9,12},{10,... | collective-permute-start | bytes 1572872 | tf_op jit(solution)/shard_map/ppermute | solution.py:641
  159.5 5.6 %collective-permute-start.27 = (f32[2,256,256]{2,1,0:T(8,128)S(1)}, f32[2,256,256]{2,1,0:T(8,128)S(1)}, u32[]{:S(2)}, u32[]{:S(2)}) collective-permute-start(f32[2,256,256]{2,1,0:T(8,128)S(1)} %get-tuple-element.62), channel_id=1, source_target_pairs={{0,1},{1,0},{2,3},{3,2},{4,5},{5,4},{6,7},{7,6},{8,9},{9,8},{10,11... | collective-permute-start | bytes 1572872 | tf_op jit(solution)/shard_map/ppermute | solution.py:641
  159.9 6.5 %collective-permute-start.26 = (f32[2,256,256]{2,1,0:T(8,128)S(1)}, f32[2,256,256]{2,1,0:T(8,128)S(1)}, u32[]{:S(2)}, u32[]{:S(2)}) collective-permute-start(f32[2,256,256]{2,1,0:T(8,128)S(1)} %get-tuple-element.61), channel_id=1, source_target_pairs={{0,1},{1,0},{2,3},{3,2},{4,5},{5,4},{6,7},{7,6},{8,9},{9,8},{10,11... | collective-permute-start | bytes 1572872 | tf_op jit(solution)/shard_map/ppermute | solution.py:641
  164.5 8.2 %collective-permute-start.31 = (f32[2,256,256]{2,1,0:T(8,128)S(1)}, f32[2,256,256]{2,1,0:T(8,128)S(1)}, u32[]{:S(2)}, u32[]{:S(2)}) collective-permute-start(f32[2,256,256]{2,1,0:T(8,128)S(1)} %get-tuple-element.70), channel_id=1, source_target_pairs={{0,1},{1,0},{2,3},{3,2},{4,5},{5,4},{6,7},{7,6},{8,9},{9,8},{10,11... | collective-permute-start | bytes 1572872 | tf_op jit(solution)/shard_map/ppermute | solution.py:641
  165.0 17.7 %collective-permute-start.33 = (f32[2,256,256]{2,1,0:T(8,128)S(1)}, f32[2,256,256]{2,1,0:T(8,128)S(1)}, u32[]{:S(2)}, u32[]{:S(2)}) collective-permute-start(f32[2,256,256]{2,1,0:T(8,128)S(1)} %get-tuple-element.72), channel_id=1, source_target_pairs={{0,4},{1,5},{2,6},{3,7},{4,0},{5,1},{6,2},{7,3},{8,12},{9,13},{10,... | collective-permute-start | bytes 1572872 | tf_op jit(solution)/shard_map/ppermute | solution.py:641
  165.1 30.7 %collective-permute-start.35 = (f32[2,256,256]{2,1,0:T(8,128)S(1)}, f32[2,256,256]{2,1,0:T(8,128)S(1)}, u32[]{:S(2)}, u32[]{:S(2)}) collective-permute-start(f32[2,256,256]{2,1,0:T(8,128)S(1)} %get-tuple-element.74), channel_id=1, source_target_pairs={{0,5},{1,4},{2,7},{3,6},{4,1},{5,0},{6,3},{7,2},{8,13},{9,12},{10,... | collective-permute-start | bytes 1572872 | tf_op jit(solution)/shard_map/ppermute | solution.py:641
  171.1 25.5 %collective-permute-start.30 = (f32[2,256,256]{2,1,0:T(8,128)S(1)}, f32[2,256,256]{2,1,0:T(8,128)S(1)}, u32[]{:S(2)}, u32[]{:S(2)}) collective-permute-start(f32[2,256,256]{2,1,0:T(8,128)S(1)} %get-tuple-element.69), channel_id=1, source_target_pairs={{0,1},{1,0},{2,3},{3,2},{4,5},{5,4},{6,7},{7,6},{8,9},{9,8},{10,11... | collective-permute-start | bytes 1572872 | tf_op jit(solution)/shard_map/ppermute | solution.py:641
  171.9 41.7 %collective-permute-start.32 = (f32[2,256,256]{2,1,0:T(8,128)S(1)}, f32[2,256,256]{2,1,0:T(8,128)S(1)}, u32[]{:S(2)}, u32[]{:S(2)}) collective-permute-start(f32[2,256,256]{2,1,0:T(8,128)S(1)} %get-tuple-element.71), channel_id=1, source_target_pairs={{0,4},{1,5},{2,6},{3,7},{4,0},{5,1},{6,2},{7,3},{8,12},{9,13},{10,... | collective-permute-start | bytes 1572872 | tf_op jit(solution)/shard_map/ppermute | solution.py:641
  172.7 51.2 %collective-permute-start.34 = (f32[2,256,256]{2,1,0:T(8,128)S(1)}, f32[2,256,256]{2,1,0:T(8,128)S(1)}, u32[]{:S(2)}, u32[]{:S(2)}) collective-permute-start(f32[2,256,256]{2,1,0:T(8,128)S(1)} %get-tuple-element.73), channel_id=1, source_target_pairs={{0,5},{1,4},{2,7},{3,6},{4,1},{5,0},{6,3},{7,2},{8,13},{9,12},{10,... | collective-permute-start | bytes 1572872 | tf_op jit(solution)/shard_map/ppermute | solution.py:641
  182.7 45.9 %collective-permute-start.20 = (f32[256,256]{1,0:T(8,128)S(1)}, f32[256,256]{1,0:T(8,128)S(1)}, u32[]{:S(2)}, u32[]{:S(2)}) collective-permute-start(f32[256,256]{1,0:T(8,128)S(1)} %get-tuple-element.55), channel_id=1, source_target_pairs={{0,0},{1,8},{2,2},{3,10},{4,4},{5,12},{6,6},{7,14},{8,1},{9,9},{10... | collective-permute-start | bytes 786440 | tf_op jit(solution)/shard_map/ppermute | solution.py:641
  195.8 35.4 %collective-permute-start.21 = (f32[256,256]{1,0:T(8,128)S(1)}, f32[256,256]{1,0:T(8,128)S(1)}, u32[]{:S(2)}, u32[]{:S(2)}) collective-permute-start(f32[256,256]{1,0:T(8,128)S(1)} %get-tuple-element.56), channel_id=1, source_target_pairs={{0,1},{1,9},{2,3},{3,11},{4,5},{5,13},{6,7},{7,15},{8,0},{9,8},{10... | collective-permute-start | bytes 786440 | tf_op jit(solution)/shard_map/ppermute | solution.py:641
  196.6 37.0 %collective-permute-start.22 = (f32[256,256]{1,0:T(8,128)S(1)}, f32[256,256]{1,0:T(8,128)S(1)}, u32[]{:S(2)}, u32[]{:S(2)}) collective-permute-start(f32[256,256]{1,0:T(8,128)S(1)} %get-tuple-element.57), channel_id=1, source_target_pairs={{0,2},{1,10},{2,0},{3,8},{4,6},{5,14},{6,4},{7,12},{8,3},{9,11},{1... | collective-permute-start | bytes 786440 | tf_op jit(solution)/shard_map/ppermute | solution.py:641
  213.6 20.7 %collective-permute-start.23 = (f32[256,256]{1,0:T(8,128)S(1)}, f32[256,256]{1,0:T(8,128)S(1)}, u32[]{:S(2)}, u32[]{:S(2)}) collective-permute-start(f32[256,256]{1,0:T(8,128)S(1)} %get-tuple-element.58), channel_id=1, source_target_pairs={{0,3},{1,11},{2,1},{3,9},{4,7},{5,15},{6,5},{7,13},{8,2},{9,10},{1... | collective-permute-start | bytes 786440 | tf_op jit(solution)/shard_map/ppermute | solution.py:641
  224.0 35.1 %copy-start.1 = (f32[2,256,1024]{2,1,0:T(8,128)S(1)}, f32[2,256,1024]{2,1,0:T(8,128)}, u32[]{:S(2)}) copy-start(f32[2,256,1024]{2,1,0:T(8,128)} %param.15) | copy-start | bytes 6291460
  227.9 6.5 %collective-permute-start.36 = (f32[256,256]{1,0:T(8,128)S(1)}, f32[256,256]{1,0:T(8,128)S(1)}, u32[]{:S(2)}, u32[]{:S(2)}) collective-permute-start(f32[256,256]{1,0:T(8,128)S(1)} %get-tuple-element.75), channel_id=1, source_target_pairs={{0,0},{1,8},{2,2},{3,10},{4,4},{5,12},{6,6},{7,14},{8,1},{9,9},{10... | collective-permute-start | bytes 786440 | tf_op jit(solution)/shard_map/ppermute | solution.py:641
  228.6 22.2 %collective-permute-start.37 = (f32[256,256]{1,0:T(8,128)S(1)}, f32[256,256]{1,0:T(8,128)S(1)}, u32[]{:S(2)}, u32[]{:S(2)}) collective-permute-start(f32[256,256]{1,0:T(8,128)S(1)} %get-tuple-element.76), channel_id=1, source_target_pairs={{0,1},{1,9},{2,3},{3,11},{4,5},{5,13},{6,7},{7,15},{8,0},{9,8},{10... | collective-permute-start | bytes 786440 | tf_op jit(solution)/shard_map/ppermute | solution.py:641
  231.2 19.6 %collective-permute-start.38 = (f32[256,256]{1,0:T(8,128)S(1)}, f32[256,256]{1,0:T(8,128)S(1)}, u32[]{:S(2)}, u32[]{:S(2)}) collective-permute-start(f32[256,256]{1,0:T(8,128)S(1)} %get-tuple-element.77), channel_id=1, source_target_pairs={{0,2},{1,10},{2,0},{3,8},{4,6},{5,14},{6,4},{7,12},{8,3},{9,11},{1... | collective-permute-start | bytes 786440 | tf_op jit(solution)/shard_map/ppermute | solution.py:641
  233.6 24.6 %collective-permute-start.39 = (f32[256,256]{1,0:T(8,128)S(1)}, f32[256,256]{1,0:T(8,128)S(1)}, u32[]{:S(2)}, u32[]{:S(2)}) collective-permute-start(f32[256,256]{1,0:T(8,128)S(1)} %get-tuple-element.78), channel_id=1, source_target_pairs={{0,3},{1,11},{2,1},{3,9},{4,7},{5,15},{6,5},{7,13},{8,2},{9,10},{1... | collective-permute-start | bytes 786440 | tf_op jit(solution)/shard_map/ppermute | solution.py:641
  (24 other events, 62.7 us)

commit v5 on v4

--- a/solution.py
+++ b/solution.py
@@ -345,8 +345,13 @@
     ]
 
 
-def read_layer(ref, at, rows):
-    return [ref[a // 2, at[0], at[1], rows, lane_block(a % 2)] for a in range(y_radix)]
+def read_layer(place_ref, near_ref, far_ref, at, rows):
+    layer = []
+    for a in range(y_radix):
+        g = a // 2
+        index = (g % 2, at[0], at[1], rows, lane_block(a % 2))
+        layer.append(jnp.where(place_ref[0] == g // 2, near_ref[index], far_ref[index]))
+    return layer
 
 
 def screen_of(scale_ref, layer):
@@ -360,13 +365,13 @@
     return cosine, sine * phase
 
 
-def turn_kernel(keeps_field, at, scale_ref, *refs):
-    blocks, layer_ref, refs = refs[:4], refs[4], refs[5:]
+def turn_kernel(keeps_field, at, place_ref, scale_ref, *refs):
+    blocks, layer_refs, refs = refs[:4], refs[4:6], refs[6:]
     table_ref, inv_upper, inv_lower, upper_ref, lower_ref = refs[:5]
     outs = refs[5:]
     for rows in row_groups(blocks[0].shape[1]):
         terms = inverse_y(read_y_blocks(blocks, rows), table_ref, inv_upper, inv_lower)
-        layer = read_layer(layer_ref, at, rows)
+        layer = read_layer(place_ref, *layer_refs, at, rows)
         terms = [multiply(terms[a], screen_of(scale_ref, layer[a])) for a in range(y_radix)]
         if keeps_field:
             for a in range(y_radix):
@@ -381,11 +386,11 @@
 def image_kernel(own_ready, at, place_ref, scale_ref, *refs):
     own_count = 1 if own_ready else 4
     own, refs = refs[:own_count], refs[own_count:]
-    blocks, layer_ref, refs = refs[:4], refs[4], refs[5:]
+    blocks, layer_refs, refs = refs[:4], refs[4:6], refs[6:]
     table_ref, inv_upper, inv_lower = refs[:3]
     outs, quarters = refs[3:7], refs[7]
     for rows in row_groups(blocks[0].shape[1]):
-        layer = read_layer(layer_ref, at, rows)
+        layer = read_layer(place_ref, *layer_refs, at, rows)
         other = inverse_y(read_y_blocks(blocks, rows), table_ref, inv_upper, inv_lower)
         if not own_ready:
             mine = inverse_y(read_y_blocks(own, rows), table_ref, inv_upper, inv_lower)
@@ -518,34 +523,34 @@
     )(place, field, table, *matrices)
 
 
-def turn_rows(keeps_field, at, scale, blocks, layers, table, inverse, forward):
+def turn_rows(keeps_field, at, place, scale, blocks, layers, table, inverse, forward):
     parts, rows, width = blocks[0].shape
     out = [jax.ShapeDtypeStruct((parts, rows, width), jnp.float32)] * 4
     if keeps_field:
         out = out + [jax.ShapeDtypeStruct((parts, rows, 4 * width), jnp.float32)]
     return pl.pallas_call(
         functools.partial(turn_kernel, keeps_field, at),
-        in_specs=[smem] + [vmem] * 10,
+        in_specs=[smem, smem] + [vmem] * 11,
         out_specs=[vmem] * len(out),
         out_shape=out,
         compiler_params=pltpu.CompilerParams(vmem_limit_bytes=row_limit),
         cost_estimate=estimate(4),
         name="turn_rows",
-    )(scale, *blocks, layers, table, *inverse, *forward)
+    )(place, scale, *blocks, *layers, table, *inverse, *forward)
 
 
 def image_rows(at, place, scale, own, blocks, layers, table, inverse):
     parts, rows, width = blocks[0].shape
     return pl.pallas_call(
         functools.partial(image_kernel, len(own) == 1, at),
-        in_specs=[smem, smem] + [vmem] * (len(own) + 8),
+        in_specs=[smem, smem] + [vmem] * (len(own) + 9),
         out_specs=[vmem] * 4,
         out_shape=[jax.ShapeDtypeStruct((rows, width), jnp.float32)] * 4,
         scratch_shapes=[pltpu.VMEM((4, rows, width), jnp.float32)],
         compiler_params=pltpu.CompilerParams(vmem_limit_bytes=row_limit),
         cost_estimate=estimate(3),
         name="image_rows",
-    )(place, scale, *own, *blocks, layers, table, *inverse)
+    )(place, scale, *own, *blocks, *layers, table, *inverse)
 
 
 def move_columns(swaps, blocks, tables, move, forward, inverse):
@@ -678,8 +683,7 @@
         )
         other = to_freq(both)
         pair = jnp.where(x == 0, jnp.stack([both, other]), jnp.stack([other, both]))
-        far = to_shot(pair)
-        return jnp.where(s == 0, jnp.concatenate([pair, far]), jnp.concatenate([far, pair]))
+        return pair, to_shot(pair)
 
     y_steps = y_table(c, y_cols)
     spectra = origin_rows(wavefields[0], place, y_steps, row_forward)
@@ -734,7 +738,7 @@
             for slot in (1, 0):
                 blocks = y_blocks([near[0][slot], near[1][slot]])
                 turned[slot] = turn_rows(
-                    slot == 0, (depth_step, slot), scale + waits[slot], blocks, layers, y_steps,
+                    slot == 0, (depth_step, slot), place, scale + waits[slot], blocks, layers, y_steps,
                     row_inverse, row_forward,
                 )
             blocks_in = [

time: 260 us -> 264 us (1.015)
  other arithmetic: 17.3 us -> 12 us
  Pallas kernels: 40.7 us -> 45.4 us
    select_n x1 -> x0, other arithmetic: 4.05 us -> none  [all_columns(): jnp.where(s == 0, jnp.concatenate([pair, far]), jnp.concatenate([far, pai...]
    unnamed x64 -> x74, local copies, waits for them, and re-layouts: 12.2 us -> 14.9 us
    pallas_call x2, Pallas kernels: 7.51 us -> 10.2 us  [turn_rows(): pl.pallas_call(functools.partial(turn_kernel, keeps_field, at), in_specs=...]
  transfers between devices with their start and end apart: 40 -> 40, of which waited for: 12 -> 12; matrix products, arithmetic and copies ran while one was open for 10% -> 8% of each run, Pallas kernels for 16% -> 17%
where the time goes in v5:
time: 264 us; the launch traced here: 263 us
  waiting for transfers between devices  121 us (46%)
  starting transfers between devices  54.5 us (21%)
  Pallas kernels  45.4 us (17%)
  local copies, waits for them, and re-layouts  25.8 us (10%)
  other arithmetic  12 us (5%)
  between operations  3.83 us (1%)
    ppermute x40, waiting for transfers between devices, send(): return lax.ppermute(array, axes, route(sizes, target))  121 us
    ppermute x40, starting transfers between devices, send(): return lax.ppermute(array, axes, route(sizes, target))  54.5 us
    pallas_call x4, Pallas kernels, move_columns(): pl.pallas_call(x_kernel, in_specs=[smem] + [vmem] * (x_radix + 8), out_sp...  21.3 us
    unnamed x74, local copies, waits for them, and re-layouts  14.9 us
    pallas_call x2, Pallas kernels, turn_rows(): pl.pallas_call(functools.partial(turn_kernel, keeps_field, at), in_specs=...  10.2 us
    pallas_call x2, Pallas kernels, image_rows(): pl.pallas_call(functools.partial(image_kernel, len(own) == 1, at), in_spe...  9.37 us
  transfers between devices with their start and end apart: 40, of which 12 were waited for; matrix products, arithmetic and copies ran while one was open for 8% of the time, Pallas kernels for 17%

profile of v5, /device:TPU:0, one launch (start us, length us, event | category | flops | bytes accessed | tf_op | source)
XLA Modules:
  0.0 262.9 jit_solution(16175869118872381176)
XLA Ops:
  0.0 1.6 copy-done
  2.3 3.0 %collective-permute-start.12 = (f32[2,256,128]{2,1,0:T(8,128)}, f32[2,256,128]{2,1,0:T(8,128)}, u32[]{:S(2)}, u32[]{:S(2)}) collective-permute-start(f32[2,256,128]{2,1,0:T(8,128)} %constant_dynamic-slice_fusion.2), channel_id=1, source_target_pairs={{0,4},{1,5},{2,6},{3,7},{4,0},{5,1},{6,2},{7,3},{8,12},{9,13},{10,... | collective-permute-start | bytes 786440 | tf_op jit(solution)/shard_map/ppermute | solution.py:646
  5.4 2.6 collective-permute-start.13
  8.3 2.2 copy-done.12
  12.3 4.6 %origin_rows.1 = (f32[2,2,256,256]{3,2,1,0:T(8,128)S(1)}, f32[2,2,256,256]{3,2,1,0:T(8,128)S(1)}, f32[2,2,256,256]{3,2,1,0:T(8,128)}, f32[2,2,256,256]{3,2,1,0:T(8,128)}) custom-call(s32[4]{0:T(128)S(1)} %pad_add_fusion.place_ref, f32[2,2,256,1024]{3,2,1,0:T(8,128)S(1)} %bitcast.54, f32[8,2,128]{2,1,0:T(2,128)S(1)} %pad_maximum_fusion.4.table_ref.refs_6_.refs_7_.refs_10_, ...), custom_call_target="tpu_custom_call" | custom-call | flops 6000000000 | bytes 18000000 | tf_op jit(solution)/shard_map/origin_rows/pallas_call | solution.py:498
  18.6 8.4 %collective-permute-done.13 = f32[2,256,128]{2,1,0:T(8,128)} collective-permute-done((f32[2,256,128]{2,1,0:T(8,128)}, f32[2,256,128]{2,1,0:T(8,128)}, u32[]{:S(2)}, u32[]{:S(2)}) %collective-permute-start.13) | collective-permute-done | bytes 262176 | tf_op jit(solution)/shard_map/ppermute | solution.py:646
  27.0 2.2 pad_maximum_fusion.2
  29.2 1.4 broadcast_select_fusion.2
  31.5 4.8 %collective-permute-start.1 = (f32[2,256,256]{2,1,0:T(8,128)S(1)}, f32[2,256,256]{2,1,0:T(8,128)S(1)}, u32[]{:S(2)}, u32[]{:S(2)}) collective-permute-start(f32[2,256,256]{2,1,0:T(8,128)S(1)} %get-tuple-element.86), channel_id=1, source_target_pairs={{0,4},{1,5},{2,6},{3,7},{4,0},{5,1},{6,2},{7,3},{8,12},{9,13},{10,... | collective-permute-start | bytes 1572872 | tf_op jit(solution)/shard_map/ppermute | solution.py:646
  36.3 1.1 slice_bitcast_fusion.5
  38.4 1.5 collective-permute-start.3
  39.8 1.5 broadcast_select_fusion
  41.3 1.1 slice_bitcast_fusion
  43.4 1.0 slice_bitcast_fusion.1
  44.4 1.9 collective-permute-start.8
  46.3 12.1 %collective-permute-done.1.refs_1_ = f32[2,256,256]{2,1,0:T(8,128)S(1)} collective-permute-done((f32[2,256,256]{2,1,0:T(8,128)S(1)}, f32[2,256,256]{2,1,0:T(8,128)S(1)}, u32[]{:S(2)}, u32[]{:S(2)}) %collective-permute-start.1) | collective-permute-done | bytes 524320 | tf_op jit(solution)/shard_map/ppermute | solution.py:646
  62.6 1.1 maximum_select_fusion.2
  63.7 1.5 collective-permute-start.16
  66.4 3.4 %fusion.1 = (f32[8,1,128,256]{3,2,1,0:T(8,128)S(1)}, f32[8,1,128,256]{3,2,1,0:T(8,128)S(1)}, f32[8,1,128,256]{3,2,1,0:T(8,128)S(1)}, f32[8,1,128,256]{3,2,1,0:T(8,128)S(1)}) fusion(f32[256]{0:T(256)S(1)} %get-tuple-element.105, f32[8,128]{1,0:T(8,128)S(1)} %fusion.24, f32[]{:T(128)} %bitcast.17, f32[]{:T(128)S(6)} %convert_element_type.96, ...), kind=kLoop, calls=%fused_computation.10 | loop fusion | flops 20971520 | bytes 4200456 | tf_op jit(solution)/shard_map/mul | solution.py:631
  69.9 19.2 %collective-permute-done.16 = f32[2,2,256,256]{3,2,1,0:T(8,128)S(1)} collective-permute-done((f32[2,2,256,256]{3,2,1,0:T(8,128)}, f32[2,2,256,256]{3,2,1,0:T(8,128)S(1)}, u32[]{:S(2)}, u32[]{:S(2)}) %collective-permute-start.16) | collective-permute-done | bytes 1048608 | tf_op jit(solution)/shard_map/ppermute | solution.py:646
  89.3 1.6 collective-permute-start.17
  92.0 2.4 collective-permute-start.9
  95.2 6.0 %move_columns.4 = (f32[2,256,256]{2,1,0:T(8,128)S(1)}, f32[2,256,256]{2,1,0:T(8,128)S(1)}, f32[2,256,256]{2,1,0:T(8,128)}, f32[2,256,256]{2,1,0:T(8,128)}) custom-call(s32[2]{0:T(128)S(1)} %pad_add_fusion.1.swap_ref, f32[2,256,256]{2,1,0:T(8,128)S(1)} %copy-done.11, f32[2,256,256]{2,1,0:T(8,128)S(1)} %copy-done.14, ...), custom_call_target="tpu_custom_call" | custom-call | flops 6000000000 | bytes 18000000 | tf_op jit(solution)/shard_map/move_columns/pallas_call | solution.py:559
  102.0 15.4 %collective-permute-start.24 = (f32[2,256,256]{2,1,0:T(8,128)}, f32[2,256,256]{2,1,0:T(8,128)}, u32[]{:S(2)}, u32[]{:S(2)}) collective-permute-start(f32[2,256,256]{2,1,0:T(8,128)} %get-tuple-element.45), channel_id=1, source_target_pairs={{0,1},{1,0},{2,3},{3,2},{4,5},{5,4},{6,7},{7,6},{8,9},{9,8},{10,11... | collective-permute-start | bytes 1572872 | tf_op jit(solution)/shard_map/ppermute | solution.py:646
  117.5 3.5 %collective-permute-done.8.refs_2_ = f32[2,256,256]{2,1,0:T(8,128)} collective-permute-done((f32[2,256,256]{2,1,0:T(8,128)}, f32[2,256,256]{2,1,0:T(8,128)}, u32[]{:S(2)}, u32[]{:S(2)}) %collective-permute-start.8) | collective-permute-done | bytes 524320 | tf_op jit(solution)/shard_map/ppermute | solution.py:646
  121.0 6.2 %move_columns.5 = (f32[2,256,256]{2,1,0:T(8,128)S(1)}, f32[2,256,256]{2,1,0:T(8,128)S(1)}, f32[2,256,256]{2,1,0:T(8,128)}, f32[2,256,256]{2,1,0:T(8,128)}) custom-call(s32[2]{0:T(128)S(1)} %pad_add_fusion.1.swap_ref, f32[2,256,256]{2,1,0:T(8,128)S(1)} %copy-done.10, f32[2,256,256]{2,1,0:T(8,128)} %collective-permute-done.7.refs_1_, ...), custom_call_target="tpu_custom_call" | custom-call | flops 6000000000 | bytes 18000000 | tf_op jit(solution)/shard_map/move_columns/pallas_call | solution.py:559
  128.8 10.6 %collective-permute-done.4.refs_1_ = f32[2,256,256]{2,1,0:T(8,128)} collective-permute-done((f32[2,256,256]{2,1,0:T(8,128)S(1)}, f32[2,256,256]{2,1,0:T(8,128)}, u32[]{:S(2)}, u32[]{:S(2)}) %collective-permute-start.4) | collective-permute-done | bytes 524320 | tf_op jit(solution)/shard_map/ppermute | solution.py:646
  139.9 1.3 slice.57
  141.2 1.2 slice.58
  144.8 1.0 copy-done.18
  146.7 5.0 %turn_rows.3 = (f32[2,256,256]{2,1,0:T(8,128)S(1)}, f32[2,256,256]{2,1,0:T(8,128)S(1)}, f32[2,256,256]{2,1,0:T(8,128)S(1)}, f32[2,256,256]{2,1,0:T(8,128)S(1)}) custom-call(s32[4]{0:T(128)S(1)} %pad_add_fusion.place_ref, f32[1]{0:T(128)} %bitcast.9.scale_ref, f32[2,256,256]{2,1,0:T(8,128)S(1)} %copy-done.16, f32[2,256,256]{2,1,0:T(8,128)S(1)} %copy-done.18, ...), custom_call_target="tpu_custom_call" | custom-call | flops 4000000000 | bytes 12000000 | tf_op jit(solution)/shard_map/turn_rows/pallas_call | solution.py:531
  151.9 5.1 %turn_rows.2 = (f32[2,256,256]{2,1,0:T(8,128)S(1)}, f32[2,256,256]{2,1,0:T(8,128)S(1)}, f32[2,256,256]{2,1,0:T(8,128)S(1)}, f32[2,256,256]{2,1,0:T(8,128)S(1)}, f32[2,256,1024]{2,1,0:T(8,128)S(1)}) custom-call(s32[4]{0:T(128)S(1)} %pad_add_fusion.place_ref, f32[1]{0:T(128)S(6)} %add.694.scale_ref, f32[2,256,256]{2,1,0:T(8,128)S(1)} %copy-done.30, ...), custom_call_target="tpu_custom_call" | custom-call | flops 4000000000 | bytes 12000000 | tf_op jit(solution)/shard_map/turn_rows/pallas_call | solution.py:531
  157.6 1.7 collective-permute-start.19
  161.1 4.4 %move_columns.7 = (f32[2,256,256]{2,1,0:T(8,128)S(1)}, f32[2,256,256]{2,1,0:T(8,128)S(1)}, f32[2,256,256]{2,1,0:T(8,128)S(1)}, f32[2,256,256]{2,1,0:T(8,128)S(1)}) custom-call(s32[2]{0:T(128)S(1)} %add_add_fusion.swap_ref, f32[2,256,256]{2,1,0:T(8,128)S(1)} %get-tuple-element.64.refs_0_, f32[2,256,256]{2,1,0:T(8,128)S(1)} %get-tuple-element.65.refs_1_, ...), custom_call_target="tpu_custom_call" | custom-call | flops 6000000000 | bytes 18000000 | tf_op jit(solution)/shard_map/move_columns/pallas_call | solution.py:559
  166.0 1.4 collective-permute-start.35
  167.4 4.6 %move_columns.6 = (f32[2,256,256]{2,1,0:T(8,128)S(1)}, f32[2,256,256]{2,1,0:T(8,128)S(1)}, f32[2,256,256]{2,1,0:T(8,128)S(1)}, f32[2,256,256]{2,1,0:T(8,128)S(1)}) custom-call(s32[2]{0:T(128)S(1)} %add_add_fusion.swap_ref, f32[2,256,256]{2,1,0:T(8,128)S(1)} %get-tuple-element.59.refs_0_, f32[2,256,256]{2,1,0:T(8,128)S(1)} %get-tuple-element.60.refs_1_, ...), custom_call_target="tpu_custom_call" | custom-call | flops 6000000000 | bytes 18000000 | tf_op jit(solution)/shard_map/move_columns/pallas_call | solution.py:559
  174.3 4.2 %image_rows.2 = (f32[256,256]{1,0:T(8,128)S(1)}, f32[256,256]{1,0:T(8,128)S(1)}, f32[256,256]{1,0:T(8,128)S(1)}, f32[256,256]{1,0:T(8,128)S(1)}) custom-call(s32[4]{0:T(128)S(1)} %pad_add_fusion.place_ref, f32[1]{0:T(128)} %bitcast.9.scale_ref, f32[2,256,1024]{2,1,0:T(8,128)S(1)} %get-tuple-element.52.refs_0_, ...), custom_call_target="tpu_custom_call" | custom-call | flops 3000000000 | bytes 9000000 | tf_op jit(solution)/shard_map/image_rows/pallas_call | solution.py:544
  178.5 5.3 %collective-permute-done.33.refs_5_ = f32[2,256,256]{2,1,0:T(8,128)S(1)} collective-permute-done((f32[2,256,256]{2,1,0:T(8,128)S(1)}, f32[2,256,256]{2,1,0:T(8,128)S(1)}, u32[]{:S(2)}, u32[]{:S(2)}) %collective-permute-start.33) | collective-permute-done | bytes 524320 | tf_op jit(solution)/shard_map/ppermute | solution.py:646
  184.4 12.4 %collective-permute-done.35.refs_7_ = f32[2,256,256]{2,1,0:T(8,128)S(1)} collective-permute-done((f32[2,256,256]{2,1,0:T(8,128)S(1)}, f32[2,256,256]{2,1,0:T(8,128)S(1)}, u32[]{:S(2)}, u32[]{:S(2)}) %collective-permute-start.35) | collective-permute-done | bytes 524320 | tf_op jit(solution)/shard_map/ppermute | solution.py:646
  197.6 1.5 collective-permute-start.22
  199.1 15.5 %collective-permute-done.32.refs_4_ = f32[2,256,256]{2,1,0:T(8,128)S(1)} collective-permute-done((f32[2,256,256]{2,1,0:T(8,128)S(1)}, f32[2,256,256]{2,1,0:T(8,128)S(1)}, u32[]{:S(2)}, u32[]{:S(2)}) %collective-permute-start.32) | collective-permute-done | bytes 524320 | tf_op jit(solution)/shard_map/ppermute | solution.py:646
  214.9 10.1 %collective-permute-done.34.refs_6_ = f32[2,256,256]{2,1,0:T(8,128)S(1)} collective-permute-done((f32[2,256,256]{2,1,0:T(8,128)S(1)}, f32[2,256,256]{2,1,0:T(8,128)S(1)}, u32[]{:S(2)}, u32[]{:S(2)}) %collective-permute-start.34) | collective-permute-done | bytes 524320 | tf_op jit(solution)/shard_map/ppermute | solution.py:646
  225.0 1.6 copy-done.3
  226.6 5.2 %image_rows.3 = (f32[256,256]{1,0:T(8,128)S(1)}, f32[256,256]{1,0:T(8,128)S(1)}, f32[256,256]{1,0:T(8,128)S(1)}, f32[256,256]{1,0:T(8,128)S(1)}) custom-call(s32[4]{0:T(128)S(1)} %pad_add_fusion.place_ref, f32[1]{0:T(128)} %bitcast.9.scale_ref, f32[2,256,256]{2,1,0:T(8,128)S(1)} %get-tuple-element.63.refs_0_, f32[2,256,256]{2,1,0:T(8,128)S(1)} %get-tuple-element.68.refs_1_, ...), custom_call_target="tpu_custom_call" | custom-call | flops 3000000000 | bytes 9000000 | tf_op jit(solution)/shard_map/image_rows/pallas_call | solution.py:544
  232.5 2.6 collective-permute-start.37
  235.1 2.4 collective-permute-start.38
  238.3 16.4 %collective-permute-done.37 = f32[256,256]{1,0:T(8,128)S(1)} collective-permute-done((f32[256,256]{1,0:T(8,128)S(1)}, f32[256,256]{1,0:T(8,128)S(1)}, u32[]{:S(2)}, u32[]{:S(2)}) %collective-permute-start.37) | collective-permute-done | bytes 262176 | tf_op jit(solution)/shard_map/ppermute | solution.py:646
  254.7 7.3 %collective-permute-done.39 = f32[256,256]{1,0:T(8,128)S(1)} collective-permute-done((f32[256,256]{1,0:T(8,128)S(1)}, f32[256,256]{1,0:T(8,128)S(1)}, u32[]{:S(2)}, u32[]{:S(2)}) %collective-permute-start.39) | collective-permute-done | bytes 262176 | tf_op jit(solution)/shard_map/ppermute | solution.py:646
  (168 shorter events, 27.0 us)
Async XLA Ops:
  2.3 16.3 %collective-permute-start.12 = (f32[2,256,128]{2,1,0:T(8,128)}, f32[2,256,128]{2,1,0:T(8,128)}, u32[]{:S(2)}, u32[]{:S(2)}) collective-permute-start(f32[2,256,128]{2,1,0:T(8,128)} %constant_dynamic-slice_fusion.2), channel_id=1, source_target_pairs={{0,4},{1,5},{2,6},{3,7},{4,0},{5,1},{6,2},{7,3},{8,12},{9,13},{10,... | collective-permute-start | bytes 786440 | tf_op jit(solution)/shard_map/ppermute | solution.py:646
  5.4 21.7 %collective-permute-start.13 = (f32[2,256,128]{2,1,0:T(8,128)}, f32[2,256,128]{2,1,0:T(8,128)}, u32[]{:S(2)}, u32[]{:S(2)}) collective-permute-start(f32[2,256,128]{2,1,0:T(8,128)} %constant_dynamic-slice_fusion.2), channel_id=1, source_target_pairs={{0,8},{1,9},{2,10},{3,11},{4,12},{5,13},{6,14},{7,15},{8,0},{9,1},... | collective-permute-start | bytes 786440 | tf_op jit(solution)/shard_map/ppermute | solution.py:646
  7.9 19.1 %collective-permute-start.14 = (f32[2,256,128]{2,1,0:T(8,128)}, f32[2,256,128]{2,1,0:T(8,128)}, u32[]{:S(2)}, u32[]{:S(2)}) collective-permute-start(f32[2,256,128]{2,1,0:T(8,128)} %constant_dynamic-slice_fusion.2), channel_id=1, source_target_pairs={{0,12},{1,13},{2,14},{3,15},{4,8},{5,9},{6,10},{7,11},{8,4},{9,5},... | collective-permute-start | bytes 786440 | tf_op jit(solution)/shard_map/ppermute | solution.py:646
  17.8 11.4 %collective-permute-start = (f32[2,2,256,256]{3,2,1,0:T(8,128)}, f32[2,2,256,256]{3,2,1,0:T(8,128)}, u32[]{:S(2)}, u32[]{:S(2)}) collective-permute-start(f32[2,2,256,256]{3,2,1,0:T(8,128)} %get-tuple-element.43), channel_id=1, source_target_pairs={{0,1},{1,0},{2,3},{3,2},{4,5},{5,4},{6,7},{7,6},{8,9},{9,8},{10,11... | collective-permute-start | bytes 3145736 | tf_op jit(solution)/shard_map/ppermute | solution.py:646
  17.8 22.0 %collective-permute-start.6 = (f32[2,2,256,256]{3,2,1,0:T(8,128)}, f32[2,2,256,256]{3,2,1,0:T(8,128)}, u32[]{:S(2)}, u32[]{:S(2)}) collective-permute-start(f32[2,2,256,256]{3,2,1,0:T(8,128)} %get-tuple-element.47), channel_id=1, source_target_pairs={{0,1},{1,0},{2,3},{3,2},{4,5},{5,4},{6,7},{7,6},{8,9},{9,8},{10,11... | collective-permute-start | bytes 3145736 | tf_op jit(solution)/shard_map/ppermute | solution.py:646
  18.5 10.7 %copy-start.9 = (f32[2,2,256,256]{3,2,1,0:T(8,128)S(1)}, f32[2,2,256,256]{3,2,1,0:T(8,128)}, u32[]{:S(2)}) copy-start(f32[2,2,256,256]{3,2,1,0:T(8,128)} %copy-done.8) | copy-start | bytes 3145732
  31.5 26.9 %collective-permute-start.1 = (f32[2,256,256]{2,1,0:T(8,128)S(1)}, f32[2,256,256]{2,1,0:T(8,128)S(1)}, u32[]{:S(2)}, u32[]{:S(2)}) collective-permute-start(f32[2,256,256]{2,1,0:T(8,128)S(1)} %get-tuple-element.86), channel_id=1, source_target_pairs={{0,4},{1,5},{2,6},{3,7},{4,0},{5,1},{6,2},{7,3},{8,12},{9,13},{10,... | collective-permute-start | bytes 1572872 | tf_op jit(solution)/shard_map/ppermute | solution.py:646
  37.4 53.9 %collective-permute-start.2 = (f32[2,256,256]{2,1,0:T(8,128)}, f32[2,256,256]{2,1,0:T(8,128)}, u32[]{:S(2)}, u32[]{:S(2)}) collective-permute-start(f32[2,256,256]{2,1,0:T(8,128)} %get-tuple-element.87), channel_id=1, source_target_pairs={{0,8},{1,9},{2,10},{3,11},{4,12},{5,13},{6,14},{7,15},{8,0},{9,1},... | collective-permute-start | bytes 1572872 | tf_op jit(solution)/shard_map/ppermute | solution.py:646
  38.4 56.1 %collective-permute-start.3 = (f32[2,256,256]{2,1,0:T(8,128)}, f32[2,256,256]{2,1,0:T(8,128)}, u32[]{:S(2)}, u32[]{:S(2)}) collective-permute-start(f32[2,256,256]{2,1,0:T(8,128)} %get-tuple-element.85), channel_id=1, source_target_pairs={{0,12},{1,13},{2,14},{3,15},{4,8},{5,9},{6,10},{7,11},{8,4},{9,5},... | collective-permute-start | bytes 1572872 | tf_op jit(solution)/shard_map/ppermute | solution.py:646
  41.3 19.2 %copy-start.34 = (f32[2,4,256,128]{3,2,1,0:T(8,128)S(1)}, f32[2,4,256,128]{3,2,1,0:T(8,128)}, u32[]{:S(2)}) copy-start(f32[2,4,256,128]{3,2,1,0:T(8,128)} %pad_maximum_fusion.2) | copy-start | bytes 3145732
  42.4 59.7 %collective-permute-start.7 = (f32[2,256,256]{2,1,0:T(8,128)}, f32[2,256,256]{2,1,0:T(8,128)}, u32[]{:S(2)}, u32[]{:S(2)}) collective-permute-start(f32[2,256,256]{2,1,0:T(8,128)} %get-tuple-element.90), channel_id=1, source_target_pairs={{0,4},{1,5},{2,6},{3,7},{4,0},{5,1},{6,2},{7,3},{8,12},{9,13},{10,... | collective-permute-start | bytes 1572872 | tf_op jit(solution)/shard_map/ppermute | solution.py:646
  43.4 17.4 %copy-start.33 = (s32[4]{0:T(128)S(1)}, s32[4]{0:T(128)}, u32[]{:S(2)}) copy-start(s32[4]{0:T(128)} %constant.231.clone) | copy-start | bytes 52
  44.4 76.5 %collective-permute-start.8 = (f32[2,256,256]{2,1,0:T(8,128)}, f32[2,256,256]{2,1,0:T(8,128)}, u32[]{:S(2)}, u32[]{:S(2)}) collective-permute-start(f32[2,256,256]{2,1,0:T(8,128)} %get-tuple-element.91), channel_id=1, source_target_pairs={{0,8},{1,9},{2,10},{3,11},{4,12},{5,13},{6,14},{7,15},{8,0},{9,1},... | collective-permute-start | bytes 1572872 | tf_op jit(solution)/shard_map/ppermute | solution.py:646
  60.6 2.0 collective-permute-start.15
  63.7 25.4 %collective-permute-start.16 = (f32[2,2,256,256]{3,2,1,0:T(8,128)}, f32[2,2,256,256]{3,2,1,0:T(8,128)S(1)}, u32[]{:S(2)}, u32[]{:S(2)}) collective-permute-start(f32[2,2,256,256]{3,2,1,0:T(8,128)} %maximum_select_fusion.2), channel_id=1, source_target_pairs={{0,2},{1,3},{2,0},{3,1},{4,6},{5,7},{6,4},{7,5},{8,10},{9,11},{10,... | collective-permute-start | bytes 3145736 | tf_op jit(solution)/shard_map/ppermute | solution.py:646
  89.3 85.0 %copy-start.2 = (f32[2,2,2,256,256]{4,3,2,1,0:T(8,128)}, f32[2,2,2,256,256]{4,3,2,1,0:T(8,128)S(1)}, u32[]{:S(2)}) copy-start(f32[2,2,2,256,256]{4,3,2,1,0:T(8,128)S(1)} %maximum_select_fusion.refs_4_.refs_5_.refs_8_) | copy-start | bytes 6291460
  89.3 54.4 %collective-permute-start.17 = (f32[2,2,2,256,256]{4,3,2,1,0:T(8,128)S(1)}, f32[2,2,2,256,256]{4,3,2,1,0:T(8,128)}, u32[]{:S(2)}, u32[]{:S(2)}) collective-permute-start(f32[2,2,2,256,256]{4,3,2,1,0:T(8,128)S(1)} %maximum_select_fusion.refs_4_.refs_5_.refs_8_), channel_id=1, source_target_pairs={{0,16},{1,17},{2,18},{3,19},{4,20},{5,21},{6,22},{7,23},{8,24},{9,... | collective-permute-start | bytes 6291464 | tf_op jit(solution)/shard_map/ppermute | solution.py:646
  92.0 28.9 %collective-permute-start.9 = (f32[2,256,256]{2,1,0:T(8,128)S(1)}, f32[2,256,256]{2,1,0:T(8,128)S(1)}, u32[]{:S(2)}, u32[]{:S(2)}) collective-permute-start(f32[2,256,256]{2,1,0:T(8,128)S(1)} %copy-done.35), channel_id=1, source_target_pairs={{0,12},{1,13},{2,14},{3,15},{4,8},{5,9},{6,10},{7,11},{8,4},{9,5},... | collective-permute-start | bytes 1572872 | tf_op jit(solution)/shard_map/ppermute | solution.py:646
  101.2 19.7 %copy-start.15 = (f32[2,256,256]{2,1,0:T(8,128)}, f32[2,256,256]{2,1,0:T(8,128)S(1)}, u32[]{:S(2)}) copy-start(f32[2,256,256]{2,1,0:T(8,128)S(1)} %get-tuple-element.44.refs_0_) | copy-start | bytes 1572868
  101.2 38.2 %collective-permute-start.5 = (f32[2,256,256]{2,1,0:T(8,128)}, f32[2,256,256]{2,1,0:T(8,128)}, u32[]{:S(2)}, u32[]{:S(2)}) collective-permute-start(f32[2,256,256]{2,1,0:T(8,128)} %get-tuple-element.45), channel_id=1, source_target_pairs={{0,5},{1,4},{2,7},{3,6},{4,1},{5,0},{6,3},{7,2},{8,13},{9,12},{10,... | collective-permute-start | bytes 1572872 | tf_op jit(solution)/shard_map/ppermute | solution.py:646
  101.3 19.6 %copy-start.10 = (f32[2,256,256]{2,1,0:T(8,128)S(1)}, f32[2,256,256]{2,1,0:T(8,128)}, u32[]{:S(2)}) copy-start(f32[2,256,256]{2,1,0:T(8,128)} %get-tuple-element.92.refs_0_) | copy-start | bytes 1572868
  102.0 25.2 %copy-start.6 = (f32[8,2,128,256]{3,2,1,0:T(8,128)}, f32[8,2,128,256]{3,2,1,0:T(8,128)S(1)}, u32[]{:S(2)}) copy-start(f32[8,2,128,256]{3,2,1,0:T(8,128)S(1)} %pad_maximum_fusion.1.refs_7_) | copy-start | bytes 6291460
  102.0 41.6 %collective-permute-start.24 = (f32[2,256,256]{2,1,0:T(8,128)}, f32[2,256,256]{2,1,0:T(8,128)}, u32[]{:S(2)}, u32[]{:S(2)}) collective-permute-start(f32[2,256,256]{2,1,0:T(8,128)} %get-tuple-element.45), channel_id=1, source_target_pairs={{0,1},{1,0},{2,3},{3,2},{4,5},{5,4},{6,7},{7,6},{8,9},{9,8},{10,11... | collective-permute-start | bytes 1572872 | tf_op jit(solution)/shard_map/ppermute | solution.py:646
  120.9 18.5 %collective-permute-start.4 = (f32[2,256,256]{2,1,0:T(8,128)S(1)}, f32[2,256,256]{2,1,0:T(8,128)}, u32[]{:S(2)}, u32[]{:S(2)}) collective-permute-start(f32[2,256,256]{2,1,0:T(8,128)S(1)} %get-tuple-element.44.refs_0_), channel_id=1, source_target_pairs={{0,4},{1,5},{2,6},{3,7},{4,0},{5,1},{6,2},{7,3},{8,12},{9,13},{10,... | collective-permute-start | bytes 1572872 | tf_op jit(solution)/shard_map/ppermute | solution.py:646
  128.8 14.9 %collective-permute-start.25 = (f32[2,256,256]{2,1,0:T(8,128)}, f32[2,256,256]{2,1,0:T(8,128)}, u32[]{:S(2)}, u32[]{:S(2)}) collective-permute-start(f32[2,256,256]{2,1,0:T(8,128)} %get-tuple-element.54), channel_id=1, source_target_pairs={{0,1},{1,0},{2,3},{3,2},{4,5},{5,4},{6,7},{7,6},{8,9},{9,8},{10,11... | collective-permute-start | bytes 1572872 | tf_op jit(solution)/shard_map/ppermute | solution.py:646
  139.4 12.4 %collective-permute-start.10 = (f32[2,256,256]{2,1,0:T(8,128)}, f32[2,256,256]{2,1,0:T(8,128)}, u32[]{:S(2)}, u32[]{:S(2)}) collective-permute-start(f32[2,256,256]{2,1,0:T(8,128)} %get-tuple-element.50), channel_id=1, source_target_pairs={{0,1},{1,0},{2,3},{3,2},{4,5},{5,4},{6,7},{7,6},{8,9},{9,8},{10,11... | collective-permute-start | bytes 1572872 | tf_op jit(solution)/shard_map/ppermute | solution.py:646
  139.4 12.4 %collective-permute-start.11 = (f32[2,256,256]{2,1,0:T(8,128)}, f32[2,256,256]{2,1,0:T(8,128)}, u32[]{:S(2)}, u32[]{:S(2)}) collective-permute-start(f32[2,256,256]{2,1,0:T(8,128)} %get-tuple-element.51), channel_id=1, source_target_pairs={{0,1},{1,0},{2,3},{3,2},{4,5},{5,4},{6,7},{7,6},{8,9},{9,8},{10,11... | collective-permute-start | bytes 1572872 | tf_op jit(solution)/shard_map/ppermute | solution.py:646
  143.6 15.7 %collective-permute-start.18 = (f32[2,256,256]{2,1,0:T(8,128)}, f32[2,256,256]{2,1,0:T(8,128)S(1)}, u32[]{:S(2)}, u32[]{:S(2)}) collective-permute-start(f32[2,256,256]{2,1,0:T(8,128)} %copy-done.17), channel_id=1, source_target_pairs={{0,4},{1,5},{2,6},{3,7},{4,0},{5,1},{6,2},{7,3},{8,12},{9,13},{10,... | collective-permute-start | bytes 1572872 | tf_op jit(solution)/shard_map/ppermute | solution.py:646
  151.7 9.3 %collective-permute-start.29 = (f32[2,256,256]{2,1,0:T(8,128)S(1)}, f32[2,256,256]{2,1,0:T(8,128)S(1)}, u32[]{:S(2)}, u32[]{:S(2)}) collective-permute-start(f32[2,256,256]{2,1,0:T(8,128)S(1)} %get-tuple-element.67), channel_id=1, source_target_pairs={{0,1},{1,0},{2,3},{3,2},{4,5},{5,4},{6,7},{7,6},{8,9},{9,8},{10,11... | collective-permute-start | bytes 1572872 | tf_op jit(solution)/shard_map/ppermute | solution.py:646
  157.0 4.0 %collective-permute-start.28 = (f32[2,256,256]{2,1,0:T(8,128)S(1)}, f32[2,256,256]{2,1,0:T(8,128)S(1)}, u32[]{:S(2)}, u32[]{:S(2)}) collective-permute-start(f32[2,256,256]{2,1,0:T(8,128)S(1)} %get-tuple-element.66), channel_id=1, source_target_pairs={{0,1},{1,0},{2,3},{3,2},{4,5},{5,4},{6,7},{7,6},{8,9},{9,8},{10,11... | collective-permute-start | bytes 1572872 | tf_op jit(solution)/shard_map/ppermute | solution.py:646
  157.6 15.2 %collective-permute-start.19 = (f32[2,256,256]{2,1,0:T(8,128)}, f32[2,256,256]{2,1,0:T(8,128)S(1)}, u32[]{:S(2)}, u32[]{:S(2)}) collective-permute-start(f32[2,256,256]{2,1,0:T(8,128)} %get-tuple-element.54), channel_id=1, source_target_pairs={{0,5},{1,4},{2,7},{3,6},{4,1},{5,0},{6,3},{7,2},{8,13},{9,12},{10,... | collective-permute-start | bytes 1572872 | tf_op jit(solution)/shard_map/ppermute | solution.py:646
  160.5 5.5 %collective-permute-start.27 = (f32[2,256,256]{2,1,0:T(8,128)S(1)}, f32[2,256,256]{2,1,0:T(8,128)S(1)}, u32[]{:S(2)}, u32[]{:S(2)}) collective-permute-start(f32[2,256,256]{2,1,0:T(8,128)S(1)} %get-tuple-element.62), channel_id=1, source_target_pairs={{0,1},{1,0},{2,3},{3,2},{4,5},{5,4},{6,7},{7,6},{8,9},{9,8},{10,11... | collective-permute-start | bytes 1572872 | tf_op jit(solution)/shard_map/ppermute | solution.py:646
  161.0 6.5 %collective-permute-start.26 = (f32[2,256,256]{2,1,0:T(8,128)S(1)}, f32[2,256,256]{2,1,0:T(8,128)S(1)}, u32[]{:S(2)}, u32[]{:S(2)}) collective-permute-start(f32[2,256,256]{2,1,0:T(8,128)S(1)} %get-tuple-element.61), channel_id=1, source_target_pairs={{0,1},{1,0},{2,3},{3,2},{4,5},{5,4},{6,7},{7,6},{8,9},{9,8},{10,11... | collective-permute-start | bytes 1572872 | tf_op jit(solution)/shard_map/ppermute | solution.py:646
  165.5 8.3 %collective-permute-start.31 = (f32[2,256,256]{2,1,0:T(8,128)S(1)}, f32[2,256,256]{2,1,0:T(8,128)S(1)}, u32[]{:S(2)}, u32[]{:S(2)}) collective-permute-start(f32[2,256,256]{2,1,0:T(8,128)S(1)} %get-tuple-element.70), channel_id=1, source_target_pairs={{0,1},{1,0},{2,3},{3,2},{4,5},{5,4},{6,7},{7,6},{8,9},{9,8},{10,11... | collective-permute-start | bytes 1572872 | tf_op jit(solution)/shard_map/ppermute | solution.py:646
  166.0 17.8 %collective-permute-start.33 = (f32[2,256,256]{2,1,0:T(8,128)S(1)}, f32[2,256,256]{2,1,0:T(8,128)S(1)}, u32[]{:S(2)}, u32[]{:S(2)}) collective-permute-start(f32[2,256,256]{2,1,0:T(8,128)S(1)} %get-tuple-element.72), channel_id=1, source_target_pairs={{0,4},{1,5},{2,6},{3,7},{4,0},{5,1},{6,2},{7,3},{8,12},{9,13},{10,... | collective-permute-start | bytes 1572872 | tf_op jit(solution)/shard_map/ppermute | solution.py:646
  166.0 30.8 %collective-permute-start.35 = (f32[2,256,256]{2,1,0:T(8,128)S(1)}, f32[2,256,256]{2,1,0:T(8,128)S(1)}, u32[]{:S(2)}, u32[]{:S(2)}) collective-permute-start(f32[2,256,256]{2,1,0:T(8,128)S(1)} %get-tuple-element.74), channel_id=1, source_target_pairs={{0,5},{1,4},{2,7},{3,6},{4,1},{5,0},{6,3},{7,2},{8,13},{9,12},{10,... | collective-permute-start | bytes 1572872 | tf_op jit(solution)/shard_map/ppermute | solution.py:646
  172.0 25.6 %collective-permute-start.30 = (f32[2,256,256]{2,1,0:T(8,128)S(1)}, f32[2,256,256]{2,1,0:T(8,128)S(1)}, u32[]{:S(2)}, u32[]{:S(2)}) collective-permute-start(f32[2,256,256]{2,1,0:T(8,128)S(1)} %get-tuple-element.69), channel_id=1, source_target_pairs={{0,1},{1,0},{2,3},{3,2},{4,5},{5,4},{6,7},{7,6},{8,9},{9,8},{10,11... | collective-permute-start | bytes 1572872 | tf_op jit(solution)/shard_map/ppermute | solution.py:646
  172.8 41.8 %collective-permute-start.32 = (f32[2,256,256]{2,1,0:T(8,128)S(1)}, f32[2,256,256]{2,1,0:T(8,128)S(1)}, u32[]{:S(2)}, u32[]{:S(2)}) collective-permute-start(f32[2,256,256]{2,1,0:T(8,128)S(1)} %get-tuple-element.71), channel_id=1, source_target_pairs={{0,4},{1,5},{2,6},{3,7},{4,0},{5,1},{6,2},{7,3},{8,12},{9,13},{10,... | collective-permute-start | bytes 1572872 | tf_op jit(solution)/shard_map/ppermute | solution.py:646
  173.8 51.2 %collective-permute-start.34 = (f32[2,256,256]{2,1,0:T(8,128)S(1)}, f32[2,256,256]{2,1,0:T(8,128)S(1)}, u32[]{:S(2)}, u32[]{:S(2)}) collective-permute-start(f32[2,256,256]{2,1,0:T(8,128)S(1)} %get-tuple-element.73), channel_id=1, source_target_pairs={{0,5},{1,4},{2,7},{3,6},{4,1},{5,0},{6,3},{7,2},{8,13},{9,12},{10,... | collective-permute-start | bytes 1572872 | tf_op jit(solution)/shard_map/ppermute | solution.py:646
  183.7 48.7 %collective-permute-start.20 = (f32[256,256]{1,0:T(8,128)S(1)}, f32[256,256]{1,0:T(8,128)S(1)}, u32[]{:S(2)}, u32[]{:S(2)}) collective-permute-start(f32[256,256]{1,0:T(8,128)S(1)} %get-tuple-element.55), channel_id=1, source_target_pairs={{0,0},{1,8},{2,2},{3,10},{4,4},{5,12},{6,6},{7,14},{8,1},{9,9},{10... | collective-permute-start | bytes 786440 | tf_op jit(solution)/shard_map/ppermute | solution.py:646
  196.8 38.3 %collective-permute-start.21 = (f32[256,256]{1,0:T(8,128)S(1)}, f32[256,256]{1,0:T(8,128)S(1)}, u32[]{:S(2)}, u32[]{:S(2)}) collective-permute-start(f32[256,256]{1,0:T(8,128)S(1)} %get-tuple-element.56), channel_id=1, source_target_pairs={{0,1},{1,9},{2,3},{3,11},{4,5},{5,13},{6,7},{7,15},{8,0},{9,8},{10... | collective-permute-start | bytes 786440 | tf_op jit(solution)/shard_map/ppermute | solution.py:646
  197.6 39.9 %collective-permute-start.22 = (f32[256,256]{1,0:T(8,128)S(1)}, f32[256,256]{1,0:T(8,128)S(1)}, u32[]{:S(2)}, u32[]{:S(2)}) collective-permute-start(f32[256,256]{1,0:T(8,128)S(1)} %get-tuple-element.57), channel_id=1, source_target_pairs={{0,2},{1,10},{2,0},{3,8},{4,6},{5,14},{6,4},{7,12},{8,3},{9,11},{1... | collective-permute-start | bytes 786440 | tf_op jit(solution)/shard_map/ppermute | solution.py:646
  214.6 23.5 %collective-permute-start.23 = (f32[256,256]{1,0:T(8,128)S(1)}, f32[256,256]{1,0:T(8,128)S(1)}, u32[]{:S(2)}, u32[]{:S(2)}) collective-permute-start(f32[256,256]{1,0:T(8,128)S(1)} %get-tuple-element.58), channel_id=1, source_target_pairs={{0,3},{1,11},{2,1},{3,9},{4,7},{5,15},{6,5},{7,13},{8,2},{9,10},{1... | collective-permute-start | bytes 786440 | tf_op jit(solution)/shard_map/ppermute | solution.py:646
  226.6 36.4 %copy-start.1 = (f32[2,256,1024]{2,1,0:T(8,128)S(1)}, f32[2,256,1024]{2,1,0:T(8,128)}, u32[]{:S(2)}) copy-start(f32[2,256,1024]{2,1,0:T(8,128)} %param.15) | copy-start | bytes 6291460
  231.8 6.5 %collective-permute-start.36 = (f32[256,256]{1,0:T(8,128)S(1)}, f32[256,256]{1,0:T(8,128)S(1)}, u32[]{:S(2)}, u32[]{:S(2)}) collective-permute-start(f32[256,256]{1,0:T(8,128)S(1)} %get-tuple-element.75), channel_id=1, source_target_pairs={{0,0},{1,8},{2,2},{3,10},{4,4},{5,12},{6,6},{7,14},{8,1},{9,9},{10... | collective-permute-start | bytes 786440 | tf_op jit(solution)/shard_map/ppermute | solution.py:646
  232.5 22.2 %collective-permute-start.37 = (f32[256,256]{1,0:T(8,128)S(1)}, f32[256,256]{1,0:T(8,128)S(1)}, u32[]{:S(2)}, u32[]{:S(2)}) collective-permute-start(f32[256,256]{1,0:T(8,128)S(1)} %get-tuple-element.76), channel_id=1, source_target_pairs={{0,1},{1,9},{2,3},{3,11},{4,5},{5,13},{6,7},{7,15},{8,0},{9,8},{10... | collective-permute-start | bytes 786440 | tf_op jit(solution)/shard_map/ppermute | solution.py:646
  235.1 19.6 %collective-permute-start.38 = (f32[256,256]{1,0:T(8,128)S(1)}, f32[256,256]{1,0:T(8,128)S(1)}, u32[]{:S(2)}, u32[]{:S(2)}) collective-permute-start(f32[256,256]{1,0:T(8,128)S(1)} %get-tuple-element.77), channel_id=1, source_target_pairs={{0,2},{1,10},{2,0},{3,8},{4,6},{5,14},{6,4},{7,12},{8,3},{9,11},{1... | collective-permute-start | bytes 786440 | tf_op jit(solution)/shard_map/ppermute | solution.py:646
  237.5 24.6 %collective-permute-start.39 = (f32[256,256]{1,0:T(8,128)S(1)}, f32[256,256]{1,0:T(8,128)S(1)}, u32[]{:S(2)}, u32[]{:S(2)}) collective-permute-start(f32[256,256]{1,0:T(8,128)S(1)} %get-tuple-element.78), channel_id=1, source_target_pairs={{0,3},{1,11},{2,1},{3,9},{4,7},{5,15},{6,5},{7,13},{8,2},{9,10},{1... | collective-permute-start | bytes 786440 | tf_op jit(solution)/shard_map/ppermute | solution.py:646
  (29 other events, 97.7 us)
